TPU v7x, 32 devices: a whole 2x2x4 slice. The times are simulated.
32 devices in a mesh: expert: 16 (over z, y, x), tensor: 2 (over core).
Axes of the slice: x: 2, y: 2, z: 4, core: 2. Of those that a mesh axis runs over, the one named last changes fastest.
Arguments:
- tokens: bfloat16 [2, 2048, 1536], P(None, 'expert'), may hold values from -6 to 6
- cotangent: bfloat16 [2, 2048, 1536], P(None, 'expert'), may hold values from -6 to 6
- positions: int32 [2, 2048], P(None, 'expert'), may hold values from 0 to 127, as said below
- routes: int32 [2, 2048, 4], P(None, 'expert'), may hold values from 0 to 31, all different within a row; in each aligned block of 64 rows (0 to 63, 64 to 127, ..., all dimensions but the last counted through in order) at most 12 rows name the same one
- attention_gain: float32 [1536], replicated, may hold values from 0.1 to 1.9
- feedforward_gain: float32 [1536], replicated, may hold values from 0.1 to 1.9
- query_weight: bfloat16 [1536, 1536], P(None, 'tensor'), may hold values from -0.15625 to 0.15625
- key_matrix: bfloat16 [1536, 256], P(None, 'tensor'), may hold values from -0.15625 to 0.15625
- value_matrix: bfloat16 [1536, 256], P(None, 'tensor'), may hold values from -0.15625 to 0.15625
- output_weight: bfloat16 [1536, 1536], P('tensor'), may hold values from -1.25 to 1.25
- router_weight: bfloat16 [1536, 32], replicated, may hold values from -0.078125 to 0.078125
- gate_weight: bfloat16 [1536, 24576], P(None, 'expert'), may hold values from -0.15625 to 0.15625
- up_weight: bfloat16 [1536, 24576], P(None, 'expert'), may hold values from -0.15625 to 0.15625
- down_weight: bfloat16 [24576, 1536], P('expert'), may hold values from -0.625 to 0.625
Outputs:
- layer_out: bfloat16 [2, 2048, 1536], P(None, 'expert')
- tokens_grad: float32 [2, 2048, 1536], P(None, 'expert')
- attention_gain_grad: float32 [1536], replicated
- feedforward_gain_grad: float32 [1536], replicated
- query_weight_grad: float32 [1536, 1536], P(None, 'tensor')
- key_weight_grad: float32 [1536, 256], P(None, 'tensor')
- value_weight_grad: float32 [1536, 256], P(None, 'tensor')
- output_weight_grad: float32 [1536, 1536], P('tensor')
- router_weight_grad: float32 [1536, 32], replicated
- gate_weight_grad: float32 [1536, 24576], P(None, 'expert')
- up_weight_grad: float32 [1536, 24576], P(None, 'expert')
- down_weight_grad: float32 [24576, 1536], P('expert')
Inputs may be any that keep to these rules, and one draw needn't show every extreme that they name: In each block of 128 rows (one sequence), positions count 0, 1, 2, ... within each packed document and restart at 0 where a new document begins; every block begins with 0, and some block is a single document. `routes`: each row names 4 different experts; in each aligned block of 64 rows (half a sequence) no expert is named by more than 12 rows.
All inputs are finite; a program needn't handle non-finite values.
Results may differ from a plain program's by a relative error of at most 0.015.
The roundings to bfloat16 on the way count: a program that leaves them out, or rounds other values in their place, can miss the bound.
Values may be sent and summed in bfloat16 or wider, within the bound.
A program may use at most 256 MiB of HBM per device.

v0:
```python
import jax
import jax.numpy as jnp
from jax import lax
from jax.sharding import PartitionSpec as P

HEAD_SIZE = 128
EXPERTS = 32


epsilon = 1e-05
theta_base = 1000000.0
masked_score = -1e30


def rms_norm(value_row_states, gain_vector):
    return (
        value_row_states
        * lax.rsqrt(jnp.mean(value_row_states * value_row_states, axis=-1, keepdims=True) + epsilon)
        * gain_vector
    )


def gelu_exact(value_row_states):
    return jax.nn.gelu(value_row_states, approximate=False)


def rope_tables(positions, head_dim):
    half_dim = head_dim // 2
    inverse = jnp.exp(
        -jnp.log(theta_base) * (2.0 * jnp.arange(half_dim, dtype=jnp.float32) / head_dim)
    )
    angles = positions.astype(jnp.float32)[:, None] * inverse[None, :]
    return (jnp.cos(angles), jnp.sin(angles))


def widen_table(table_part, value_row_states):
    return table_part.reshape(
        (table_part.shape[0],) + (1,) * (value_row_states.ndim - 2) + (table_part.shape[1],)
    )


def rotary_apply(value_row_states, cosine_table, sine_table):
    half_dim = value_row_states.shape[-1] // 2
    first_part = value_row_states[..., :half_dim]
    second = value_row_states[..., half_dim:]
    cos_wide = widen_table(cosine_table, value_row_states)
    sin_wide = widen_table(sine_table, value_row_states)
    return jnp.concatenate(
        [first_part * cos_wide - second * sin_wide, second * cos_wide + first_part * sin_wide],
        axis=-1,
    )


def unrotate(value_row_states, cosine_table, sine_table):
    half_dim = value_row_states.shape[-1] // 2
    first_part = value_row_states[..., :half_dim]
    second = value_row_states[..., half_dim:]
    cos_wide = widen_table(cosine_table, value_row_states)
    sin_wide = widen_table(sine_table, value_row_states)
    return jnp.concatenate(
        [first_part * cos_wide + second * sin_wide, second * cos_wide - first_part * sin_wide],
        axis=-1,
    )


def block_scores(query_block, key_row_states, starts, row_ids, offset, block_rows, score_scale):
    query_ids = offset + jnp.arange(block_rows, dtype=jnp.int32)
    allowed = (row_ids[None, :] <= query_ids[:, None]) & (row_ids[None, :] >= starts[:, None])
    scores = (
        jnp.einsum(
            "qcgd,kcd->cgqk", query_block, key_row_states, preferred_element_type=jnp.float32
        )
        * score_scale
    )
    return jnp.where(allowed, scores, masked_score)


def attention_forward(
    query_rows, key_row_states, value_rows, starts, row_ids, block_rows, score_scale
):

    def one_block(block_index):
        offset = block_index * block_rows
        scores = block_scores(
            query_rows, key_row_states, starts, row_ids, offset, block_rows, score_scale
        )
        row_peak = jnp.max(scores, axis=-1, keepdims=True)
        weights = jnp.exp(scores - row_peak)
        totals = jnp.sum(weights, axis=-1, keepdims=True)
        prob_low = (weights / totals).astype(jnp.bfloat16)
        attention_output = jnp.einsum(
            "cgqk,kcd->qcgd", prob_low, value_rows, preferred_element_type=jnp.float32
        )
        return (attention_output.astype(jnp.bfloat16), row_peak[..., 0] + jnp.log(totals[..., 0]))

    return lax.map(one_block, jnp.arange(query_rows.shape[0] // block_rows, dtype=jnp.int32))


def attention_backward(
    query_rows,
    key_row_states,
    value_rows,
    starts,
    row_ids,
    block_rows,
    score_scale,
    log_totals,
    attended_grad,
):

    def one_block(carried, block_index):
        key_grad, value_grad = carried
        offset = block_index * block_rows
        scores = block_scores(
            query_rows, key_row_states, starts, row_ids, offset, block_rows, score_scale
        )
        probs = jnp.exp(scores - log_totals[block_index][..., None])
        prob_low = probs.astype(jnp.bfloat16)
        prob_grad = jnp.einsum(
            "qcgd,kcd->cgqk", attended_grad, value_rows, preferred_element_type=jnp.float32
        )
        row_dot = jnp.sum(probs * prob_grad, axis=-1, keepdims=True)
        score_grad = (probs * (prob_grad - row_dot)).astype(jnp.bfloat16)
        query_grad = (
            jnp.einsum(
                "cgqk,kcd->qcgd", score_grad, key_row_states, preferred_element_type=jnp.float32
            )
            * score_scale
        )
        key_grad = (
            key_grad
            + jnp.einsum(
                "cgqk,qcgd->kcd", score_grad, query_rows, preferred_element_type=jnp.float32
            )
            * score_scale
        )
        value_grad = value_grad + jnp.einsum(
            "cgqk,qcgd->kcd", prob_low, attended_grad, preferred_element_type=jnp.float32
        )
        return ((key_grad, value_grad), query_grad)

    empty_grad = jnp.zeros(key_row_states.shape, jnp.float32)
    totals_out, query_grad = lax.scan(
        one_block,
        (empty_grad, empty_grad),
        jnp.arange(query_rows.shape[0] // block_rows, dtype=jnp.int32),
    )
    return (query_grad.reshape(query_rows.shape), totals_out[0], totals_out[1])


def spread_rows(base, group, capacity, n_dev, per_dev, width):
    widened = jnp.broadcast_to(
        base.reshape(EXPERTS, 1, capacity, width), (EXPERTS, group, capacity, width)
    )
    return widened.reshape(n_dev, per_dev * capacity, width)


def collect_rows(back, group, capacity, width, slot_index, rows, top_count):
    summed = jnp.sum(back.reshape(EXPERTS, group, capacity, width), axis=1).astype(jnp.bfloat16)
    return (
        summed.reshape(EXPERTS * capacity, width)[slot_index]
        .reshape(rows, top_count, width)
        .astype(jnp.float32)
    )


def local(
    tokens,
    cotangent,
    positions,
    routes,
    attention_gain,
    feedforward_gain,
    query_weight,
    key_matrix,
    value_matrix,
    output_weight,
    router_weight,
    gate_weight,
    up_weight,
    down_weight,
):
    micro_count, length, model_width = tokens.shape
    head_dim = HEAD_SIZE
    kv_local = key_matrix.shape[1] // head_dim
    query_group_count = query_weight.shape[1] // head_dim // kv_local
    top_count = routes.shape[2]
    n_dev = lax.axis_size("expert")
    n_tensor = lax.axis_size("tensor")
    half = length // n_tensor
    offset = lax.axis_index("tensor") * half
    per_dev = max(1, EXPERTS // n_dev)
    group = max(1, n_dev // EXPERTS)
    local_width = gate_weight.shape[1]
    ff_local = local_width // per_dev
    capacity = max(2, 3 * half * top_count // (2 * EXPERTS))
    block_rows = min(512, length)
    score_scale = head_dim ** (-0.5)
    expert_ids = jnp.arange(EXPERTS, dtype=jnp.int32)
    row_ids = jnp.arange(length, dtype=jnp.int32)
    gate_three = gate_weight.reshape(model_width, per_dev, ff_local)
    up_three = up_weight.reshape(model_width, per_dev, ff_local)
    down_three = down_weight.reshape(per_dev, ff_local, model_width)
    query_sum = jnp.zeros(query_weight.shape, jnp.float32)
    key_sum = jnp.zeros(key_matrix.shape, jnp.float32)
    value_sum = jnp.zeros(value_matrix.shape, jnp.float32)
    output_sum = jnp.zeros(output_weight.shape, jnp.float32)
    router_sum = jnp.zeros(router_weight.shape, jnp.float32)
    attn_gain_sum = jnp.zeros(attention_gain.shape, jnp.float32)
    ffn_gain_sum = jnp.zeros(feedforward_gain.shape, jnp.float32)
    gate_sum = jnp.zeros(gate_weight.shape, jnp.float32)
    up_sum = jnp.zeros(up_weight.shape, jnp.float32)
    down_sum = jnp.zeros(down_weight.shape, jnp.float32)
    layer_outputs = []
    input_grads = []
    for micro_index in range(micro_count):
        states = tokens[micro_index].astype(jnp.float32)
        out_grad = cotangent[micro_index].astype(jnp.float32)
        place = positions[micro_index]
        chosen = routes[micro_index]
        starts = row_ids - place
        cosine_table, sine_table = rope_tables(place, head_dim)
        normed_full, attn_norm_pull = jax.vjp(rms_norm, states, attention_gain)
        normalized_input = normed_full.astype(jnp.bfloat16)
        query_pre = jnp.dot(
            normalized_input, query_weight, preferred_element_type=jnp.float32
        ).reshape(length, kv_local, query_group_count, head_dim)
        query_rows = rotary_apply(query_pre, cosine_table, sine_table).astype(jnp.bfloat16)
        key_pre = jnp.dot(normalized_input, key_matrix, preferred_element_type=jnp.float32).reshape(
            length, kv_local, head_dim
        )
        key_row_states = rotary_apply(key_pre, cosine_table, sine_table).astype(jnp.bfloat16)
        value_rows = (
            jnp.dot(normalized_input, value_matrix, preferred_element_type=jnp.float32)
            .astype(jnp.bfloat16)
            .reshape(length, kv_local, head_dim)
        )
        attention_output, log_totals = attention_forward(
            query_rows, key_row_states, value_rows, starts, row_ids, block_rows, score_scale
        )
        attention_output = attention_output.reshape(length, kv_local * query_group_count * head_dim)
        attn_part = jnp.dot(attention_output, output_weight, preferred_element_type=jnp.float32)
        hidden_state = states + lax.psum(attn_part, "tensor")
        normed_ffn_full, ffn_norm_pull = jax.vjp(rms_norm, hidden_state, feedforward_gain)
        normed_ffn = normed_ffn_full.astype(jnp.bfloat16)
        state_half = lax.dynamic_slice_in_dim(normed_ffn, offset, half, 0)
        route_half = lax.dynamic_slice_in_dim(chosen, offset, half, 0)
        grad_half = lax.dynamic_slice_in_dim(out_grad, offset, half, 0)
        route_mask = (route_half[..., None] == expert_ids[None, None, :]).astype(jnp.float32)

        def gate_softmax(logits, route_mask=route_mask):
            return jax.nn.softmax(jnp.sum(logits[:, None, :] * route_mask, axis=-1), axis=-1)

        logits = jnp.dot(state_half, router_weight, preferred_element_type=jnp.float32)
        gate_probs, gate_pull = jax.vjp(gate_softmax, logits)
        flat_routes = route_half.reshape(-1)
        route_onehot = (flat_routes[:, None] == expert_ids[None, :]).astype(jnp.int32)
        ranks = jnp.sum((jnp.cumsum(route_onehot, axis=0) - route_onehot) * route_onehot, axis=1)
        slot_index = flat_routes * capacity + ranks
        copies = jnp.repeat(state_half, top_count, axis=0)
        send_rows = (
            jnp.zeros((EXPERTS * capacity, model_width), jnp.bfloat16).at[slot_index].set(copies)
        )
        received = lax.all_to_all(
            spread_rows(send_rows, group, capacity, n_dev, per_dev, model_width),
            "expert",
            split_axis=0,
            concat_axis=0,
            tiled=True,
        ).reshape(n_dev, per_dev, capacity, model_width)
        gate_pre = jnp.einsum(
            "skcd,dkf->skcf", received, gate_three, preferred_element_type=jnp.float32
        )
        up_pre = jnp.einsum(
            "skcd,dkf->skcf", received, up_three, preferred_element_type=jnp.float32
        )
        activated, gelu_pull = jax.vjp(gelu_exact, gate_pre)
        expert_hidden = (activated * up_pre).astype(jnp.bfloat16)
        partial_out = jnp.einsum(
            "skcf,kfd->skcd", expert_hidden, down_three, preferred_element_type=jnp.float32
        )
        back_rows = lax.all_to_all(
            partial_out.reshape(n_dev, per_dev * capacity, model_width).astype(jnp.bfloat16),
            "expert",
            split_axis=0,
            concat_axis=0,
            tiled=True,
        ).astype(jnp.float32)
        returned_rows = collect_rows(
            back_rows, group, capacity, model_width, slot_index, half, top_count
        )
        mixture_half = jnp.sum(gate_probs[..., None] * returned_rows, axis=1)
        mixture = lax.all_gather(
            mixture_half.astype(jnp.bfloat16), "tensor", axis=0, tiled=True
        ).astype(mixture_half.dtype)
        layer_outputs.append((hidden_state + mixture).astype(jnp.bfloat16))
        gate_grad = jnp.sum(grad_half[:, None, :] * returned_rows, axis=-1)
        row_grad = (
            (gate_probs[..., None] * grad_half[:, None, :])
            .astype(jnp.bfloat16)
            .reshape(-1, model_width)
        )
        send_grad = (
            jnp.zeros((EXPERTS * capacity, model_width), jnp.bfloat16).at[slot_index].set(row_grad)
        )
        grad_received = lax.all_to_all(
            spread_rows(send_grad, group, capacity, n_dev, per_dev, model_width),
            "expert",
            split_axis=0,
            concat_axis=0,
            tiled=True,
        ).reshape(n_dev, per_dev, capacity, model_width)
        hidden_grad = jnp.einsum(
            "skcd,kfd->skcf", grad_received, down_three, preferred_element_type=jnp.float32
        )
        down_part = jnp.einsum(
            "skcf,skcd->kfd", expert_hidden, grad_received, preferred_element_type=jnp.float32
        ).reshape(down_weight.shape)
        gate_pre_grad = gelu_pull(hidden_grad * up_pre)[0].astype(jnp.bfloat16)
        up_pre_grad = (hidden_grad * activated).astype(jnp.bfloat16)
        gate_part = jnp.einsum(
            "skcd,skcf->dkf", received, gate_pre_grad, preferred_element_type=jnp.float32
        ).reshape(gate_weight.shape)
        up_part = jnp.einsum(
            "skcd,skcf->dkf", received, up_pre_grad, preferred_element_type=jnp.float32
        ).reshape(up_weight.shape)
        input_part = jnp.einsum(
            "skcf,dkf->skcd", gate_pre_grad, gate_three, preferred_element_type=jnp.float32
        )
        input_part = input_part + jnp.einsum(
            "skcf,dkf->skcd", up_pre_grad, up_three, preferred_element_type=jnp.float32
        )
        input_back = lax.all_to_all(
            input_part.reshape(n_dev, per_dev * capacity, model_width).astype(jnp.bfloat16),
            "expert",
            split_axis=0,
            concat_axis=0,
            tiled=True,
        ).astype(jnp.float32)
        route_input = collect_rows(
            input_back, group, capacity, model_width, slot_index, half, top_count
        )
        logit_grad = gate_pull(gate_grad)[0].astype(jnp.bfloat16)
        router_part = jnp.dot(state_half.T, logit_grad, preferred_element_type=jnp.float32)
        ffn_half_grad = jnp.sum(route_input, axis=1) + jnp.dot(
            logit_grad, router_weight.T, preferred_element_type=jnp.float32
        )
        gate_sum = gate_sum + gate_part
        up_sum = up_sum + up_part
        down_sum = down_sum + down_part
        router_sum = router_sum + router_part
        normed_ffn_grad = lax.all_gather(ffn_half_grad, "tensor", axis=0, tiled=True)
        state_norm_grad, ffn_gain_grad = ffn_norm_pull(normed_ffn_grad)
        state_grad = out_grad + state_norm_grad
        ffn_gain_sum = ffn_gain_sum + ffn_gain_grad
        attention_grad = state_grad.astype(jnp.bfloat16)
        output_sum = output_sum + jnp.dot(
            attention_output.T, attention_grad, preferred_element_type=jnp.float32
        )
        attended_grad = (
            jnp.dot(attention_grad, output_weight.T, preferred_element_type=jnp.float32)
            .astype(jnp.bfloat16)
            .reshape(length, kv_local, query_group_count, head_dim)
        )
        query_grad, key_grad, value_grad = attention_backward(
            query_rows,
            key_row_states,
            value_rows,
            starts,
            row_ids,
            block_rows,
            score_scale,
            log_totals,
            attended_grad,
        )
        query_grad = (
            unrotate(query_grad, cosine_table, sine_table).astype(jnp.bfloat16).reshape(length, -1)
        )
        key_grad = (
            unrotate(key_grad, cosine_table, sine_table).astype(jnp.bfloat16).reshape(length, -1)
        )
        value_grad = value_grad.astype(jnp.bfloat16).reshape(length, -1)
        query_sum = query_sum + jnp.dot(
            normalized_input.T, query_grad, preferred_element_type=jnp.float32
        )
        key_sum = key_sum + jnp.dot(
            normalized_input.T, key_grad, preferred_element_type=jnp.float32
        )
        value_sum = value_sum + jnp.dot(
            normalized_input.T, value_grad, preferred_element_type=jnp.float32
        )
        normed_part = jnp.dot(query_grad, query_weight.T, preferred_element_type=jnp.float32)
        normed_part = normed_part + jnp.dot(
            key_grad, key_matrix.T, preferred_element_type=jnp.float32
        )
        normed_part = normed_part + jnp.dot(
            value_grad, value_matrix.T, preferred_element_type=jnp.float32
        )
        normed_grad = lax.psum(normed_part, "tensor")
        state_in_grad, attn_gain_grad = attn_norm_pull(normed_grad)
        attn_gain_sum = attn_gain_sum + attn_gain_grad
        input_grads.append(state_grad + state_in_grad)
    gate_sum, up_sum, down_sum, router_sum = lax.psum(
        (gate_sum, up_sum, down_sum, router_sum), "tensor"
    )
    reduced = lax.psum(
        (query_sum, key_sum, value_sum, output_sum, router_sum, attn_gain_sum, ffn_gain_sum),
        "expert",
    )
    return (
        jnp.stack(layer_outputs),
        jnp.stack(input_grads),
        reduced[5],
        reduced[6],
        reduced[0],
        reduced[1],
        reduced[2],
        reduced[3],
        reduced[4],
        gate_sum,
        up_sum,
        down_sum,
    )


def solution(mesh):
    in_specs = (
        P(None, "expert", None),
        P(None, "expert", None),
        P(None, "expert"),
        P(None, "expert", None),
        P(),
        P(),
        P(None, "tensor"),
        P(None, "tensor"),
        P(None, "tensor"),
        P("tensor", None),
        P(),
        P(None, "expert"),
        P(None, "expert"),
        P("expert", None),
    )
    out_specs = (
        P(None, "expert", None),
        P(None, "expert", None),
        P(),
        P(),
        P(None, "tensor"),
        P(None, "tensor"),
        P(None, "tensor"),
        P("tensor", None),
        P(),
        P(None, "expert"),
        P(None, "expert"),
        P("expert", None),
    )
    return jax.shard_map(local, mesh=mesh, in_specs=in_specs, out_specs=out_specs, check_vma=False)
```

profile of v0, /device:TPU:16, one launch (start us, length us, event | category | flops | bytes accessed | tf_op | source)
XLA Modules:
  0.0 876.7 jit_solution(1799834284221418255)
XLA Ops:
  16.7 4.3 copy.209
  34.5 19.2 %all-reduce.12.cloned.1.call-done = (f32[128,1536]{1,0:T(8,128)}, f32[128,1536]{1,0:T(8,128)}) async-done(((f32[128,1536]{1,0:T(8,128)}, f32[128,1536]{1,0:T(8,128)}), (f32[128,1536]{1,0:T(8,128)}, f32[128,1536]{1,0:T(8,128)})) %all-reduce.12.cloned.1.call-update) | async-done | bytes 1572880 | tf_op jit(solution)/shard_map/psum | solution.py:243
  60.2 3.5 scatter_custom_fusion
  63.7 7.0 all-to-all-start
  82.9 3.8 scatter_custom_fusion.2
  86.7 11.9 %all-to-all-done = bf16[16,24,1536]{2,1,0:T(8,128)(2,1)S(1)} async-done(((bf16[16,24,1536]{2,1,0:T(8,128)(2,1)}), bf16[16,24,1536]{2,1,0:T(8,128)(2,1)S(1)}, u32[]{:S(2)}, u32[]{:S(2)}) %all-to-all-start) | async-done | bytes 1179680 | tf_op jit(solution)/shard_map/all_to_all | solution.py:264
  98.6 6.2 all-to-all-start.4
  107.7 10.6 %reshape.1165 = bf16[1536,2,768]{2,1,0:T(2,128)(2,1)} reshape(bf16[1536,1536]{1,0:T(8,128)(2,1)} %param.25) | data formatting | bytes 9437184 | tf_op jit(solution)/shard_map/reshape | solution.py:201
  118.4 10.6 %reshape.1166 = bf16[1536,2,768]{2,1,0:T(2,128)(2,1)} reshape(bf16[1536,1536]{1,0:T(8,128)(2,1)} %param.26) | data formatting | bytes 9437184 | tf_op jit(solution)/shard_map/reshape | solution.py:202
  149.9 3.5 scatter_custom_fusion.1
  154.6 6.9 all-to-all-start.2
  163.2 4.0 scatter_custom_fusion.3
  170.9 3.9 fusion.12
  175.7 4.8 multiply_convert_fusion.3
  180.5 7.1 all-to-all-done.2
  187.6 5.9 all-to-all-start.6
  193.5 5.4 fusion.45
  199.0 4.5 fusion.8
  214.6 6.2 all-to-all-done.6
  220.8 5.2 all-to-all-start.5
  227.9 7.6 multiply_convert_fusion.2
  245.3 5.2 fusion.254
  252.5 6.4 all-to-all-start.1
  258.9 9.4 %bitcast_add_fusion.2 = f32[2,768,1536]{2,1,0:T(8,128)} fusion(f32[2,768,1536,1]{2,1,3,0:T(8,128)} %fusion.254, bf16[16,2,12,768]{3,0,2,1:T(8,128)(2,1)} %copy-done.164, bf16[16,2,12,1536]{3,0,2,1:T(8,128)(2,1)} %bitcast.686), kind=kOutput, calls=%fused_computation.10 | convolution fusion | flops 908328960 | bytes 20643840 | tf_op jit(solution)/shard_map/skcd,skcf->dkf/dot_general | solution.py:321
  268.3 9.6 %copy.260 = f32[1536,1536]{1,0:T(8,128)} copy(f32[1536,1536]{0,1:T(8,128)} %bitcast.650) | data formatting | bytes 18874368 | tf_op jit(solution)/shard_map/add | solution.py:348
  277.9 6.6 fusion.255
  286.3 5.2 all-to-all-start.7
  291.5 9.4 %bitcast_add_fusion.1 = f32[2,768,1536]{2,1,0:T(8,128)} fusion(f32[2,768,1536,1]{2,1,3,0:T(8,128)} %fusion.255, bf16[16,2,12,768]{3,0,2,1:T(8,128)(2,1)} %copy-done.57, bf16[16,2,12,1536]{3,0,2,1:T(8,128)(2,1)} %bitcast.687), kind=kOutput, calls=%fused_computation.9 | convolution fusion | flops 908328960 | bytes 20643840 | tf_op jit(solution)/shard_map/skcd,skcf->dkf/dot_general | solution.py:324
  300.9 9.6 %copy.261 = f32[1536,1536]{1,0:T(8,128)} copy(f32[1536,1536]{0,1:T(8,128)} %bitcast.649) | data formatting | bytes 18874368 | tf_op jit(solution)/shard_map/add | solution.py:349
  310.4 6.6 fusion.256
  317.9 6.1 all-to-all-start.3
  324.2 9.4 %bitcast_add_fusion = f32[2,768,1536]{2,1,0:T(8,128)} fusion(f32[2,768,1536,1]{2,1,3,0:T(8,128)} %fusion.256, bf16[16,2,12,768]{3,0,2,1:T(8,128)(2,1)} %copy-done.48, bf16[16,2,12,1536]{3,0,2,1:T(8,128)(2,1)} %bitcast.684), kind=kOutput, calls=%fused_computation.8 | convolution fusion | flops 908328960 | bytes 20643840 | tf_op jit(solution)/shard_map/skcf,skcd->kfd/dot_general | solution.py:316
  338.4 3.4 gather_fusion
  343.5 3.5 multiply_reduce_fusion.1
  347.1 3.4 gather_fusion.3
  354.5 3.1 reduce_sum.339
  360.6 3.4 gather_fusion.1
  365.7 2.8 multiply_reduce_fusion
  372.6 3.0 multiply_reduce_fusion.7
  411.2 3.1 convolution_add_fusion.1
  414.3 3.7 convolution_add_fusion
  418.0 82.7 %all-reduce.10.cloned.1.call-done = (f32[128,1536]{1,0:T(8,128)}, f32[128,1536]{1,0:T(8,128)}, f32[1536,32]{0,1:T(8,128)}, f32[1536,1536]{1,0:T(8,128)}, f32[1536,1536]{1,0:T(8,128)}, /*index=5*/f32[1536,1536]{1,0:T(8,128)}) async-done(((f32[128,1536]{1,0:T(8,128)}, f32[128,1536]{1,0:T(8,128)}, f32[1536,32]{0,1:T(8,128)}, f32[1536,1536]{1,0:T(8,128)}, f32[1536,1536]{1,0:T(8,128)}, ...) | async-done | bytes 30081040 | tf_op jit(solution)/shard_map/psum | solution.py:399
  505.4 68.1 %all-reduce = (f32[1536]{0:T(1024)}, f32[1536]{0:T(1024)}) all-reduce(f32[1536]{0:T(1024)S(1)} %add.333, f32[1536]{0:T(1024)S(1)} %copy-done.107), channel_id=1, replica_groups=mesh['expert'=16,'tensor'=2] {'expert'}, use_global_device_ids=true, to_apply=%region_46.47 | all-reduce | flops 3072 | bytes 24576 | tf_op jit(solution)/shard_map/psum | solution.py:406
  577.4 261.6 %all-reduce.8.cloned.1.call-done = (f32[1536,768]{1,0:T(8,128)}, f32[1536,128]{1,0:T(8,128)}, f32[1536,128]{1,0:T(8,128)}, f32[768,1536]{1,0:T(8,128)}, f32[1536,32]{0,1:T(8,128)}) async-done(((f32[1536,768]{1,0:T(8,128)}, f32[1536,128]{1,0:T(8,128)}, f32[1536,128]{1,0:T(8,128)}, f32[768,1536]{1,0:T(8,128)}, f32[1536,32]{0,1:T(8,128)}), (f32[1536,768]{1,0:T(8,128)}, f32[1536,128]{1,0:T(8,128)}, ...) | async-done | bytes 11206672 | tf_op jit(solution)/shard_map/psum | solution.py:406
  838.9 5.0 copy.358
  849.1 8.5 copy.363
  857.6 8.4 copy.364
  865.9 3.7 copy.365
  (562 shorter events, 167.0 us)
Async XLA Ops:
  7.2 19.7 %copy-start = (bf16[768,1536]{1,0:T(8,128)(2,1)S(1)}, bf16[768,1536]{1,0:T(8,128)(2,1)}, u32[]{:S(2)}) copy-start(bf16[768,1536]{1,0:T(8,128)(2,1)} %param.23) | copy-start | bytes 7077892
  7.2 46.5 %all-reduce.12.cloned.1.call-start = ((), (), s32[]{:S(2)}) async-start(), calls=%async_computation.10 | async-start | bytes 3145728 | tf_op jit(solution)/shard_map/psum | solution.py:243
  11.8 9.2 %copy-start.112 = (f32[128]{0:T(128)}, f32[128]{0:T(128)S(1)}, u32[]{:S(2)}) copy-start(f32[128]{0:T(128)S(1)} %get-tuple-element.229) | copy-start | bytes 1540
  11.8 11.8 %copy-start.116 = (f32[128]{0:T(128)}, f32[128]{0:T(128)S(1)}, u32[]{:S(2)}) copy-start(f32[128]{0:T(128)S(1)} %get-tuple-element.230) | copy-start | bytes 1540
  16.7 12.1 %copy-start.106 = (bf16[128,128,1]{1,0,2:T(8,128)(2,1)}, bf16[128,128,1]{1,0,2:T(8,128)(2,1)S(1)}, u32[]{:S(2)}) copy-start(bf16[128,128,1]{1,0,2:T(8,128)(2,1)S(1)} %fusion.79) | copy-start | bytes 98308
  33.1 45.8 %copy-start.110 = (s32[1,64,4]{1,2,0:T(4,128)}, s32[1,64,4]{1,2,0:T(4,128)S(1)}, u32[]{:S(2)}) copy-start(s32[1,64,4]{1,2,0:T(4,128)S(1)} %get-tuple-element.226) | copy-start | bytes 3076
  33.1 121.5 %copy-start.108 = (s32[1,64,4]{1,2,0:T(4,128)}, s32[1,64,4]{1,2,0:T(4,128)S(1)}, u32[]{:S(2)}) copy-start(s32[1,64,4]{1,2,0:T(4,128)S(1)} %get-tuple-element.166) | copy-start | bytes 3076
  34.5 25.7 %copy-start.143 = (s32[256,1]{0,1:T(1,128)}, s32[256,1]{0,1:T(1,128)S(1)}, u32[]{:S(2)}) copy-start(s32[256,1]{0,1:T(1,128)S(1)} %compare_select_fusion.1) | copy-start | bytes 3076
  63.7 34.9 %all-to-all-start = ((bf16[16,24,1536]{2,1,0:T(8,128)(2,1)}), bf16[16,24,1536]{2,1,0:T(8,128)(2,1)S(1)}, u32[]{:S(2)}, u32[]{:S(2)}) async-start(bf16[16,24,1536]{2,1,0:T(8,128)(2,1)} %bitcast.668), calls=%async_computation | async-start | bytes 2359296 | tf_op jit(solution)/shard_map/all_to_all | solution.py:264
  78.9 7.8 copy-start.87
  78.9 7.8 copy-start.125
  98.6 56.0 %all-to-all-start.4 = ((bf16[16,24,1536]{2,1,0:T(8,128)(2,1)}), bf16[16,24,1536]{2,1,0:T(8,128)(2,1)}, u32[]{:S(2)}, u32[]{:S(2)}) async-start(bf16[16,24,1536]{2,1,0:T(8,128)(2,1)} %bitcast.665), calls=%async_computation.4 | async-start | bytes 2359296 | tf_op jit(solution)/shard_map/all_to_all | solution.py:306
  118.4 10.6 %copy-start.135 = (s32[1,64,4]{1,2,0:T(4,128)S(1)}, s32[1,64,4]{1,2,0:T(4,128)}, u32[]{:S(2)}) copy-start(s32[1,64,4]{1,2,0:T(4,128)} %get-tuple-element.165) | copy-start | bytes 3076
  137.6 7.4 copy-start.121
  154.6 13.2 %copy-start.141 = (f32[64]{0:T(128)}, f32[64]{0:T(128)S(1)}, u32[]{:S(2)}) copy-start(f32[64]{0:T(128)S(1)} %fusion.230) | copy-start | bytes 772
  154.6 33.0 %all-to-all-start.2 = ((bf16[16,24,1536]{2,1,0:T(8,128)(2,1)}), bf16[16,24,1536]{2,1,0:T(8,128)(2,1)}, u32[]{:S(2)}, u32[]{:S(2)}) async-start(bf16[16,24,1536]{2,1,0:T(8,128)(2,1)} %bitcast.667), calls=%async_computation.2 | async-start | bytes 2359296 | tf_op jit(solution)/shard_map/all_to_all | solution.py:264
  180.5 23.0 %copy-start.56 = (bf16[16,2,12,768]{3,0,2,1:T(8,128)(2,1)}, bf16[16,2,12,768]{3,0,2,1:T(8,128)(2,1)S(1)}, u32[]{:S(2)}) copy-start(bf16[16,2,12,768]{3,0,2,1:T(8,128)(2,1)S(1)} %get-tuple-element.159) | copy-start | bytes 1769476
  187.6 15.9 %slice-start = ((s8[4718592]{0:T(1024)(128)(4,1)}), s8[524288]{0:T(1024)(128)(4,1)S(1)}, s32[]{:S(2)}) async-start(s8[4718592]{0:T(1024)(128)(4,1)} %bitcast.627), calls=%async_computation.11 | async-start | bytes 1048576
  187.6 33.2 %all-to-all-start.6 = ((bf16[16,24,1536]{2,1,0:T(8,128)(2,1)}), bf16[16,24,1536]{2,1,0:T(8,128)(2,1)}, u32[]{:S(2)}, u32[]{:S(2)}) async-start(bf16[16,24,1536]{2,1,0:T(8,128)(2,1)} %bitcast.666), calls=%async_computation.6 | async-start | bytes 2359296 | tf_op jit(solution)/shard_map/all_to_all | solution.py:306
  193.5 10.0 %slice-start.1 = ((s8[4718592]{0:T(1024)(128)(4,1)}), s8[4194304]{0:T(1024)(128)(4,1)S(1)}, s32[]{:S(2)}) async-start(s8[4718592]{0:T(1024)(128)(4,1)} %bitcast.627), calls=%async_computation.12 | async-start | bytes 8388608
  199.0 8.0 copy-start.47
  199.0 8.0 slice-start.6
  205.3 7.2 slice-start.13
  220.8 31.7 %all-to-all-start.5 = ((bf16[16,24,1536]{2,1,0:T(8,128)(2,1)}), bf16[16,24,1536]{2,1,0:T(8,128)(2,1)S(1)}, u32[]{:S(2)}, u32[]{:S(2)}) async-start(bf16[16,24,1536]{2,1,0:T(8,128)(2,1)} %copy.240), calls=%async_computation.5 | async-start | bytes 2359296 | tf_op jit(solution)/shard_map/all_to_all | solution.py:333
  226.1 9.5 %slice-start.2 = ((s8[4718592]{0:T(1024)(128)(4,1)}), s8[4194304]{0:T(1024)(128)(4,1)S(1)}, s32[]{:S(2)}) async-start(s8[4718592]{0:T(1024)(128)(4,1)} %bitcast.630), calls=%async_computation.13 | async-start | bytes 8388608
  226.1 11.2 %slice-start.15 = ((s8[4718592]{0:T(1024)(128)(4,1)}), s8[4194304]{0:T(1024)(128)(4,1)S(1)}, s32[]{:S(2)}) async-start(s8[4718592]{0:T(1024)(128)(4,1)} %bitcast.660), calls=%async_computation.26 | async-start | bytes 8388608
  227.9 7.7 copy-start.42
  227.9 7.7 slice-start.3
  227.9 7.7 copy-start.44
  227.9 7.7 copy-start.165
  227.9 9.4 %slice-start.16 = ((s8[4718592]{0:T(1024)(128)(4,1)}), s8[524288]{0:T(1024)(128)(4,1)S(1)}, s32[]{:S(2)}) async-start(s8[4718592]{0:T(1024)(128)(4,1)} %bitcast.660), calls=%async_computation.27 | async-start | bytes 1048576
  252.5 33.7 %all-to-all-start.1 = ((bf16[16,24,1536]{2,1,0:T(8,128)(2,1)}), bf16[16,24,1536]{2,1,0:T(8,128)(2,1)}, u32[]{:S(2)}, u32[]{:S(2)}) async-start(bf16[16,24,1536]{2,1,0:T(8,128)(2,1)} %copy.222), calls=%async_computation.1 | async-start | bytes 2359296 | tf_op jit(solution)/shard_map/all_to_all | solution.py:282
  286.3 31.7 %all-to-all-start.7 = ((bf16[16,24,1536]{2,1,0:T(8,128)(2,1)}), bf16[16,24,1536]{2,1,0:T(8,128)(2,1)}, u32[]{:S(2)}, u32[]{:S(2)}) async-start(bf16[16,24,1536]{2,1,0:T(8,128)(2,1)} %copy.252), calls=%async_computation.7 | async-start | bytes 2359296 | tf_op jit(solution)/shard_map/all_to_all | solution.py:333
  317.9 42.7 %all-to-all-start.3 = ((bf16[16,24,1536]{2,1,0:T(8,128)(2,1)}), bf16[16,24,1536]{2,1,0:T(8,128)(2,1)}, u32[]{:S(2)}, u32[]{:S(2)}) async-start(bf16[16,24,1536]{2,1,0:T(8,128)(2,1)} %copy.235), calls=%async_computation.3 | async-start | bytes 2359296 | tf_op jit(solution)/shard_map/all_to_all | solution.py:282
  324.0 9.6 %copy-start.130 = (s32[1024]{0:T(1024)S(1)}, s32[1024]{0:T(1024)}, u32[]{:S(2)}) copy-start(s32[1024]{0:T(1024)} %pad_clamp_fusion.1) | copy-start | bytes 12292
  324.0 176.7 %all-reduce.10.cloned.1.call-start = ((), (), s32[]{:S(2)}) async-start(), calls=%async_computation.9 | async-start | bytes 60162048 | tf_op jit(solution)/shard_map/psum | solution.py:399
  372.5 7.4 copy-start.13
  372.6 7.4 copy-start.23
  404.5 434.4 %all-reduce.8.cloned.1.call-start = ((), (), s32[]{:S(2)}) async-start(), calls=%async_computation.8 | async-start | bytes 22413312 | tf_op jit(solution)/shard_map/psum | solution.py:406
  504.7 68.8 %copy-start.153 = (f32[128]{0:T(128)S(1)}, f32[128]{0:T(128)}, u32[]{:S(2)}) copy-start(f32[128]{0:T(128)} %copy-done.152) | copy-start | bytes 1540
  504.7 68.8 %copy-start.151 = (f32[128]{0:T(128)S(1)}, f32[128]{0:T(128)}, u32[]{:S(2)}) copy-start(f32[128]{0:T(128)} %copy-done.150) | copy-start | bytes 1540
  504.7 68.8 %copy-start.115 = (f32[128]{0:T(128)S(1)}, f32[128]{0:T(128)}, u32[]{:S(2)}) copy-start(f32[128]{0:T(128)} %copy-done.112) | copy-start | bytes 1540
  504.7 68.8 %copy-start.119 = (f32[128]{0:T(128)S(1)}, f32[128]{0:T(128)}, u32[]{:S(2)}) copy-start(f32[128]{0:T(128)} %copy-done.116) | copy-start | bytes 1540
  838.9 7.3 slice-start.17
  838.9 7.3 slice-start.18
  849.1 16.8 %slice-start.10 = ((s8[9437184]{0:T(1024)(128)(4,1)}), s8[4194304]{0:T(1024)(128)(4,1)S(1)}, s32[]{:S(2)}) async-start(s8[9437184]{0:T(1024)(128)(4,1)} %bitcast.647), calls=%async_computation.21 | async-start | bytes 8388608
  849.1 16.8 %slice-start.11 = ((s8[9437184]{0:T(1024)(128)(4,1)}), s8[4194304]{0:T(1024)(128)(4,1)S(1)}, s32[]{:S(2)}) async-start(s8[9437184]{0:T(1024)(128)(4,1)} %bitcast.647), calls=%async_computation.22 | async-start | bytes 8388608
  857.6 8.4 slice-start.12
  (149 other events, 364.5 us)
Sparse Core Ops, SparseCore 0:
  31.9 21.7 all-reduce.11
  404.6 96.0 all-reduce.9
  507.7 331.1 all-reduce.7
where the time goes:
time: 891 us; the launch traced here: 877 us
  waiting for transfers between devices  393 us (44%)
  local copies, waits for them, and re-layouts  159 us (18%)
  matrix products  126 us (14%)
  blocking collectives  77.5 us (9%)
  other arithmetic  54.7 us (6%)
  starting transfers between devices  49.4 us (6%)
  between operations  16.5 us (2%)
    psum x1, waiting for transfers between devices, local(): lax.psum((query_sum, key_sum, value_sum, output_sum, router_sum, attn_gai...  262 us
    psum x1, waiting for transfers between devices, local(): normed_grad = lax.psum(normed_part, 'tensor')  82.7 us
    psum x1, blocking collectives, local(): lax.psum((query_sum, key_sum, value_sum, output_sum, router_sum, attn_gai...  68.1 us
    unnamed x381, local copies, waits for them, and re-layouts  48.2 us
    psum x1, waiting for transfers between devices, local(): hidden_state = states + lax.psum(attn_part, 'tensor')  19.2 us
    all_to_all x2, waiting for transfers between devices, local(): lax.all_to_all(spread_rows(send_rows, group, capacity, n_dev, per_dev, mo...  19 us
  transfers between devices with their start and end apart: 11, of which 9 were waited for; matrix products, arithmetic and copies ran while one was open for 27% of the time, Pallas kernels for 0%

commit v1 on v0

--- a/solution.py
+++ b/solution.py
@@ -1,6 +1,10 @@
+import functools
+
 import jax
 import jax.numpy as jnp
 from jax import lax
+from jax.experimental import pallas as pl
+from jax.experimental.pallas import tpu as pltpu
 from jax.sharding import PartitionSpec as P
 
 HEAD_SIZE = 128
@@ -255,7 +259,10 @@
         gate_probs, gate_pull = jax.vjp(gate_softmax, logits)
         flat_routes = route_half.reshape(-1)
         route_onehot = (flat_routes[:, None] == expert_ids[None, :]).astype(jnp.int32)
-        ranks = jnp.sum((jnp.cumsum(route_onehot, axis=0) - route_onehot) * route_onehot, axis=1)
+        ahead = jnp.tril(jnp.ones((half * top_count, half * top_count), jnp.float32), -1)
+        ranks = jnp.sum(
+            jnp.dot(ahead, route_onehot.astype(jnp.float32)).astype(jnp.int32) * route_onehot, axis=1
+        )
         slot_index = flat_routes * capacity + ranks
         copies = jnp.repeat(state_half, top_count, axis=0)
         send_rows = (
@@ -417,6 +424,774 @@
         reduced[2],
         reduced[3],
         reduced[4],
+        gate_sum,
+        up_sum,
+        down_sum,
+    )
+
+
+MESH = pl.DeviceIdType.MESH
+ANY = pl.ANY
+VMEM_LIMIT = 60 * 2**20
+
+
+def mm(a, b):
+    return lax.dot_general(a, b, (((1,), (0,)), ((), ())), preferred_element_type=jnp.float32)
+
+
+def mm_nt(a, b):
+    return lax.dot_general(a, b, (((1,), (1,)), ((), ())), preferred_element_type=jnp.float32)
+
+
+def mm_tn(a, b):
+    return lax.dot_general(a, b, (((0,), (0,)), ((), ())), preferred_element_type=jnp.float32)
+
+
+def remote(src, dst, send_sem, recv_sem, device):
+    return pltpu.make_async_remote_copy(
+        src_ref=src,
+        dst_ref=dst,
+        send_sem=send_sem,
+        recv_sem=recv_sem,
+        device_id=device,
+        device_id_type=MESH,
+    )
+
+
+def tiles(count, body):
+    def step(i, carry):
+        body(i)
+        return carry
+
+    lax.fori_loop(0, count, step, 0)
+
+
+def cols(i, width):
+    return pl.ds(pl.multiple_of(i * width, width), width)
+
+
+def moe_kernel(
+    x_ref, g_ref, rt_ref, wg_hbm, wu_hbm, wd_hbm,
+    mix_ref, dx_ref, rx_ref, rh_ref, rg_ref, ru_ref, re_ref,
+    xz, gz, rz, xs, gs, xr, gr, eg, hid, gpg, upg, ys, ds_, yr, dr, zy, zd, yz, dz,
+    onehot, prob, gg, wg, wu, wd,
+    r_s, r_r, za_s, za_r, xa_s, xa_r, xb_s, xb_r, zb_s, zb_r, pair_s, pair_r, w_sem, own_sem,
+):
+    e = lax.axis_index("expert")
+    c = lax.axis_index("tensor")
+    z = e // 4
+    o = lax.rem(e, 4) * 2 + c
+    micro = x_ref.shape[0]
+    half = x_ref.shape[1] // 2
+    width = g_ref.shape[2]
+    ff = wg.shape[1]
+    col = 4 * half
+    rows = xs.shape[1]
+    blk = rows // 8
+    cap = blk // 4
+    me = 2 * e + c
+    tw = 256
+    nt = width // tw
+
+    def z_dev(k):
+        return (lax.rem(z + k, 4) * 4 + lax.rem(e, 4), c)
+
+    def z_back(k):
+        return (lax.rem(z + 4 - k, 4) * 4 + lax.rem(e, 4), c)
+
+    def p_dev(d):
+        t = lax.rem(o + d, 8)
+        return (z * 4 + t // 2, lax.rem(t, 2))
+
+    def p_back(d):
+        t = lax.rem(o + 8 - d, 8)
+        return (z * 4 + t // 2, lax.rem(t, 2))
+
+    barrier = pltpu.get_barrier_semaphore()
+    for k in range(1, 4):
+        pl.semaphore_signal(barrier, inc=1, device_id=z_dev(k), device_id_type=MESH)
+    for d in range(1, 8):
+        pl.semaphore_signal(barrier, inc=1, device_id=p_dev(d), device_id_type=MESH)
+    loads = [
+        pltpu.make_async_copy(wg_hbm.at[:, cols(c, ff)], wg, w_sem.at[0]),
+        pltpu.make_async_copy(wu_hbm.at[:, cols(c, ff)], wu, w_sem.at[1]),
+        pltpu.make_async_copy(wd_hbm.at[cols(c, ff), :], wd, w_sem.at[2]),
+    ]
+    for cp in loads:
+        cp.start()
+    pl.semaphore_wait(barrier, 10)
+
+    mine = pl.ds(pl.multiple_of(c * half, half), half)
+    sent = []
+    got_r = []
+    for k in range(1, 4):
+        cp = remote(rt_ref, rz.at[k], r_s.at[k], r_r.at[k], z_dev(k))
+        cp.start()
+        sent.append(cp)
+        got_r.append(cp)
+    got_z = {}
+
+    def z_send(m):
+        for a, (src, dst) in enumerate(((g_ref, gz), (x_ref, xz))):
+            for k in range(1, 4):
+                i = (m * 2 + a) * 4 + k
+                cp = remote(
+                    src.at[m, mine, :], dst.at[m, pl.ds(k * half, half), :],
+                    za_s.at[i], za_r.at[i], z_dev(k),
+                )
+                cp.start()
+                sent.append(cp)
+                got_z[(m, a, k)] = cp
+
+    z_send(0)
+    for m in range(micro):
+        xz[m, 0:half, :] = x_ref[m, mine, :]
+        gz[m, 0:half, :] = g_ref[m, mine, :]
+    rz[0] = rt_ref[...]
+    for cp in got_r:
+        cp.wait_recv()
+
+    lanes = micro * half
+    up = lax.broadcasted_iota(jnp.int32, (lanes, lanes), 0)
+    across = lax.broadcasted_iota(jnp.int32, (lanes, lanes), 1)
+    before = ((up < across) & (up // half == across // half)).astype(jnp.bfloat16)
+    expert = 8 * z + lax.rem(o + lax.broadcasted_iota(jnp.int32, (8, lanes), 0), 8)
+    place_row = lax.broadcasted_iota(jnp.int32, (lanes, col), 0)
+    place_col = lax.broadcasted_iota(jnp.int32, (lanes, col), 1)
+    slots = [jnp.zeros((8, col), jnp.float32) for _ in range(micro)]
+    for k in range(4):
+        named = rz[k]
+        hit = named[0:1, :] == expert
+        for j in range(1, rt_ref.shape[0] // 2):
+            hit = hit | (named[j : j + 1, :] == expert)
+        mask = jnp.where(hit, 1.0, 0.0)
+        rank = mm(mask.astype(jnp.bfloat16), before)
+        slot = (mask * (rank + (cap * k + 1))).astype(jnp.bfloat16)
+        for m in range(micro):
+            at = place_col - k * half
+            put = (at >= 0) & (at < half) & (place_row == at + m * half)
+            slots[m] = slots[m] + mm(slot, put.astype(jnp.bfloat16))
+    number = lax.broadcasted_iota(jnp.int32, (blk, col), 0) + 1
+    for m in range(micro):
+        for d in range(8):
+            row = slots[m][d : d + 1, :].astype(jnp.int32)
+            onehot[m, d * blk : (d + 1) * blk, :] = jnp.where(row == number, 1.0, 0.0).astype(
+                jnp.bfloat16
+            )
+
+    got_p = {}
+
+    def pack(m):
+        for a, (src, out, dst) in enumerate(((gz, gs, gr), (xz, xs, xr))):
+            for k in range(1, 4):
+                got_z[(m, a, k)].wait_recv()
+
+            def body(i, src=src, out=out):
+                at = cols(i, tw)
+                out[m, :, at] = mm(onehot[m], src[m, :, at]).astype(jnp.bfloat16)
+
+            tiles(nt, body)
+            if a == 1:
+                out[m, :, width:] = mm(onehot[m], src[m, :, width:]).astype(jnp.bfloat16)
+            dst[m, 0:blk, :] = out[m, 0:blk, :]
+            for d in range(1, 8):
+                i = (m * 2 + a) * 8 + d
+                at = pl.ds(d * blk, blk)
+                cp = remote(
+                    out.at[m, at, :], dst.at[m, at, :], xa_s.at[i], xa_r.at[i], p_dev(d)
+                )
+                cp.start()
+                sent.append(cp)
+                got_p[(m, a, d)] = cp
+
+    for m in range(1, micro):
+        z_send(m)
+    for m in range(micro):
+        pack(m)
+    for cp in loads:
+        cp.wait()
+
+    got_b = {}
+    lane = lax.broadcasted_iota(jnp.int32, (1, 128), 1)
+
+    def to_pair(m):
+        for i, (src, dst) in enumerate(
+            ((xr, rx_ref), (hid, rh_ref), (gpg, rg_ref), (upg, ru_ref), (eg, re_ref))
+        ):
+            src_at = src.at[m, :, 0:width] if i == 0 else src.at[m]
+            n = m * 8 + i
+            cp = remote(src_at, dst.at[c, m], pair_s.at[n], pair_r.at[n], (e, 1 - c))
+            cp.start()
+            sent.append(cp)
+            got_b[("pair", m, i)] = cp
+            cp = pltpu.make_async_copy(src_at, dst.at[c, m], own_sem.at[n])
+            cp.start()
+            loads.append(cp)
+
+    loads.clear()
+
+    def run(m):
+        for a in range(2):
+            for d in range(1, 8):
+                got_p[(m, a, d)].wait_recv()
+        tail = xr[m, :, width:].astype(jnp.float32)
+        pick = (lane == me) | (lane == me + 32)
+        prob[...] = jnp.broadcast_to(
+            jnp.sum(jnp.where(pick, tail, 0.0), axis=1, keepdims=True), (rows, 128)
+        )
+        gg[...] = jnp.zeros_like(gg)
+
+        def weigh(i):
+            at = cols(i, tw)
+            eg[m, :, at] = (prob[:, 0:1] * gr[m, :, at].astype(jnp.float32)).astype(jnp.bfloat16)
+
+        tiles(nt, weigh)
+
+        def inner(i):
+            at = cols(i, tw)
+            xrow = xr[m, :, 0:width]
+            gate = mm(xrow, wg[:, at])
+            upv = mm(xrow, wu[:, at])
+            back = mm_nt(eg[m], wd[at, :])
+            cdf = 0.5 * (1.0 + lax.erf(gate * 0.7071067811865476))
+            act = gate * cdf
+            slope = cdf + gate * (jnp.exp(gate * gate * -0.5) * 0.3989422804014327)
+            hid[m, :, at] = (act * upv).astype(jnp.bfloat16)
+            gpg[m, :, at] = (back * upv * slope).astype(jnp.bfloat16)
+            upg[m, :, at] = (back * act).astype(jnp.bfloat16)
+
+        tiles(ff // tw, inner)
+
+        def outer(i):
+            at = cols(i, tw)
+            low = mm(hid[m], wd[:, at]).astype(jnp.bfloat16).astype(jnp.float32)
+            gg[...] += jnp.broadcast_to(
+                jnp.sum(low * gr[m, :, at].astype(jnp.float32), axis=1, keepdims=True),
+                (rows, 128),
+            )
+            ys[m, :, at] = (prob[:, 0:1] * low).astype(jnp.bfloat16)
+
+        tiles(nt, outer)
+
+        def inputs(i):
+            at = cols(i, tw)
+            ds_[m, :, at] = (mm_nt(gpg[m], wg[at, :]) + mm_nt(upg[m], wu[at, :])).astype(
+                jnp.bfloat16
+            )
+
+        tiles(nt, inputs)
+        total = gg[...]
+        high = total.astype(jnp.bfloat16).astype(jnp.float32)
+        ds_[m, :, width:] = jnp.where(
+            lane == me, high, jnp.where(lane == me + 32, total - high, 0.0)
+        ).astype(jnp.bfloat16)
+        for a, (src, dst) in enumerate(((ds_, dr), (ys, yr))):
+            dst[m, 0:blk, :] = src[m, 0:blk, :]
+            for d in range(1, 8):
+                i = (m * 2 + a) * 8 + d
+                at = pl.ds(d * blk, blk)
+                cp = remote(
+                    src.at[m, at, :], dst.at[m, at, :], xb_s.at[i], xb_r.at[i], p_back(d)
+                )
+                cp.start()
+                sent.append(cp)
+                got_b[(m, a, d)] = cp
+        to_pair(m)
+
+    for m in range(micro):
+        run(m)
+
+    got_c = {}
+
+    def gather(m, a):
+        src, out, dst = ((dr, zd, dz), (yr, zy, yz))[a]
+        for d in range(1, 8):
+            got_b[(m, a, d)].wait_recv()
+
+        def body(i):
+            at = cols(i, tw)
+            out[m, :, at] = mm_tn(onehot[m], src[m, :, at]).astype(jnp.bfloat16)
+
+        tiles(nt, body)
+        if a == 0:
+            out[m, :, width:] = mm_tn(onehot[m], src[m, :, width:]).astype(jnp.bfloat16)
+        for k in range(1, 4):
+            i = (m * 2 + a) * 4 + k
+            at = pl.ds(k * half, half)
+            cp = remote(out.at[m, at, :], dst.at[m, at, :], zb_s.at[i], zb_r.at[i], z_back(k))
+            cp.start()
+            sent.append(cp)
+            got_c[(m, a, k)] = cp
+
+    def finish(m, a):
+        own, other, out = ((zd, dz, dx_ref), (zy, yz, mix_ref))[a]
+        for k in range(1, 4):
+            got_c[(m, a, k)].wait_recv()
+        total = own[m, 0:half, :].astype(jnp.float32)
+        for k in range(1, 4):
+            total = total + other[m, k * half : (k + 1) * half, :].astype(jnp.float32)
+        out[m, mine, :] = total.astype(out.dtype)
+        n = m * 8 + 5 + a
+        cp = remote(
+            out.at[m, mine, :], out.at[m, mine, :], pair_s.at[n], pair_r.at[n], (e, 1 - c)
+        )
+        cp.start()
+        sent.append(cp)
+        got_c[("pair", m, a)] = cp
+
+    order = [(m, a) for a in range(2) for m in range(micro)]
+    for i, (m, a) in enumerate(order):
+        gather(m, a)
+        if i >= 1:
+            finish(*order[i - 1])
+    finish(*order[-1])
+    for m in range(micro):
+        for i in range(5):
+            got_b[("pair", m, i)].wait_recv()
+        for a in range(2):
+            got_c[("pair", m, a)].wait_recv()
+    for cp in loads:
+        cp.wait()
+    for cp in sent:
+        cp.wait_send()
+
+
+def moe_call(xrows, grows, routes_t, gate_weight, up_weight, down_weight):
+    micro, length, wide = xrows.shape
+    width = grows.shape[2]
+    half = length // 2
+    ff = gate_weight.shape[1] // 2
+    cap = 3 * half * 4 // (2 * EXPERTS)
+    rows = 8 * 4 * cap
+    bf = jnp.bfloat16
+    f32 = jnp.float32
+    vmem = pl.BlockSpec(memory_space=pltpu.VMEM)
+    hbm = pl.BlockSpec(memory_space=ANY)
+
+    def buf(*shape, dtype=bf):
+        return pltpu.VMEM(shape, dtype)
+
+    sem = pltpu.SemaphoreType.DMA
+    col = 4 * half
+    return pl.pallas_call(
+        moe_kernel,
+        out_shape=(
+            jax.ShapeDtypeStruct((micro, length, width), bf),
+            jax.ShapeDtypeStruct((micro, length, wide), f32),
+            jax.ShapeDtypeStruct((2, micro, rows, width), bf),
+            jax.ShapeDtypeStruct((2, micro, rows, ff), bf),
+            jax.ShapeDtypeStruct((2, micro, rows, ff), bf),
+            jax.ShapeDtypeStruct((2, micro, rows, ff), bf),
+            jax.ShapeDtypeStruct((2, micro, rows, width), bf),
+        ),
+        in_specs=[vmem, vmem, vmem, hbm, hbm, hbm],
+        out_specs=(vmem, vmem, hbm, hbm, hbm, hbm, hbm),
+        scratch_shapes=[
+            buf(micro, col, wide), buf(micro, col, width), buf(4, 8, micro * half, dtype=jnp.int32),
+            buf(micro, rows, wide), buf(micro, rows, width), buf(micro, rows, wide), buf(micro, rows, width),
+            buf(micro, rows, width), buf(micro, rows, ff), buf(micro, rows, ff), buf(micro, rows, ff),
+            buf(micro, rows, width), buf(micro, rows, wide), buf(micro, rows, width), buf(micro, rows, wide),
+            buf(micro, col, width), buf(micro, col, wide), buf(micro, col, width), buf(micro, col, wide),
+            buf(micro, rows, col), buf(rows, 128, dtype=f32), buf(rows, 128, dtype=f32),
+            buf(width, ff), buf(width, ff), buf(ff, width),
+            sem((4,)), sem((4,)), sem((8 * micro,)), sem((8 * micro,)), sem((16 * micro,)), sem((16 * micro,)),
+            sem((16 * micro,)), sem((16 * micro,)), sem((8 * micro,)), sem((8 * micro,)), sem((8 * micro,)),
+            sem((8 * micro,)), sem((3,)), sem((8 * micro,)),
+        ],
+        compiler_params=pltpu.CompilerParams(
+            collective_id=1, has_side_effects=True, vmem_limit_bytes=VMEM_LIMIT
+        ),
+        cost_estimate=pl.CostEstimate(
+            flops=2 * 6 * micro * rows * width * ff, bytes_accessed=40 * 2**20, transcendentals=0
+        ),
+        name="moe_rows",
+    )(xrows, grows, routes_t, gate_weight, up_weight, down_weight)
+
+
+def grads_kernel(x_ref, h_ref, g_ref, u_ref, e_ref, gate_out, up_out, down_out):
+    gate_out[...] = mm_tn(x_ref[0], g_ref[0])
+    up_out[...] = mm_tn(x_ref[0], u_ref[0])
+    down_out[...] = mm_tn(h_ref[0], e_ref[0])
+
+
+def grads_call(rx, rh, rg, ru, re):
+    _, micro, rows, width = rx.shape
+    ff = rh.shape[3]
+    n = micro * rows
+    tw = 256
+    per = ff // tw
+    f32 = jnp.float32
+    wide = pl.BlockSpec((1, n, width), lambda i: (i // per, 0, 0))
+    thin = pl.BlockSpec((1, n, tw), lambda i: (i // per, 0, i % per))
+    return pl.pallas_call(
+        grads_kernel,
+        grid=(2 * per,),
+        in_specs=[wide, thin, thin, thin, wide],
+        out_specs=(
+            pl.BlockSpec((width, tw), lambda i: (0, i)),
+            pl.BlockSpec((width, tw), lambda i: (0, i)),
+            pl.BlockSpec((tw, width), lambda i: (i, 0)),
+        ),
+        out_shape=(
+            jax.ShapeDtypeStruct((width, 2 * ff), f32),
+            jax.ShapeDtypeStruct((width, 2 * ff), f32),
+            jax.ShapeDtypeStruct((2 * ff, width), f32),
+        ),
+        compiler_params=pltpu.CompilerParams(vmem_limit_bytes=VMEM_LIMIT),
+        cost_estimate=pl.CostEstimate(
+            flops=2 * 6 * n * width * ff, bytes_accessed=45 * 2**20, transcendentals=0
+        ),
+        name="expert_grads",
+    )(
+        rx.reshape(2, n, width), rh.reshape(2, n, ff), rg.reshape(2, n, ff),
+        ru.reshape(2, n, ff), re.reshape(2, n, width),
+    )
+
+
+def reduce_kernel(
+    n_ref, d_ref, a_ref, g_ref, s_ref, oa, ob, os,
+    fn, fd, fa, fg, fs, pa, pb, za, zb, zs,
+    f_s, f_r, y_s, y_r, z_s, z_r, p_s, p_r,
+):
+    e = lax.axis_index("expert")
+    c = lax.axis_index("tensor")
+    z = e // 4
+    q = lax.rem(e, 4)
+    qx = lax.rem(q, 2)
+    qy = q // 2
+    rows = n_ref.shape[0]
+    wn = n_ref.shape[1] // 2
+    wd = d_ref.shape[1] // 2
+    wa = a_ref.shape[1] // 2
+    wg = g_ref.shape[1] // 2
+    ws = s_ref.shape[1] // 4
+    hs = s_ref.shape[0] // 4
+    ha = wn // 4
+    hb = wa // 4
+
+    def flip(bit, by):
+        return lax.rem(bit + by, 2)
+
+    def p_dev(d):
+        return (z * 4 + flip(qy, d // 2) * 2 + flip(qx, d % 2), c)
+
+    def z_dev(k):
+        return (lax.rem(z + k, 4) * 4 + q, c)
+
+    def part(i, size):
+        return pl.ds(pl.multiple_of(i * size, size), size)
+
+    barrier = pltpu.get_barrier_semaphore()
+    for k in range(1, 4):
+        pl.semaphore_signal(barrier, inc=1, device_id=z_dev(k), device_id_type=MESH)
+        pl.semaphore_signal(barrier, inc=1, device_id=p_dev(k), device_id_type=MESH)
+    pl.semaphore_wait(barrier, 6)
+
+    sent = []
+    got = []
+    for d in (3, 1, 2):
+        r = flip(qx, d % 2)
+        s = flip(qy, d // 2)
+        at = pl.ds(d * rows, rows)
+        for i, (src, dst) in enumerate(
+            (
+                (n_ref.at[:, part(r, wn)], fn.at[at, :]),
+                (d_ref.at[:, part(s, wd)], fd.at[at, :]),
+                (a_ref.at[:, part(r, wa)], fa.at[at, :]),
+                (g_ref.at[:, part(s, wg)], fg.at[at, :]),
+                (s_ref.at[part(s * 2 + r, hs), :], fs.at[d]),
+            )
+        ):
+            cp = remote(src, dst, f_s.at[d * 5 + i], f_r.at[d * 5 + i], p_dev(d))
+            cp.start()
+            sent.append(cp)
+            got.append(cp)
+    fn[0:rows, :] = n_ref[:, part(qx, wn)]
+    fd[0:rows, :] = d_ref[:, part(qy, wd)]
+    fa[0:rows, :] = a_ref[:, part(qx, wa)]
+    fg[0:rows, :] = g_ref[:, part(qy, wg)]
+    total = s_ref[part(q, hs), :].astype(jnp.float32)
+    for cp in got:
+        cp.wait_recv()
+    for d in range(1, 4):
+        total = total + fs[d].astype(jnp.float32)
+    fs[0] = total.astype(jnp.bfloat16)
+    tw = 256
+
+    def one(i):
+        at = cols(i, tw)
+        pa[:, at] = mm_tn(fn[...], fd[:, at]).astype(jnp.bfloat16)
+
+    tiles(wd // tw, one)
+
+    def two(i):
+        at = cols(i, tw)
+        pb[:, at] = mm_tn(fa[...], fg[:, at]).astype(jnp.bfloat16)
+
+    tiles(wg // tw, two)
+
+    got = []
+    for k in (2, 1, 3):
+        t = lax.rem(z + k, 4)
+        for i, (src, dst) in enumerate(
+            (
+                (pa.at[part(t, ha), :], za.at[k]),
+                (pb.at[part(t, hb), :], zb.at[k]),
+                (fs.at[0, :, part(t, ws)], zs.at[k]),
+            )
+        ):
+            cp = remote(src, dst, y_s.at[k * 3 + i], y_r.at[k * 3 + i], z_dev(k))
+            cp.start()
+            sent.append(cp)
+            got.append(cp)
+    for cp in got:
+        cp.wait_recv()
+
+    def spots(px, py, t):
+        return (
+            oa.at[part(px * 4 + t, ha), part(py, wd)],
+            ob.at[part(px * 4 + t, hb), part(py, wg)],
+            os.at[part(py * 2 + px, hs), part(t, ws)],
+        )
+
+    def store(ref, first, others):
+        acc = first.astype(jnp.float32)
+        for k in range(1, 4):
+            acc = acc + others[k].astype(jnp.float32)
+        ref[...] = acc.astype(jnp.bfloat16)
+
+    mine = spots(qx, qy, z)
+    store(mine[0], pa[part(z, ha), :], za)
+    store(mine[1], pb[part(z, hb), :], zb)
+    store(mine[2], fs[0, :, part(z, ws)], zs)
+
+    got_z = {}
+    got_p = {}
+
+    def send(ref, i, k, d, j):
+        n = ((k * 3) + i) * 4 + j
+        cp = remote(ref, ref, p_s.at[n], p_r.at[n], p_dev(d))
+        cp.start()
+        sent.append(cp)
+        got_p[(k, i, j)] = cp
+
+    for k in (2, 1, 3):
+        for i in range(3):
+            cp = remote(mine[i], mine[i], z_s.at[k * 3 + i], z_r.at[k * 3 + i], z_dev(k))
+            cp.start()
+            sent.append(cp)
+            got_z[(k, i)] = cp
+
+    def own(k):
+        here = spots(qx, qy, lax.rem(z + 4 - k, 4))
+        if k:
+            for i in range(3):
+                got_z[(k, i)].wait_recv()
+        for i in range(3):
+            send(here[i], i, k, 1, 1)
+            send(here[i], i, k, 2, 2)
+
+    def forward(k):
+        t = lax.rem(z + 4 - k, 4)
+        beside = spots(flip(qx, 1), qy, t)
+        above = spots(qx, flip(qy, 1), t)
+        got_p[(k, 0, 1)].wait_recv()
+        send(beside[0], 0, k, 2, 3)
+        got_p[(k, 2, 1)].wait_recv()
+        send(beside[2], 2, k, 2, 3)
+        got_p[(k, 1, 2)].wait_recv()
+        send(above[1], 1, k, 1, 3)
+
+    turns = (0, 1, 3, 2)
+    for n, k in enumerate(turns):
+        own(k)
+        if n:
+            forward(turns[n - 1])
+    forward(turns[-1])
+    for k in range(4):
+        for i in range(3):
+            first = 2 if i in (0, 2) else 1
+            got_p[(k, i, first)].wait_recv()
+            got_p[(k, i, 3)].wait_recv()
+    for cp in sent:
+        cp.wait_send()
+
+
+def reduce_call(normed, dqkv, attended, agrad, small):
+    bf = jnp.bfloat16
+    rows = normed.shape[0]
+    wn, wd = normed.shape[1], dqkv.shape[1]
+    wa, wg = attended.shape[1], agrad.shape[1]
+    vmem = pl.BlockSpec(memory_space=pltpu.VMEM)
+
+    def buf(*shape):
+        return pltpu.VMEM(shape, bf)
+
+    sem = pltpu.SemaphoreType.DMA
+    hs, ws = small.shape[0] // 4, small.shape[1] // 4
+    return pl.pallas_call(
+        reduce_kernel,
+        out_shape=(
+            jax.ShapeDtypeStruct((wn, wd), bf),
+            jax.ShapeDtypeStruct((wa, wg), bf),
+            jax.ShapeDtypeStruct(small.shape, bf),
+        ),
+        in_specs=[vmem] * 5,
+        out_specs=(vmem,) * 3,
+        scratch_shapes=[
+            buf(4 * rows, wn // 2), buf(4 * rows, wd // 2), buf(4 * rows, wa // 2), buf(4 * rows, wg // 2),
+            buf(4, hs, small.shape[1]),
+            buf(wn // 2, wd // 2), buf(wa // 2, wg // 2),
+            buf(4, wn // 8, wd // 2), buf(4, wa // 8, wg // 2), buf(4, hs, ws),
+            sem((20,)), sem((20,)), sem((12,)), sem((12,)), sem((12,)), sem((12,)), sem((48,)), sem((48,)),
+        ],
+        compiler_params=pltpu.CompilerParams(
+            collective_id=2, has_side_effects=True, vmem_limit_bytes=VMEM_LIMIT
+        ),
+        cost_estimate=pl.CostEstimate(
+            flops=2 * rows * 4 * (wn * wd + wa * wg) // 4, bytes_accessed=10 * 2**20, transcendentals=0
+        ),
+        name="reduce_grads",
+    )(normed, dqkv, attended, agrad, small)
+
+
+def suits(mesh):
+    return mesh.shape["expert"] == 16 and mesh.shape["tensor"] == 2
+
+
+def local_fast(
+    tokens, cotangent, positions, routes, attention_gain, feedforward_gain, query_weight, key_matrix,
+    value_matrix, output_weight, router_weight, gate_weight, up_weight, down_weight,
+):
+    micro_count, length, model_width = tokens.shape
+    head_dim = HEAD_SIZE
+    kv_local = key_matrix.shape[1] // head_dim
+    query_group_count = query_weight.shape[1] // head_dim // kv_local
+    half = length // 2
+    c = lax.axis_index("tensor")
+    f32 = jnp.float32
+    bf = jnp.bfloat16
+    score_scale = head_dim ** (-0.5)
+    row_ids = jnp.arange(length, dtype=jnp.int32)
+    expert_ids = jnp.arange(EXPERTS, dtype=jnp.int32)
+
+    kept = []
+    for m in range(micro_count):
+        states = tokens[m].astype(f32)
+        place = positions[m]
+        tables = rope_tables(place, head_dim)
+        normed_full, attn_pull = jax.vjp(rms_norm, states, attention_gain)
+        normed = normed_full.astype(bf)
+        query_pre = jnp.dot(normed, query_weight, preferred_element_type=f32).reshape(
+            length, kv_local, query_group_count, head_dim
+        )
+        q = rotary_apply(query_pre, *tables).astype(bf)
+        key_pre = jnp.dot(normed, key_matrix, preferred_element_type=f32).reshape(
+            length, kv_local, head_dim
+        )
+        k = rotary_apply(key_pre, *tables).astype(bf)
+        v = (
+            jnp.dot(normed, value_matrix, preferred_element_type=f32)
+            .astype(bf)
+            .reshape(length, kv_local, head_dim)
+        )
+        att, log_totals = attention_forward(
+            q, k, v, row_ids - place, row_ids, length, score_scale
+        )
+        att = att.reshape(length, -1)
+        part = jnp.dot(att, output_weight, preferred_element_type=f32)
+        kept.append((states, place, tables, normed, attn_pull, q, k, v, att, log_totals, part))
+    parts = lax.psum(jnp.stack([t[-1] for t in kept]), "tensor")
+    hidden = jnp.stack([t[0] for t in kept]) + parts
+    ffn_full, ffn_pull = jax.vjp(rms_norm, hidden, feedforward_gain)
+    normed_ffn = ffn_full.astype(bf)
+    logits = jnp.dot(normed_ffn, router_weight, preferred_element_type=f32)
+    mask = jnp.any(routes[..., None] == expert_ids, axis=2)
+    top = jnp.max(jnp.where(mask, logits, -jnp.inf), axis=-1, keepdims=True)
+    weight = jnp.where(mask, jnp.exp(logits - top), 0.0)
+    probs = weight / jnp.sum(weight, axis=-1, keepdims=True)
+    high = lax.reduce_precision(probs, 8, 7)
+    xrows = jnp.concatenate(
+        [
+            normed_ffn, high.astype(bf), (probs - high).astype(bf),
+            jnp.zeros((micro_count, length, 128 - 2 * EXPERTS), bf),
+        ],
+        axis=-1,
+    )
+    mine = lax.dynamic_slice_in_dim(routes, c * half, half, 1)
+    routes_t = mine.transpose(2, 0, 1).reshape(routes.shape[2], micro_count * half)
+    routes_t = jnp.concatenate([routes_t, jnp.full_like(routes_t, -1)], axis=0)
+    mix, dx, rx, rh, rg, ru, re = moe_call(
+        xrows, cotangent, routes_t, gate_weight, up_weight, down_weight
+    )
+    layer_out = (hidden + mix.astype(f32)).astype(bf)
+    gate_sum, up_sum, down_sum = grads_call(rx, rh, rg, ru, re)
+    gate_grad = dx[..., model_width : model_width + EXPERTS] + dx[
+        ..., model_width + EXPERTS : model_width + 2 * EXPERTS
+    ]
+    logit_grad = probs * (gate_grad - jnp.sum(probs * gate_grad, axis=-1, keepdims=True))
+    logit_grad = logit_grad.astype(bf)
+    normed_ffn_grad = dx[..., :model_width] + jnp.dot(
+        logit_grad, router_weight.T, preferred_element_type=f32
+    )
+    state_norm_grad, ffn_gain_grad = ffn_pull(normed_ffn_grad)
+    state_grad = cotangent.astype(f32) + state_norm_grad
+    agrad = state_grad.astype(bf)
+    router_t = jnp.einsum(
+        "mtx,mtd->xd", logit_grad, normed_ffn, preferred_element_type=f32
+    )
+    back = []
+    for m in range(micro_count):
+        states, place, tables, normed, attn_pull, q, k, v, att, log_totals, part = kept[m]
+        attended_grad = (
+            jnp.dot(agrad[m], output_weight.T, preferred_element_type=f32)
+            .astype(bf)
+            .reshape(length, kv_local, query_group_count, head_dim)
+        )
+        dq, dk, dv = attention_backward(
+            q, k, v, row_ids - place, row_ids, length, score_scale, log_totals, attended_grad
+        )
+        dq = unrotate(dq, *tables).astype(bf).reshape(length, -1)
+        dk = unrotate(dk, *tables).astype(bf).reshape(length, -1)
+        dv = dv.astype(bf).reshape(length, -1)
+        part = jnp.dot(dq, query_weight.T, preferred_element_type=f32)
+        part = part + jnp.dot(dk, key_matrix.T, preferred_element_type=f32)
+        part = part + jnp.dot(dv, value_matrix.T, preferred_element_type=f32)
+        back.append((jnp.concatenate([dq, dk, dv], axis=1), part))
+    normed_grad = lax.psum(jnp.stack([t[1] for t in back]), "tensor")
+    input_grads = []
+    attn_gain_grad = jnp.zeros_like(attention_gain)
+    for m in range(micro_count):
+        grad, gain = kept[m][4](normed_grad[m])
+        input_grads.append(state_grad[m] + grad)
+        attn_gain_grad = attn_gain_grad + gain
+    small = jnp.concatenate(
+        [
+            router_t, ffn_gain_grad[None], attn_gain_grad[None],
+            jnp.zeros((64 - EXPERTS - 2, model_width), f32),
+        ],
+        axis=0,
+    ).astype(bf)
+    rows = micro_count * length
+    oa, ob, os = reduce_call(
+        jnp.stack([t[3] for t in kept]).reshape(rows, -1),
+        jnp.stack([t[0] for t in back]).reshape(rows, -1),
+        jnp.stack([t[8] for t in kept]).reshape(rows, -1),
+        agrad.reshape(rows, -1),
+        small,
+    )
+    wq = query_weight.shape[1]
+    os = os.astype(f32)
+    return (
+        layer_out,
+        jnp.stack(input_grads),
+        os[EXPERTS + 1],
+        os[EXPERTS],
+        oa[:, :wq].astype(f32),
+        oa[:, wq : wq + head_dim].astype(f32),
+        oa[:, wq + head_dim :].astype(f32),
+        ob.astype(f32),
+        os[:EXPERTS].T,
         gate_sum,
         up_sum,
         down_sum,
@@ -454,4 +1229,5 @@
         P(None, "expert"),
         P("expert", None),
     )
-    return jax.shard_map(local, mesh=mesh, in_specs=in_specs, out_specs=out_specs, check_vma=False)
+    body = local_fast if suits(mesh) else local
+    return jax.shard_map(body, mesh=mesh, in_specs=in_specs, out_specs=out_specs, check_vma=False)

time: 891 us -> 497 us (0.56); the launches traced: 877 us -> 496 us
  Pallas kernels: 0 us -> 391 us
  waiting for transfers between devices: 393 us -> 8.44 us
  local copies, waits for them, and re-layouts: 159 us -> 24.7 us
  matrix products: 126 us -> 19.5 us
  blocking collectives: 77.5 us -> 0 us
  starting transfers between devices: 49.4 us -> 0.26 us
  other arithmetic: 54.7 us -> 36.9 us
    pallas_call x0 -> x3, Pallas kernels: none -> 391 us  [the longest x1 194 us: moe_call(): pl.pallas_call(moe_kernel, out_shape=(jax.ShapeDtypeStruct((micro, length...]
    psum x3 -> x2, waiting for transfers between devices: 363 us -> 8.41 us  [the longest x1 8.41 us: local_fast(): parts = lax.psum(jnp.stack([t[-1] for t in kept]), 'tensor')]
    dot_general x48 -> x19, matrix products: 120 us -> 16.2 us  [the longest x2 3.34 us: local_fast(): jnp.dot(normed, query_weight, preferred_element_type=f32)]
    psum x1 -> x0, blocking collectives: 68.1 us -> none  [local(): lax.psum((query_sum, key_sum, value_sum, output_sum, router_sum, attn_gai...]
    all_to_all x8 -> x0, starting transfers between devices: 48.8 us -> none  [the longest x2 13.9 us: local(): lax.all_to_all(spread_rows(send_rows, group, capacity, n_dev, per_dev, mo...]
    unnamed x381 -> x185, local copies, waits for them, and re-layouts: 48.2 us -> 13.3 us
    all_to_all x8 -> x0, waiting for transfers between devices: 29.9 us -> none  [the longest x2 19 us: local(): lax.all_to_all(spread_rows(send_rows, group, capacity, n_dev, per_dev, mo...]
    reshape x4 -> x3, local copies, waits for them, and re-layouts: 24.6 us -> 1.56 us  [the longest x1 1.34 us: local_fast(): mine.transpose(2, 0, 1).reshape(routes.shape[2], micro_count * half)]
  transfers between devices with their start and end apart: 11 -> 2, of which waited for: 9 -> 1; matrix products, arithmetic and copies ran while one was open for 27% -> 3% of each run, Pallas kernels for 0% -> 4%
where the time goes in v1:
time: 497 us; the launch traced here: 496 us
  Pallas kernels  391 us (79%)
  other arithmetic  36.9 us (7%)
  local copies, waits for them, and re-layouts  24.7 us (5%)
  matrix products  19.5 us (4%)
  between operations  15.5 us (3%)
  waiting for transfers between devices  8.44 us (2%)
    pallas_call x1, Pallas kernels, moe_call(): pl.pallas_call(moe_kernel, out_shape=(jax.ShapeDtypeStruct((micro, length...  194 us
    pallas_call x1, Pallas kernels, reduce_call(): pl.pallas_call(reduce_kernel, out_shape=(jax.ShapeDtypeStruct((wn, wd), b...  176 us
    pallas_call x1, Pallas kernels, grads_call(): pl.pallas_call(grads_kernel, grid=(2 * per,), in_specs=[wide, thin, thin,...  21.1 us
    unnamed x185, local copies, waits for them, and re-layouts  13.3 us
  transfers between devices with their start and end apart: 2, of which 1 were waited for; matrix products, arithmetic and copies ran while one was open for 3% of the time, Pallas kernels for 4%

profile of v1, /device:TPU:16, one launch (start us, length us, event | category | flops | bytes accessed | tf_op | source)
XLA Modules:
  0.0 496.5 jit_solution(10548344120770432183)
XLA Ops:
  7.9 1.3 fusion.41
  9.8 2.1 fusion.40
  11.9 1.0 convolution_bitcast_fusion.7
  12.9 1.0 convolution_bitcast_fusion.8
  14.4 0.9 fusion.17
  15.4 0.9 fusion.18
  16.3 4.3 copy.131
  20.6 2.6 convolution_bitcast_fusion.6
  23.3 0.8 convolution_bitcast_fusion.5
  28.4 0.7 copy-done.27
  29.5 1.3 pad_maximum_fusion
  31.0 0.8 dynamic-slice_bitcast_fusion
  32.4 1.3 reshape.814
  33.7 1.7 copy.164
  35.5 1.7 copy.165
  37.2 1.3 concatenate.113.rt_ref
  38.5 1.3 fusion.59
  41.0 2.0 pad_maximum_fusion.3
  43.0 1.3 slice_convert_fusion.4
  44.3 8.4 %all-reduce.4.cloned.1.call-done = f32[2,128,1536]{2,1,0:T(8,128)} async-done(((f32[2,128,1536]{2,1,0:T(8,128)}), f32[2,128,1536]{2,1,0:T(8,128)}) %all-reduce.4.cloned.1.call-update) | async-done | bytes 1572880 | tf_op jit(solution)/shard_map/psum | solution.py:1104
  52.7 2.1 multiply_reduce_fusion.2
  56.7 1.1 concatenate.112.x_ref
  57.8 194.2 %moe_rows.1 = (bf16[2,128,1536]{2,1,0:T(8,128)(2,1)}, f32[2,128,1664]{2,1,0:T(8,128)}, bf16[2,2,384,1536]{3,2,1,0:T(8,128)(2,1)}, bf16[2,2,384,768]{3,2,1,0:T(8,...) custom-call(bf16[2,128,1664]{2,1,0:T(8,128)(2,1)} %concatenate.112.x, ...), custom_call_target="tpu_custom_call" | custom-call | flops 10871635968 | bytes 41943040 | tf_op jit(solution)/shard_map/moe_rows/pallas_call | solution.py:776
  252.0 1.2 multiply_reduce_fusion.5
  253.2 1.1 multiply_convert_fusion.3
  254.4 2.8 multiply_reduce_fusion
  257.2 1.9 fusion.133
  259.2 0.9 copy-done.17
  260.1 0.9 convolution_convert_fusion.1
  262.3 0.9 convolution_convert_fusion
  263.5 0.8 fusion.14
  266.0 0.7 copy-done.4
  266.8 0.9 fusion.138
  267.8 0.9 fusion.139
  270.7 1.3 pad_maximum_fusion.1
  271.9 0.9 copy-done.28
  272.9 0.8 pad_maximum_fusion.5
  275.0 0.8 pad_maximum_fusion.4
  276.2 21.1 %expert_grads.1 = (f32[1536,1536]{1,0:T(8,128)}, f32[1536,1536]{1,0:T(8,128)}, f32[1536,1536]{1,0:T(8,128)}) custom-call(bf16[2,768,1536]{2,1,0:T(8,128)(2,1)} %bitcast.319, bf16[2,768,768]{2,1,0:T(8,128)(2,1)} %bitcast.321, bf16[2,768,768]{2,1,0:T(8,128)(2,1)} %bitcast.322, bf16[2,768,768]{2,1,0:T(8,128)(2,1)} %bitcast.323, bf16[2,768,1536]{2,1,0:T(8,128)(2,1)} %bitcast.320), custom_call_target="tpu_custom_call" | custom-call | flops 10871635968 | bytes 47185920 | tf_op jit(solution)/shard_map/expert_grads/pallas_call | solution.py:826
  297.3 1.9 fusion.30
  299.1 0.8 maximum_maximum_fusion.s_ref
  299.9 176.0 %reduce_grads.1 = (bf16[1536,1024]{1,0:T(8,128)(2,1)}, bf16[768,1536]{1,0:T(8,128)(2,1)}, bf16[64,1536]{1,0:T(8,128)(2,1)}) custom-call(bf16[256,1536]{1,0:T(8,128)(2,1)} %bitcast.316, bf16[256,1024]{1,0:T(8,128)(2,1)} %bitcast.317, bf16[256,768]{1,0:T(8,128)(2,1)} %bitcast.318, bf16[256,1536]{1,0:T(8,128)(2,1)} %bitcast.303, ...), custom_call_target="tpu_custom_call" | custom-call | flops 1409286144 | bytes 10485760 | tf_op jit(solution)/shard_map/reduce_grads/pallas_call | solution.py:1032
  476.0 4.2 slice_convert_fusion
  480.2 2.5 slice_convert_fusion.1
  482.8 0.7 slice_bitcast_fusion.4
  484.1 2.8 convert_element_type.262
  487.4 1.3 pad_maximum_fusion.2
  488.7 1.0 copy-done.1
  (254 shorter events, 17.9 us)
Async XLA Ops:
  7.2 19.1 %copy-start = (bf16[768,1536]{1,0:T(8,128)(2,1)S(1)}, bf16[768,1536]{1,0:T(8,128)(2,1)}, u32[]{:S(2)}) copy-start(bf16[768,1536]{1,0:T(8,128)(2,1)} %param.23) | copy-start | bytes 7077892
  7.2 4.7 copy-start.6
  7.2 4.7 copy-start.50
  7.2 45.5 %all-reduce.4.cloned.1.call-start = ((), (), s32[]{:S(2)}) async-start(), calls=%async_computation | async-start | bytes 3145728 | tf_op jit(solution)/shard_map/psum | solution.py:1104
  7.3 4.7 copy-start.20
  9.2 5.2 %copy-start.81 = (f32[128]{0:T(128)}, f32[128]{0:T(128)S(1)}, u32[]{:S(2)}) copy-start(f32[128]{0:T(128)S(1)} %fusion.123) | copy-start | bytes 1540
  9.8 5.6 %copy-start.83 = (f32[128]{0:T(128)}, f32[128]{0:T(128)S(1)}, u32[]{:S(2)}) copy-start(f32[128]{0:T(128)S(1)} %fusion.124) | copy-start | bytes 1540
  9.8 4.1 copy-start.85
  9.8 4.6 copy-start.22
  13.9 10.5 %copy-start.74 = (f32[128]{0:T(128)}, f32[128]{0:T(128)S(1)}, u32[]{:S(2)}) copy-start(f32[128]{0:T(128)S(1)} %get-tuple-element.195) | copy-start | bytes 1540
  13.9 10.5 %copy-start.76 = (f32[128]{0:T(128)}, f32[128]{0:T(128)S(1)}, u32[]{:S(2)}) copy-start(f32[128]{0:T(128)S(1)} %get-tuple-element.196) | copy-start | bytes 1540
  16.3 4.3 copy-start.91
  20.6 2.6 copy-start.5
  20.6 2.6 copy-start.16
  24.0 1.9 copy-start.67
  24.5 1.8 copy-start.35
  24.5 1.8 copy-start.37
  24.5 2.5 copy-start.31
  24.5 2.5 copy-start.33
  24.8 1.4 copy-start.61
  24.8 1.4 copy-start.63
  24.9 2.2 copy-start.57
  24.9 2.2 copy-start.59
  30.8 266.4 %all-reduce.6.cloned.1.call-start = ((), (), s32[]{:S(2)}) async-start(), calls=%async_computation.1 | async-start | bytes 3145728 | tf_op jit(solution)/shard_map/psum | solution.py:1161
  52.7 2.7 copy-start.48
  54.8 1.5 copy-start.72
  57.8 196.5 %copy-start.3 = (f32[2,128,1536]{2,1,0:T(8,128)S(1)}, f32[2,128,1536]{2,1,0:T(8,128)}, u32[]{:S(2)}) copy-start(f32[2,128,1536]{2,1,0:T(8,128)} %copy-done.2) | copy-start | bytes 4718596
  254.3 2.9 copy-start.73
  254.4 2.9 copy-start.24
  254.4 2.9 copy-start.25
  254.4 2.9 copy-start.49
  254.4 2.8 copy-start.70
  263.1 1.4 copy-start.12
  263.2 1.4 copy-start.52
  265.1 1.7 copy-start.4
  271.9 3.0 copy-start.71
  273.9 1.9 copy-start.9
  276.1 21.1 %copy-start.7 = (bf16[2,128,1536]{2,1,0:T(8,128)(2,1)S(1)}, bf16[2,128,1536]{2,1,0:T(8,128)(2,1)}, u32[]{:S(2)}) copy-start(bf16[2,128,1536]{2,1,0:T(8,128)(2,1)} %param.14) | copy-start | bytes 2359300
  276.1 21.1 %copy-start.51 = (f32[1536]{0:T(1024)S(1)}, f32[1536]{0:T(1024)}, u32[]{:S(2)}) copy-start(f32[1536]{0:T(1024)} %param.18) | copy-start | bytes 18436
  276.1 21.1 %copy-start.82 = (f32[128]{0:T(128)S(1)}, f32[128]{0:T(128)}, u32[]{:S(2)}) copy-start(f32[128]{0:T(128)} %copy-done.81) | copy-start | bytes 1540
  276.1 21.1 %copy-start.84 = (f32[128]{0:T(128)S(1)}, f32[128]{0:T(128)}, u32[]{:S(2)}) copy-start(f32[128]{0:T(128)} %copy-done.83) | copy-start | bytes 1540
  476.0 6.8 %copy-start.39 = (bf16[64,1536]{1,0:T(8,128)(2,1)S(1)}, bf16[64,1536]{1,0:T(8,128)(2,1)}, u32[]{:S(2)}) copy-start(bf16[64,1536]{1,0:T(8,128)(2,1)} %get-tuple-element.130) | copy-start | bytes 589828
  480.2 3.9 copy-start.19
  484.1 2.8 copy-start.87
  484.1 2.8 copy-start.89
  484.1 2.9 copy-start.10
  484.1 2.9 copy-start.15
  487.4 2.2 copy-start.1
  (46 other events, 46.7 us)
Sparse Core Ops, SparseCore 0:
  30.9 21.7 all-reduce.3
  272.1 19.7 all-reduce.5

commit v2 on v1

--- a/solution.py
+++ b/solution.py
@@ -470,20 +470,24 @@
     return pl.ds(pl.multiple_of(i * width, width), width)
 
 
-def moe_kernel(
-    x_ref, g_ref, rt_ref, wg_hbm, wu_hbm, wd_hbm,
-    mix_ref, dx_ref, rx_ref, rh_ref, rg_ref, ru_ref, re_ref,
-    xz, gz, rz, xs, gs, xr, gr, eg, hid, gpg, upg, ys, ds_, yr, dr, zy, zd, yz, dz,
+def front_kernel(
+    tok_ref, g_ref, pos_ref, routes_ref, rt_ref, gain_a, gain_f, wq_ref, wk_ref, wv_ref, wo_ref, router_ref,
+    wg_hbm, wu_hbm, wd_hbm,
+    lay_ref, dx_ref, nrm_ref, att_ref, q_ref, k_ref, v_ref, pr_ref, tab_ref, hs_ref, x_ref,
+    rx_ref, rh_ref, rg_ref, ru_ref, re_ref,
+    xz, gz, rz, xs, gs, xr, gr, eg, hid, gpg, upg, yr, dr, yz, dz, own_part, other_part,
     onehot, prob, gg, wg, wu, wd,
-    r_s, r_r, za_s, za_r, xa_s, xa_r, xb_s, xb_r, zb_s, zb_r, pair_s, pair_r, w_sem, own_sem,
+    r_s, r_r, za_s, za_r, xa_s, xa_r, xb_s, xb_r, zb_s, zb_r, pair_s, pair_r, part_s, part_r, w_sem, own_sem,
 ):
+    ys, ds_, zy, zd = gs, xs, gz, xz
     e = lax.axis_index("expert")
     c = lax.axis_index("tensor")
     z = e // 4
     o = lax.rem(e, 4) * 2 + c
-    micro = x_ref.shape[0]
-    half = x_ref.shape[1] // 2
-    width = g_ref.shape[2]
+    micro, length, width = tok_ref.shape
+    half = length // 2
+    f32 = jnp.float32
+    bf = jnp.bfloat16
     ff = wg.shape[1]
     col = 4 * half
     rows = xs.shape[1]
@@ -531,23 +535,90 @@
         got_r.append(cp)
     got_z = {}
 
-    def z_send(m):
-        for a, (src, dst) in enumerate(((g_ref, gz), (x_ref, xz))):
-            for k in range(1, 4):
-                i = (m * 2 + a) * 4 + k
-                cp = remote(
-                    src.at[m, mine, :], dst.at[m, pl.ds(k * half, half), :],
-                    za_s.at[i], za_r.at[i], z_dev(k),
-                )
-                cp.start()
-                sent.append(cp)
-                got_z[(m, a, k)] = cp
-
-    z_send(0)
+    def z_send(m, a):
+        src, dst = ((g_ref, gz), (x_ref, xz))[a]
+        for k in range(1, 4):
+            i = (m * 2 + a) * 4 + k
+            cp = remote(
+                src.at[m, mine, :], dst.at[m, pl.ds(k * half, half), :],
+                za_s.at[i], za_r.at[i], z_dev(k),
+            )
+            cp.start()
+            sent.append(cp)
+            got_z[(m, a, k)] = cp
+        dst[m, 0:half, :] = src[m, mine, :]
+
     for m in range(micro):
-        xz[m, 0:half, :] = x_ref[m, mine, :]
-        gz[m, 0:half, :] = g_ref[m, mine, :]
+        z_send(m, 0)
     rz[0] = rt_ref[...]
+
+    head = HEAD_SIZE
+    heads = wq_ref.shape[1] // head
+    lane = lax.broadcasted_iota(jnp.int32, (1, 128), 1)
+    row = lax.broadcasted_iota(jnp.int32, (length, length), 0)
+    column = lax.broadcasted_iota(jnp.int32, (length, length), 1)
+    turn = jnp.exp(
+        (-2.0 / head * jnp.log(jnp.float32(theta_base))) * lax.rem(lane, head // 2).astype(f32)
+    )
+    allowed = []
+    for m in range(micro):
+        states = tok_ref[m].astype(f32)
+        scale = lax.rsqrt(jnp.mean(states * states, axis=1, keepdims=True) + epsilon)
+        nrm_ref[m] = (states * scale * gain_a[...]).astype(bf)
+        place = pos_ref[m : m + 1, :].astype(f32)
+        place = jnp.sum(jnp.where(row == column, place, 0.0), axis=1, keepdims=True)
+        angle = place * turn
+        tab_ref[m, 0] = jnp.cos(angle)
+        tab_ref[m, 1] = jnp.where(lane < head // 2, -1.0, 1.0) * jnp.sin(angle)
+        allowed.append((column <= row) & (column >= row - place.astype(jnp.int32)))
+
+    def rope(u, m):
+        return u * tab_ref[m, 0] + pltpu.roll(u, head // 2, 1) * tab_ref[m, 1]
+
+    everything = nrm_ref[...].reshape(micro * length, width)
+
+    def project(i):
+        both = mm(everything, wq_ref[:, cols(i, tw)])
+        for m in range(micro):
+            for j in range(tw // head):
+                at = pl.ds(pl.multiple_of((i * (tw // head) + j) * length, length), length)
+                u = both[m * length : (m + 1) * length, j * head : (j + 1) * head]
+                q_ref[m, at, :] = rope(u, m).astype(bf)
+
+    tiles(wq_ref.shape[1] // tw, project)
+    key_pre = mm(everything, wk_ref[...])
+    value_pre = mm(everything, wv_ref[...])
+    for m in range(micro):
+        at = slice(m * length, (m + 1) * length)
+        k_ref[m] = rope(key_pre[at], m).astype(bf)
+        v_ref[m] = value_pre[at].astype(bf)
+    for m in range(micro):
+        score = mm_nt(q_ref[m], k_ref[m]).reshape(heads, length, length) * (head**-0.5)
+        score = jnp.where(allowed[m][None], score, masked_score)
+        weight = jnp.exp(score - jnp.max(score, axis=-1, keepdims=True))
+        weight = weight / jnp.sum(weight, axis=-1, keepdims=True)
+        weight = weight.reshape(heads * length, length)
+        pr_ref[m] = weight
+        out = mm(weight.astype(bf), v_ref[m]).astype(bf)
+        for h in range(heads):
+            att_ref[m, :, h * head : (h + 1) * head] = out[h * length : (h + 1) * length]
+    att_all = att_ref[...].reshape(micro * length, heads * head)
+    got_part = []
+    for j in range(3):
+
+        def outward(i, j=j):
+            at = cols(i + j * (nt // 3), tw)
+            own_part[:, at] = mm(att_all, wo_ref[:, at])
+
+        tiles(nt // 3, outward)
+        at = pl.ds(j * (width // 3), width // 3)
+        cp = remote(
+            own_part.at[:, at], other_part.at[:, at], part_s.at[j], part_r.at[j], (e, 1 - c)
+        )
+        cp.start()
+        sent.append(cp)
+        got_part.append(cp)
+
     for cp in got_r:
         cp.wait_recv()
 
@@ -581,39 +652,62 @@
 
     got_p = {}
 
-    def pack(m):
-        for a, (src, out, dst) in enumerate(((gz, gs, gr), (xz, xs, xr))):
-            for k in range(1, 4):
-                got_z[(m, a, k)].wait_recv()
-
-            def body(i, src=src, out=out):
-                at = cols(i, tw)
-                out[m, :, at] = mm(onehot[m], src[m, :, at]).astype(jnp.bfloat16)
-
-            tiles(nt, body)
-            if a == 1:
-                out[m, :, width:] = mm(onehot[m], src[m, :, width:]).astype(jnp.bfloat16)
-            dst[m, 0:blk, :] = out[m, 0:blk, :]
-            for d in range(1, 8):
-                i = (m * 2 + a) * 8 + d
-                at = pl.ds(d * blk, blk)
-                cp = remote(
-                    out.at[m, at, :], dst.at[m, at, :], xa_s.at[i], xa_r.at[i], p_dev(d)
-                )
-                cp.start()
-                sent.append(cp)
-                got_p[(m, a, d)] = cp
-
-    for m in range(1, micro):
-        z_send(m)
+    def pack(m, a):
+        src, out, dst = ((gz, gs, gr), (xz, xs, xr))[a]
+        for k in range(1, 4):
+            got_z[(m, a, k)].wait_recv()
+
+        def body(i):
+            at = cols(i, tw)
+            out[m, :, at] = mm(onehot[m], src[m, :, at]).astype(bf)
+
+        tiles(nt, body)
+        if a == 1:
+            out[m, :, width:] = mm(onehot[m], src[m, :, width:]).astype(bf)
+        dst[m, 0:blk, :] = out[m, 0:blk, :]
+        for d in range(1, 8):
+            i = (m * 2 + a) * 8 + d
+            at = pl.ds(d * blk, blk)
+            cp = remote(out.at[m, at, :], dst.at[m, at, :], xa_s.at[i], xa_r.at[i], p_dev(d))
+            cp.start()
+            sent_p.setdefault((m, a), []).append(cp)
+            got_p[(m, a, d)] = cp
+
+    sent_p = {}
+    wide = lax.broadcasted_iota(jnp.int32, (EXPERTS, 128), 1)
+    double = (lax.rem(wide, EXPERTS) == lax.broadcasted_iota(jnp.int32, (EXPERTS, 128), 0)) & (
+        wide < 2 * EXPERTS
+    )
+    router = mm(router_ref[...], jnp.where(double, 1.0, 0.0).astype(bf)).astype(bf)
+    for cp in got_part:
+        cp.wait_recv()
     for m in range(micro):
-        pack(m)
+        at = slice(m * length, (m + 1) * length)
+        state = tok_ref[m].astype(f32) + (own_part[at, :] + other_part[at, :])
+        hs_ref[m] = state
+        scale = lax.rsqrt(jnp.mean(state * state, axis=1, keepdims=True) + epsilon)
+        low = (state * scale * gain_f[...]).astype(bf)
+        x_ref[m, :, 0:width] = low
+        logits = mm(low, router)
+        names = lax.rem(lane, EXPERTS)
+        hit = routes_ref[m, :, 0:1] == names
+        for j in range(1, routes_ref.shape[2]):
+            hit = hit | (routes_ref[m, :, j : j + 1] == names)
+        hit = hit & (lane < 2 * EXPERTS)
+        best = jnp.max(jnp.where(hit, logits, masked_score), axis=1, keepdims=True)
+        weight = jnp.where(hit, jnp.exp(logits - best), 0.0)
+        first = jnp.sum(jnp.where(lane < EXPERTS, weight, 0.0), axis=1, keepdims=True)
+        weight = weight / first
+        top = weight.astype(bf).astype(f32)
+        x_ref[m, :, width:] = jnp.where(lane < EXPERTS, top, weight - top).astype(bf)
+        z_send(m, 1)
+    for a in range(2):
+        for m in range(micro):
+            pack(m, a)
     for cp in loads:
         cp.wait()
 
     got_b = {}
-    lane = lax.broadcasted_iota(jnp.int32, (1, 128), 1)
-
     def to_pair(m):
         for i, (src, dst) in enumerate(
             ((xr, rx_ref), (hid, rh_ref), (gpg, rg_ref), (upg, ru_ref), (eg, re_ref))
@@ -634,6 +728,8 @@
         for a in range(2):
             for d in range(1, 8):
                 got_p[(m, a, d)].wait_recv()
+            for cp in sent_p[(m, a)]:
+                cp.wait_send()
         tail = xr[m, :, width:].astype(jnp.float32)
         pick = (lane == me) | (lane == me + 32)
         prob[...] = jnp.broadcast_to(
@@ -724,12 +820,14 @@
             got_c[(m, a, k)] = cp
 
     def finish(m, a):
-        own, other, out = ((zd, dz, dx_ref), (zy, yz, mix_ref))[a]
+        own, other, out = ((zd, dz, dx_ref), (zy, yz, lay_ref))[a]
         for k in range(1, 4):
             got_c[(m, a, k)].wait_recv()
         total = own[m, 0:half, :].astype(jnp.float32)
         for k in range(1, 4):
             total = total + other[m, k * half : (k + 1) * half, :].astype(jnp.float32)
+        if a == 1:
+            total = hs_ref[m, mine, :] + total
         out[m, mine, :] = total.astype(out.dtype)
         n = m * 8 + 5 + a
         cp = remote(
@@ -756,47 +854,63 @@
         cp.wait_send()
 
 
-def moe_call(xrows, grows, routes_t, gate_weight, up_weight, down_weight):
-    micro, length, wide = xrows.shape
-    width = grows.shape[2]
+def front_call(
+    tokens, cotangent, positions, routes, routes_t, gain_a, gain_f, wq, wk, wv, wo, router, gate_weight,
+    up_weight, down_weight,
+):
+    micro, length, width = tokens.shape
+    wide = width + 128
     half = length // 2
     ff = gate_weight.shape[1] // 2
-    cap = 3 * half * 4 // (2 * EXPERTS)
+    cap = 3 * half * routes.shape[2] // (2 * EXPERTS)
     rows = 8 * 4 * cap
     bf = jnp.bfloat16
     f32 = jnp.float32
     vmem = pl.BlockSpec(memory_space=pltpu.VMEM)
     hbm = pl.BlockSpec(memory_space=ANY)
+    heads = wq.shape[1] // HEAD_SIZE
 
     def buf(*shape, dtype=bf):
         return pltpu.VMEM(shape, dtype)
+
+    def out(*shape, dtype=bf):
+        return jax.ShapeDtypeStruct(shape, dtype)
 
     sem = pltpu.SemaphoreType.DMA
     col = 4 * half
     return pl.pallas_call(
-        moe_kernel,
+        front_kernel,
         out_shape=(
-            jax.ShapeDtypeStruct((micro, length, width), bf),
-            jax.ShapeDtypeStruct((micro, length, wide), f32),
-            jax.ShapeDtypeStruct((2, micro, rows, width), bf),
-            jax.ShapeDtypeStruct((2, micro, rows, ff), bf),
-            jax.ShapeDtypeStruct((2, micro, rows, ff), bf),
-            jax.ShapeDtypeStruct((2, micro, rows, ff), bf),
-            jax.ShapeDtypeStruct((2, micro, rows, width), bf),
+            out(micro, length, width),
+            out(micro, length, wide, dtype=f32),
+            out(micro, length, width),
+            out(micro, length, wq.shape[1]),
+            out(micro, heads * length, HEAD_SIZE),
+            out(micro, length, HEAD_SIZE),
+            out(micro, length, HEAD_SIZE),
+            out(micro, heads * length, length, dtype=f32),
+            out(micro, 2, length, HEAD_SIZE, dtype=f32),
+            out(micro, length, width, dtype=f32),
+            out(micro, length, wide),
+            out(2, micro, rows, width),
+            out(2, micro, rows, ff),
+            out(2, micro, rows, ff),
+            out(2, micro, rows, ff),
+            out(2, micro, rows, width),
         ),
-        in_specs=[vmem, vmem, vmem, hbm, hbm, hbm],
-        out_specs=(vmem, vmem, hbm, hbm, hbm, hbm, hbm),
+        in_specs=[vmem] * 12 + [hbm] * 3,
+        out_specs=(vmem,) * 11 + (hbm,) * 5,
         scratch_shapes=[
             buf(micro, col, wide), buf(micro, col, width), buf(4, 8, micro * half, dtype=jnp.int32),
             buf(micro, rows, wide), buf(micro, rows, width), buf(micro, rows, wide), buf(micro, rows, width),
             buf(micro, rows, width), buf(micro, rows, ff), buf(micro, rows, ff), buf(micro, rows, ff),
-            buf(micro, rows, width), buf(micro, rows, wide), buf(micro, rows, width), buf(micro, rows, wide),
-            buf(micro, col, width), buf(micro, col, wide), buf(micro, col, width), buf(micro, col, wide),
+            buf(micro, rows, width), buf(micro, rows, wide), buf(micro, col, width), buf(micro, col, wide),
+            buf(micro * length, width, dtype=f32), buf(micro * length, width, dtype=f32),
             buf(micro, rows, col), buf(rows, 128, dtype=f32), buf(rows, 128, dtype=f32),
             buf(width, ff), buf(width, ff), buf(ff, width),
             sem((4,)), sem((4,)), sem((8 * micro,)), sem((8 * micro,)), sem((16 * micro,)), sem((16 * micro,)),
             sem((16 * micro,)), sem((16 * micro,)), sem((8 * micro,)), sem((8 * micro,)), sem((8 * micro,)),
-            sem((8 * micro,)), sem((3,)), sem((8 * micro,)),
+            sem((8 * micro,)), sem((3,)), sem((3,)), sem((3,)), sem((8 * micro,)),
         ],
         compiler_params=pltpu.CompilerParams(
             collective_id=1, has_side_effects=True, vmem_limit_bytes=VMEM_LIMIT
@@ -804,8 +918,11 @@
         cost_estimate=pl.CostEstimate(
             flops=2 * 6 * micro * rows * width * ff, bytes_accessed=40 * 2**20, transcendentals=0
         ),
-        name="moe_rows",
-    )(xrows, grows, routes_t, gate_weight, up_weight, down_weight)
+        name="front",
+    )(
+        tokens, cotangent, positions, routes, routes_t, gain_a, gain_f, wq, wk, wv, wo, router, gate_weight,
+        up_weight, down_weight,
+    )
 
 
 def grads_kernel(x_ref, h_ref, g_ref, u_ref, e_ref, gate_out, up_out, down_out):
@@ -848,22 +965,34 @@
     )
 
 
-def reduce_kernel(
-    n_ref, d_ref, a_ref, g_ref, s_ref, oa, ob, os,
+def back_kernel(
+    tok_ref, g_ref, gain_a, gain_f, wq_ref, wk_ref, wv_ref, wo_ref, router_ref,
+    dx_ref, nrm_ref, att_ref, q_ref, k_ref, v_ref, pr_ref, tab_ref, hs_ref, x_ref,
+    tg_ref, oa, ob, os,
+    d_ref, a_ref, s_ref, sg, ag, own_part, other_part,
     fn, fd, fa, fg, fs, pa, pb, za, zb, zs,
-    f_s, f_r, y_s, y_r, z_s, z_r, p_s, p_r,
+    f_s, f_r, y_s, y_r, z_s, z_r, p_s, p_r, part_s, part_r,
 ):
+    micro, length, width = tok_ref.shape
+    f32 = jnp.float32
+    bf = jnp.bfloat16
+    head = HEAD_SIZE
+    heads = wq_ref.shape[1] // head
+    wq = wq_ref.shape[1]
+    tw = 256
+    nt = width // tw
+    n_ref = nrm_ref
     e = lax.axis_index("expert")
     c = lax.axis_index("tensor")
     z = e // 4
     q = lax.rem(e, 4)
     qx = lax.rem(q, 2)
     qy = q // 2
-    rows = n_ref.shape[0]
+    rows = micro * length
     wn = n_ref.shape[1] // 2
     wd = d_ref.shape[1] // 2
-    wa = a_ref.shape[1] // 2
-    wg = g_ref.shape[1] // 2
+    wa = att_ref.shape[1] // 2
+    wg = a_ref.shape[1] // 2
     ws = s_ref.shape[1] // 4
     hs = s_ref.shape[0] // 4
     ha = wn // 4
@@ -885,38 +1014,130 @@
     for k in range(1, 4):
         pl.semaphore_signal(barrier, inc=1, device_id=z_dev(k), device_id_type=MESH)
         pl.semaphore_signal(barrier, inc=1, device_id=p_dev(k), device_id_type=MESH)
-    pl.semaphore_wait(barrier, 6)
+    pl.semaphore_signal(barrier, inc=1, device_id=(e, 1 - c), device_id_type=MESH)
+    pl.semaphore_wait(barrier, 7)
 
     sent = []
     got = []
-    for d in (3, 1, 2):
-        r = flip(qx, d % 2)
-        s = flip(qy, d // 2)
-        at = pl.ds(d * rows, rows)
-        for i, (src, dst) in enumerate(
-            (
-                (n_ref.at[:, part(r, wn)], fn.at[at, :]),
-                (d_ref.at[:, part(s, wd)], fd.at[at, :]),
-                (a_ref.at[:, part(r, wa)], fa.at[at, :]),
-                (g_ref.at[:, part(s, wg)], fg.at[at, :]),
-                (s_ref.at[part(s * 2 + r, hs), :], fs.at[d]),
-            )
-        ):
-            cp = remote(src, dst, f_s.at[d * 5 + i], f_r.at[d * 5 + i], p_dev(d))
+
+    def factor(i, src, dst):
+        for d in (3, 1, 2):
+            r = flip(qx, d % 2)
+            s = flip(qy, d // 2)
+            at = pl.ds(d * rows, rows)
+            if i == 0 or i == 2:
+                view = src.at[:, part(r, src.shape[1] // 2)]
+            elif i == 1 or i == 3:
+                view = src.at[:, part(s, src.shape[1] // 2)]
+            else:
+                view = src.at[part(s * 2 + r, hs), :]
+            to = fs.at[d] if i == 4 else dst.at[at, :]
+            cp = remote(view, to, f_s.at[d * 5 + i], f_r.at[d * 5 + i], p_dev(d))
             cp.start()
             sent.append(cp)
             got.append(cp)
+
+    factor(0, n_ref, fn)
+    factor(2, att_ref, fa)
+
+    lane = lax.broadcasted_iota(jnp.int32, (1, 128), 1)
+    gain_row = jnp.zeros((1, width), f32)
+    s_ref[...] = jnp.zeros_like(s_ref)
+    router_row = jnp.zeros((128, width), f32)
+    for m in range(micro):
+        here = slice(m * length, (m + 1) * length)
+        tail = dx_ref[m, :, width:]
+        grad = tail + pltpu.roll(tail, 128 - EXPERTS, 1)
+        tail = x_ref[m, :, width:].astype(f32)
+        prob = jnp.where(lane < EXPERTS, tail + pltpu.roll(tail, 128 - EXPERTS, 1), 0.0)
+        shared = jnp.sum(prob * grad, axis=1, keepdims=True)
+        low = (prob * (grad - shared)).astype(bf)
+        router_row = router_row + mm_tn(low, x_ref[m, :, 0:width])
+        full = dx_ref[m, :, 0:width] + mm_nt(low[:, 0:EXPERTS], router_ref[...])
+        state = hs_ref[m]
+        scale = lax.rsqrt(jnp.mean(state * state, axis=1, keepdims=True) + epsilon)
+        u = full * gain_f[...]
+        common = jnp.mean(u * state, axis=1, keepdims=True) * (scale * scale * scale)
+        total = g_ref[m].astype(f32) + (scale * u - state * common)
+        sg[m] = total
+        a_ref[here, :] = total.astype(bf)
+        gain_row = gain_row + jnp.sum(full * state * scale, axis=0, keepdims=True)
+    s_ref[0:EXPERTS, :] = router_row[0:EXPERTS].astype(bf)
+    factor(3, a_ref, fg)
+
+    def inward(i):
+        at = cols(i, tw)
+        both = mm_nt(a_ref[...], wo_ref[at, :]).astype(bf)
+        for m in range(micro):
+            for j in range(tw // head):
+                to = pl.ds(pl.multiple_of((i * (tw // head) + j) * length, length), length)
+                ag[m, to, :] = both[m * length : (m + 1) * length, j * head : (j + 1) * head]
+
+    tiles(wq // tw, inward)
+
+    def unrope(u, m):
+        return u * tab_ref[m, 0] - pltpu.roll(u, head // 2, 1) * tab_ref[m, 1]
+
+    for m in range(micro):
+        here = slice(m * length, (m + 1) * length)
+        prob = pr_ref[m]
+        back = mm_nt(ag[m], v_ref[m])
+        shared = jnp.sum(prob * back, axis=1, keepdims=True)
+        low = (prob * (back - shared)).astype(bf)
+        dq = mm(low, k_ref[m]) * (head**-0.5)
+        for h in range(heads):
+            u = unrope(dq[h * length : (h + 1) * length], m)
+            d_ref[here, h * head : (h + 1) * head] = u.astype(bf)
+        dk = mm_tn(low, q_ref[m]) * (head**-0.5)
+        d_ref[here, wq : wq + head] = unrope(dk, m).astype(bf)
+        d_ref[here, wq + head : wq + 2 * head] = mm_tn(prob.astype(bf), ag[m]).astype(bf)
+    factor(1, d_ref, fd)
+    got_part = []
+    for j in range(3):
+
+        def outward(i, j=j):
+            at = cols(i + j * (nt // 3), tw)
+            own_part[:, at] = (
+                mm_nt(d_ref[:, 0:wq], wq_ref[at, :])
+                + mm_nt(d_ref[:, wq : wq + head], wk_ref[at, :])
+                + mm_nt(d_ref[:, wq + head :], wv_ref[at, :])
+            )
+
+        tiles(nt // 3, outward)
+        at = pl.ds(j * (width // 3), width // 3)
+        cp = remote(
+            own_part.at[:, at], other_part.at[:, at], part_s.at[j], part_r.at[j], (e, 1 - c)
+        )
+        cp.start()
+        sent.append(cp)
+        got_part.append(cp)
     fn[0:rows, :] = n_ref[:, part(qx, wn)]
     fd[0:rows, :] = d_ref[:, part(qy, wd)]
-    fa[0:rows, :] = a_ref[:, part(qx, wa)]
-    fg[0:rows, :] = g_ref[:, part(qy, wg)]
+    fa[0:rows, :] = att_ref[:, part(qx, wa)]
+    fg[0:rows, :] = a_ref[:, part(qy, wg)]
+    for cp in got_part:
+        cp.wait_recv()
+    last_row = jnp.zeros((1, width), f32)
+    for m in range(micro):
+        here = slice(m * length, (m + 1) * length)
+        full = own_part[here, :] + other_part[here, :]
+        state = tok_ref[m].astype(f32)
+        scale = lax.rsqrt(jnp.mean(state * state, axis=1, keepdims=True) + epsilon)
+        u = full * gain_a[...]
+        common = jnp.mean(u * state, axis=1, keepdims=True) * (scale * scale * scale)
+        tg_ref[m] = sg[m] + (scale * u - state * common)
+        last_row = last_row + jnp.sum(full * state * scale, axis=0, keepdims=True)
+    index = lax.broadcasted_iota(jnp.int32, (hs, 1), 0)
+    s_ref[2 * hs : 3 * hs, :] = jnp.where(
+        index == 0, gain_row, jnp.where(index == 1, last_row, 0.0)
+    ).astype(bf)
+    factor(4, s_ref, fs)
     total = s_ref[part(q, hs), :].astype(jnp.float32)
     for cp in got:
         cp.wait_recv()
     for d in range(1, 4):
         total = total + fs[d].astype(jnp.float32)
     fs[0] = total.astype(jnp.bfloat16)
-    tw = 256
 
     def one(i):
         at = cols(i, tw)
@@ -1017,42 +1238,55 @@
         cp.wait_send()
 
 
-def reduce_call(normed, dqkv, attended, agrad, small):
+def back_call(
+    tokens, cotangent, gain_a, gain_f, wq, wk, wv, wo, router, dx, nrm, att, q, k, v, pr, tab, hs, xrows
+):
     bf = jnp.bfloat16
-    rows = normed.shape[0]
-    wn, wd = normed.shape[1], dqkv.shape[1]
-    wa, wg = attended.shape[1], agrad.shape[1]
+    f32 = jnp.float32
+    micro, length, width = tokens.shape
+    rows = micro * length
+    wd = wq.shape[1] + wk.shape[1] + wv.shape[1]
+    wa = wq.shape[1]
+    heads = wa // HEAD_SIZE
     vmem = pl.BlockSpec(memory_space=pltpu.VMEM)
 
-    def buf(*shape):
-        return pltpu.VMEM(shape, bf)
+    def buf(*shape, dtype=bf):
+        return pltpu.VMEM(shape, dtype)
 
     sem = pltpu.SemaphoreType.DMA
-    hs, ws = small.shape[0] // 4, small.shape[1] // 4
+    small = (64, width)
+    hsm, wsm = 16, width // 4
     return pl.pallas_call(
-        reduce_kernel,
+        back_kernel,
         out_shape=(
-            jax.ShapeDtypeStruct((wn, wd), bf),
-            jax.ShapeDtypeStruct((wa, wg), bf),
-            jax.ShapeDtypeStruct(small.shape, bf),
+            jax.ShapeDtypeStruct((micro, length, width), f32),
+            jax.ShapeDtypeStruct((width, wd), bf),
+            jax.ShapeDtypeStruct((wa, width), bf),
+            jax.ShapeDtypeStruct(small, bf),
         ),
-        in_specs=[vmem] * 5,
-        out_specs=(vmem,) * 3,
+        in_specs=[vmem] * 19,
+        out_specs=(vmem,) * 4,
         scratch_shapes=[
-            buf(4 * rows, wn // 2), buf(4 * rows, wd // 2), buf(4 * rows, wa // 2), buf(4 * rows, wg // 2),
-            buf(4, hs, small.shape[1]),
-            buf(wn // 2, wd // 2), buf(wa // 2, wg // 2),
-            buf(4, wn // 8, wd // 2), buf(4, wa // 8, wg // 2), buf(4, hs, ws),
+            buf(rows, wd), buf(rows, width), buf(*small), buf(micro, length, width, dtype=f32),
+            buf(micro, heads * length, HEAD_SIZE), buf(rows, width, dtype=f32), buf(rows, width, dtype=f32),
+            buf(4 * rows, width // 2), buf(4 * rows, wd // 2), buf(4 * rows, wa // 2), buf(4 * rows, width // 2),
+            buf(4, hsm, width),
+            buf(width // 2, wd // 2), buf(wa // 2, width // 2),
+            buf(4, width // 8, wd // 2), buf(4, wa // 8, width // 2), buf(4, hsm, wsm),
             sem((20,)), sem((20,)), sem((12,)), sem((12,)), sem((12,)), sem((12,)), sem((48,)), sem((48,)),
+            sem((3,)), sem((3,)),
         ],
         compiler_params=pltpu.CompilerParams(
             collective_id=2, has_side_effects=True, vmem_limit_bytes=VMEM_LIMIT
         ),
         cost_estimate=pl.CostEstimate(
-            flops=2 * rows * 4 * (wn * wd + wa * wg) // 4, bytes_accessed=10 * 2**20, transcendentals=0
+            flops=2 * rows * 4 * (width * wd + wa * width) // 4, bytes_accessed=20 * 2**20, transcendentals=0
         ),
-        name="reduce_grads",
-    )(normed, dqkv, attended, agrad, small)
+        name="back",
+    )(
+        tokens, cotangent, gain_a, gain_f, wq, wk, wv, wo, router,
+        dx, nrm.reshape(rows, width), att.reshape(rows, wa), q, k, v, pr, tab, hs, xrows,
+    )
 
 
 def suits(mesh):
@@ -1064,132 +1298,34 @@
     value_matrix, output_weight, router_weight, gate_weight, up_weight, down_weight,
 ):
     micro_count, length, model_width = tokens.shape
-    head_dim = HEAD_SIZE
-    kv_local = key_matrix.shape[1] // head_dim
-    query_group_count = query_weight.shape[1] // head_dim // kv_local
     half = length // 2
     c = lax.axis_index("tensor")
     f32 = jnp.float32
-    bf = jnp.bfloat16
-    score_scale = head_dim ** (-0.5)
-    row_ids = jnp.arange(length, dtype=jnp.int32)
-    expert_ids = jnp.arange(EXPERTS, dtype=jnp.int32)
-
-    kept = []
-    for m in range(micro_count):
-        states = tokens[m].astype(f32)
-        place = positions[m]
-        tables = rope_tables(place, head_dim)
-        normed_full, attn_pull = jax.vjp(rms_norm, states, attention_gain)
-        normed = normed_full.astype(bf)
-        query_pre = jnp.dot(normed, query_weight, preferred_element_type=f32).reshape(
-            length, kv_local, query_group_count, head_dim
-        )
-        q = rotary_apply(query_pre, *tables).astype(bf)
-        key_pre = jnp.dot(normed, key_matrix, preferred_element_type=f32).reshape(
-            length, kv_local, head_dim
-        )
-        k = rotary_apply(key_pre, *tables).astype(bf)
-        v = (
-            jnp.dot(normed, value_matrix, preferred_element_type=f32)
-            .astype(bf)
-            .reshape(length, kv_local, head_dim)
-        )
-        att, log_totals = attention_forward(
-            q, k, v, row_ids - place, row_ids, length, score_scale
-        )
-        att = att.reshape(length, -1)
-        part = jnp.dot(att, output_weight, preferred_element_type=f32)
-        kept.append((states, place, tables, normed, attn_pull, q, k, v, att, log_totals, part))
-    parts = lax.psum(jnp.stack([t[-1] for t in kept]), "tensor")
-    hidden = jnp.stack([t[0] for t in kept]) + parts
-    ffn_full, ffn_pull = jax.vjp(rms_norm, hidden, feedforward_gain)
-    normed_ffn = ffn_full.astype(bf)
-    logits = jnp.dot(normed_ffn, router_weight, preferred_element_type=f32)
-    mask = jnp.any(routes[..., None] == expert_ids, axis=2)
-    top = jnp.max(jnp.where(mask, logits, -jnp.inf), axis=-1, keepdims=True)
-    weight = jnp.where(mask, jnp.exp(logits - top), 0.0)
-    probs = weight / jnp.sum(weight, axis=-1, keepdims=True)
-    high = lax.reduce_precision(probs, 8, 7)
-    xrows = jnp.concatenate(
-        [
-            normed_ffn, high.astype(bf), (probs - high).astype(bf),
-            jnp.zeros((micro_count, length, 128 - 2 * EXPERTS), bf),
-        ],
-        axis=-1,
-    )
     mine = lax.dynamic_slice_in_dim(routes, c * half, half, 1)
     routes_t = mine.transpose(2, 0, 1).reshape(routes.shape[2], micro_count * half)
     routes_t = jnp.concatenate([routes_t, jnp.full_like(routes_t, -1)], axis=0)
-    mix, dx, rx, rh, rg, ru, re = moe_call(
-        xrows, cotangent, routes_t, gate_weight, up_weight, down_weight
-    )
-    layer_out = (hidden + mix.astype(f32)).astype(bf)
+    gain_a = attention_gain[None]
+    gain_f = feedforward_gain[None]
+    layer_out, dx, nrm, att, q, k, v, pr, tab, hs, xrows, rx, rh, rg, ru, re = front_call(
+        tokens, cotangent, positions, routes, routes_t, gain_a, gain_f, query_weight, key_matrix,
+        value_matrix, output_weight, router_weight, gate_weight, up_weight, down_weight,
+    )
+    tokens_grad, oa, ob, os = back_call(
+        tokens, cotangent, gain_a, gain_f, query_weight, key_matrix, value_matrix, output_weight,
+        router_weight, dx, nrm, att, q, k, v, pr, tab, hs, xrows,
+    )
     gate_sum, up_sum, down_sum = grads_call(rx, rh, rg, ru, re)
-    gate_grad = dx[..., model_width : model_width + EXPERTS] + dx[
-        ..., model_width + EXPERTS : model_width + 2 * EXPERTS
-    ]
-    logit_grad = probs * (gate_grad - jnp.sum(probs * gate_grad, axis=-1, keepdims=True))
-    logit_grad = logit_grad.astype(bf)
-    normed_ffn_grad = dx[..., :model_width] + jnp.dot(
-        logit_grad, router_weight.T, preferred_element_type=f32
-    )
-    state_norm_grad, ffn_gain_grad = ffn_pull(normed_ffn_grad)
-    state_grad = cotangent.astype(f32) + state_norm_grad
-    agrad = state_grad.astype(bf)
-    router_t = jnp.einsum(
-        "mtx,mtd->xd", logit_grad, normed_ffn, preferred_element_type=f32
-    )
-    back = []
-    for m in range(micro_count):
-        states, place, tables, normed, attn_pull, q, k, v, att, log_totals, part = kept[m]
-        attended_grad = (
-            jnp.dot(agrad[m], output_weight.T, preferred_element_type=f32)
-            .astype(bf)
-            .reshape(length, kv_local, query_group_count, head_dim)
-        )
-        dq, dk, dv = attention_backward(
-            q, k, v, row_ids - place, row_ids, length, score_scale, log_totals, attended_grad
-        )
-        dq = unrotate(dq, *tables).astype(bf).reshape(length, -1)
-        dk = unrotate(dk, *tables).astype(bf).reshape(length, -1)
-        dv = dv.astype(bf).reshape(length, -1)
-        part = jnp.dot(dq, query_weight.T, preferred_element_type=f32)
-        part = part + jnp.dot(dk, key_matrix.T, preferred_element_type=f32)
-        part = part + jnp.dot(dv, value_matrix.T, preferred_element_type=f32)
-        back.append((jnp.concatenate([dq, dk, dv], axis=1), part))
-    normed_grad = lax.psum(jnp.stack([t[1] for t in back]), "tensor")
-    input_grads = []
-    attn_gain_grad = jnp.zeros_like(attention_gain)
-    for m in range(micro_count):
-        grad, gain = kept[m][4](normed_grad[m])
-        input_grads.append(state_grad[m] + grad)
-        attn_gain_grad = attn_gain_grad + gain
-    small = jnp.concatenate(
-        [
-            router_t, ffn_gain_grad[None], attn_gain_grad[None],
-            jnp.zeros((64 - EXPERTS - 2, model_width), f32),
-        ],
-        axis=0,
-    ).astype(bf)
-    rows = micro_count * length
-    oa, ob, os = reduce_call(
-        jnp.stack([t[3] for t in kept]).reshape(rows, -1),
-        jnp.stack([t[0] for t in back]).reshape(rows, -1),
-        jnp.stack([t[8] for t in kept]).reshape(rows, -1),
-        agrad.reshape(rows, -1),
-        small,
-    )
     wq = query_weight.shape[1]
+    wk = wq + key_matrix.shape[1]
     os = os.astype(f32)
     return (
         layer_out,
-        jnp.stack(input_grads),
+        tokens_grad,
         os[EXPERTS + 1],
         os[EXPERTS],
         oa[:, :wq].astype(f32),
-        oa[:, wq : wq + head_dim].astype(f32),
-        oa[:, wq + head_dim :].astype(f32),
+        oa[:, wq:wk].astype(f32),
+        oa[:, wk:].astype(f32),
         ob.astype(f32),
         os[:EXPERTS].T,
         gate_sum,

time: 497 us -> 418 us (0.84)
  other arithmetic: 36.9 us -> 8.55 us
  matrix products: 19.5 us -> 0 us
  between operations: 15.5 us -> 0.69 us
  local copies, waits for them, and re-layouts: 24.7 us -> 10.7 us
  waiting for transfers between devices: 8.44 us -> 0 us
  Pallas kernels: 391 us -> 398 us
    dot_general x31 -> x0, matrix products: 19.5 us -> none  [the longest x2 3.34 us: local_fast(): jnp.dot(normed, query_weight, preferred_element_type=f32)]
    psum x2 -> x0, waiting for transfers between devices: 8.41 us -> none  [the longest x1 8.41 us: local_fast(): parts = lax.psum(jnp.stack([t[-1] for t in kept]), 'tensor')]
    convert_element_type x8 -> x1, other arithmetic: 9.22 us -> 1.24 us  [local_fast(): oa[:, wk:].astype(f32)]
    unnamed x185 -> x12, local copies, waits for them, and re-layouts: 13.3 us -> 5.33 us
    another operation x12 -> x0, other arithmetic: 7.8 us -> none  [the longest x1 1.96 us: local_fast(): jnp.stack([t[3] for t in kept]).reshape(rows, -1)]
    pallas_call x2, Pallas kernels: 370 us -> 378 us  [the longest x1 196 us: front_call(): pl.pallas_call(front_kernel, out_shape=(out(micro, length, width), out(mi...]
    reduce_sum x6 -> x0, other arithmetic: 6.63 us -> none  [the longest x2 3.45 us: rms_norm(): jnp.mean(value_row_states * value_row_states, axis=-1, keepdims=True)]
  transfers between devices with their start and end apart: 2 -> 0, of which waited for: 1 -> 0; matrix products, arithmetic and copies ran while one was open for 3% -> 0% of each run, Pallas kernels for 4% -> 0%
where the time goes in v2:
time: 418 us
  Pallas kernels  398 us (95%)
  local copies, waits for them, and re-layouts  10.7 us (3%)
  other arithmetic  8.55 us (2%)
    pallas_call x1, Pallas kernels, front_call(): pl.pallas_call(front_kernel, out_shape=(out(micro, length, width), out(mi...  196 us
    pallas_call x1, Pallas kernels, back_call(): pl.pallas_call(back_kernel, out_shape=(jax.ShapeDtypeStruct((micro, lengt...  182 us
    pallas_call x1, Pallas kernels, grads_call(): pl.pallas_call(grads_kernel, grid=(2 * per,), in_specs=[wide, thin, thin,...  20.2 us

profile of v2, /device:TPU:16, one launch (start us, length us, event | category | flops | bytes accessed | tf_op | source)
XLA Modules:
  0.0 418.0 jit_solution(12335227311086688617)
XLA Ops:
  0.6 0.8 dynamic-slice_bitcast_fusion
  1.4 0.1 reshape.48
  1.5 0.6 concatenate.3.rt_ref
  2.1 1.8 copy.28.router_ref
  3.9 1.3 broadcast_in_dim.7.gain_a
  5.2 1.3 broadcast_in_dim.8.gain_f
  6.5 1.5 copy.27.routes_ref
  8.0 196.3 %front.1 = (bf16[2,128,1536]{2,1,0:T(8,128)(2,1)}, f32[2,128,1664]{2,1,0:T(8,128)}, bf16[2,128,1536]{2,1,0:T(8,128)(2,1)}, bf16[2,128,768]{2,1,0:T(8,128)(2,1)},...) custom-call(bf16[2,128,1536]{2,1,0:T(8,128)(2,1)} %tok_ref.3, ...), custom_call_target="tpu_custom_call" | custom-call | flops 10871635968 | bytes 41943040 | tf_op jit(solution)/shard_map/front/pallas_call | solution.py:881
  204.3 20.2 %expert_grads.1 = (f32[1536,1536]{1,0:T(8,128)}, f32[1536,1536]{1,0:T(8,128)}, f32[1536,1536]{1,0:T(8,128)}) custom-call(bf16[2,768,1536]{2,1,0:T(8,128)(2,1)} %bitcast.13, bf16[2,768,768]{2,1,0:T(8,128)(2,1)} %bitcast.15, bf16[2,768,768]{2,1,0:T(8,128)(2,1)} %bitcast.16, bf16[2,768,768]{2,1,0:T(8,128)(2,1)} %bitcast.17, bf16[2,768,1536]{2,1,0:T(8,128)(2,1)} %bitcast.14), custom_call_target="tpu_custom_call" | custom-call | flops 10871635968 | bytes 47185920 | tf_op jit(solution)/shard_map/expert_grads/pallas_call | solution.py:943
  224.5 181.6 %back.1 = (f32[2,128,1536]{2,1,0:T(8,128)}, bf16[1536,1024]{1,0:T(8,128)(2,1)}, bf16[768,1536]{1,0:T(8,128)(2,1)}, bf16[64,1536]{1,0:T(8,128)(2,1)}) custom-call(bf16[2,128,1536]{2,1,0:T(8,128)(2,1)} %tok_ref.3, bf16[2,128,1536]{2,1,0:T(8,128)(2,1)} %g_ref.3, f32[1,1536]{1,0:T(1,128)} %broadcast_in_dim.7.gain_a, f32[1,1536]{1,0:T(1,128)} %broadcast_in_dim.8.gain_f, ...), custom_call_target="tpu_custom_call" | custom-call | flops 1409286144 | bytes 20971520 | tf_op jit(solution)/shard_map/back/pallas_call | solution.py:1259
  406.1 0.0 copy-start
  406.1 4.6 %convert_element_type.19 = f32[768,1536]{1,0:T(8,128)} convert(bf16[768,1536]{1,0:T(8,128)(2,1)} %get-tuple-element.49) | non-fusion elementwise | flops 1179648 | bytes 7077888 | tf_op jit(solution)/shard_map/convert_element_type | solution.py:1329
  410.8 0.0 copy-done
  410.8 0.0 copy-start.3
  410.8 2.6 slice_convert_fusion
  413.4 0.0 copy-start.2
  413.4 0.0 copy-start.1
  413.4 1.2 slice_convert_fusion.1
  414.6 0.0 copy-done.3
  414.7 0.7 slice_bitcast_fusion
  415.4 0.6 slice_reduce_fusion
  416.0 0.0 copy-done.2
  416.0 0.9 copy.32
  416.9 0.0 copy-done.1
  416.9 1.1 copy.33
  (2 shorter events, 0.0 us)
Async XLA Ops:
  406.1 4.7 %copy-start = (bf16[1536,1024]{1,0:T(8,128)(2,1)S(1)}, bf16[1536,1024]{1,0:T(8,128)(2,1)}, u32[]{:S(2)}) copy-start(bf16[1536,1024]{1,0:T(8,128)(2,1)} %get-tuple-element.48) | copy-start | bytes 9437188
  410.8 3.9 copy-start.3
  413.4 2.6 copy-start.2
  413.4 3.5 copy-start.1

commit v3 on v2

--- a/solution.py
+++ b/solution.py
@@ -471,13 +471,13 @@
 
 
 def front_kernel(
-    tok_ref, g_ref, pos_ref, routes_ref, rt_ref, gain_a, gain_f, wq_ref, wk_ref, wv_ref, wo_ref, router_ref,
+    tok_ref, g_ref, pos_ref, routes_ref, gain_a, gain_f, wq_ref, wk_ref, wv_ref, wo_ref, router_ref,
     wg_hbm, wu_hbm, wd_hbm,
     lay_ref, dx_ref, nrm_ref, att_ref, q_ref, k_ref, v_ref, pr_ref, tab_ref, hs_ref, x_ref,
     rx_ref, rh_ref, rg_ref, ru_ref, re_ref,
-    xz, gz, rz, xs, gs, xr, gr, eg, hid, gpg, upg, yr, dr, yz, dz, own_part, other_part,
+    xz, gz, rz, xs, gs, xr, gr, eg, hid, gpg, upg, yr, dr, yz, dz, own_part, other_part, rel,
     onehot, prob, gg, wg, wu, wd,
-    r_s, r_r, za_s, za_r, xa_s, xa_r, xb_s, xb_r, zb_s, zb_r, pair_s, pair_r, part_s, part_r, w_sem, own_sem,
+    r_s, r_r, za_s, za_r, xa_s, xa_r, xb_s, xb_r, zb_s, zb_r, pair_s, pair_r, part_s, part_r, fw_s, fw_r, rel_s, rel_r, w_sem, own_sem,
 ):
     ys, ds_, zy, zd = gs, xs, gz, xz
     e = lax.axis_index("expert")
@@ -511,6 +511,27 @@
         t = lax.rem(o + 8 - d, 8)
         return (z * 4 + t // 2, lax.rem(t, 2))
 
+    inner = (z == 1) | (z == 2)
+    edge = (z == 0) | (z == 3)
+    not_first = z != 0
+    not_last = z != 3
+    beside = jnp.where((z == 0) | (z == 3), jnp.where(z == 0, 1, 2), jnp.where(z == 1, 0, 3))
+    beside_dev = (beside * 4 + lax.rem(e, 4), c)
+    far_slot = jnp.where(z == 1, 1, 3)
+    far_back = jnp.where(z == 0, 1, 3)
+
+    @pl.when(z == 3)
+    def _():
+        for m in range(micro):
+            yz[m, half : 2 * half, :] = jnp.zeros((half, width), bf)
+            dz[m, half : 2 * half, :] = jnp.zeros((half, width + 128), bf)
+
+    @pl.when(z == 0)
+    def _():
+        for m in range(micro):
+            yz[m, 3 * half : 4 * half, :] = jnp.zeros((half, width), bf)
+            dz[m, 3 * half : 4 * half, :] = jnp.zeros((half, width + 128), bf)
+
     barrier = pltpu.get_barrier_semaphore()
     for k in range(1, 4):
         pl.semaphore_signal(barrier, inc=1, device_id=z_dev(k), device_id_type=MESH)
@@ -529,28 +550,50 @@
     sent = []
     got_r = []
     for k in range(1, 4):
-        cp = remote(rt_ref, rz.at[k], r_s.at[k], r_r.at[k], z_dev(k))
+        cp = remote(routes_ref, rz.at[k], r_s.at[k], r_r.at[k], z_dev(k))
         cp.start()
         sent.append(cp)
         got_r.append(cp)
     got_z = {}
 
+    sent_if = []
+    got_f = {}
+
+    def start_if(cond, cp):
+        pl.when(cond)(cp.start)
+        sent_if.append((cond, cp))
+
     def z_send(m, a):
         src, dst = ((g_ref, gz), (x_ref, xz))[a]
-        for k in range(1, 4):
+        for k in (2, 1, 3):
             i = (m * 2 + a) * 4 + k
             cp = remote(
                 src.at[m, mine, :], dst.at[m, pl.ds(k * half, half), :],
                 za_s.at[i], za_r.at[i], z_dev(k),
             )
-            cp.start()
-            sent.append(cp)
+            if k == 2:
+                cp.start()
+                sent.append(cp)
+            else:
+                start_if(not_last if k == 1 else not_first, cp)
             got_z[(m, a, k)] = cp
         dst[m, 0:half, :] = src[m, mine, :]
 
+    def z_forward(m, a):
+        dst = (gz, xz)[a]
+        i = (m * 2 + a) * 4
+        got_z[(m, a, 2)].wait_recv()
+        cp = remote(
+            dst.at[m, pl.ds(2 * half, half), :],
+            dst.at[m, pl.ds(pl.multiple_of(far_slot * half, half), half), :],
+            fw_s.at[m * 2 + a], za_r.at[i + far_slot], beside_dev,
+        )
+        pl.when(inner)(cp.start)
+        got_f[(m, a)] = cp
+
     for m in range(micro):
         z_send(m, 0)
-    rz[0] = rt_ref[...]
+    rz[0] = routes_ref[...]
 
     head = HEAD_SIZE
     heads = wq_ref.shape[1] // head
@@ -564,7 +607,7 @@
     for m in range(micro):
         states = tok_ref[m].astype(f32)
         scale = lax.rsqrt(jnp.mean(states * states, axis=1, keepdims=True) + epsilon)
-        nrm_ref[m] = (states * scale * gain_a[...]).astype(bf)
+        nrm_ref[m] = (states * scale * gain_a[...].reshape(1, width)).astype(bf)
         place = pos_ref[m : m + 1, :].astype(f32)
         place = jnp.sum(jnp.where(row == column, place, 0.0), axis=1, keepdims=True)
         angle = place * turn
@@ -586,6 +629,7 @@
                 q_ref[m, at, :] = rope(u, m).astype(bf)
 
     tiles(wq_ref.shape[1] // tw, project)
+    z_forward(0, 0)
     key_pre = mm(everything, wk_ref[...])
     value_pre = mm(everything, wv_ref[...])
     for m in range(micro):
@@ -619,34 +663,31 @@
         sent.append(cp)
         got_part.append(cp)
 
+    z_forward(1, 0)
     for cp in got_r:
         cp.wait_recv()
 
-    lanes = micro * half
-    up = lax.broadcasted_iota(jnp.int32, (lanes, lanes), 0)
-    across = lax.broadcasted_iota(jnp.int32, (lanes, lanes), 1)
-    before = ((up < across) & (up // half == across // half)).astype(jnp.bfloat16)
-    expert = 8 * z + lax.rem(o + lax.broadcasted_iota(jnp.int32, (8, lanes), 0), 8)
-    place_row = lax.broadcasted_iota(jnp.int32, (lanes, col), 0)
-    place_col = lax.broadcasted_iota(jnp.int32, (lanes, col), 1)
-    slots = [jnp.zeros((8, col), jnp.float32) for _ in range(micro)]
+    before = ((row < column) & (row // half == column // half)).astype(bf)
+    expert = 8 * z + lax.rem(o + lax.broadcasted_iota(jnp.int32, (8, length), 0), 8)
+    place_row = lax.broadcasted_iota(jnp.int32, (length, col), 0)
+    place_col = lax.broadcasted_iota(jnp.int32, (length, col), 1)
+    slots = [jnp.zeros((8, col), f32) for _ in range(micro)]
     for k in range(4):
-        named = rz[k]
-        hit = named[0:1, :] == expert
-        for j in range(1, rt_ref.shape[0] // 2):
-            hit = hit | (named[j : j + 1, :] == expert)
-        mask = jnp.where(hit, 1.0, 0.0)
-        rank = mm(mask.astype(jnp.bfloat16), before)
-        slot = (mask * (rank + (cap * k + 1))).astype(jnp.bfloat16)
+        at = place_col - k * half
+        put = ((at >= 0) & (at < half) & (place_row == at + c * half)).astype(bf)
         for m in range(micro):
-            at = place_col - k * half
-            put = (at >= 0) & (at < half) & (place_row == at + m * half)
-            slots[m] = slots[m] + mm(slot, put.astype(jnp.bfloat16))
+            named = rz[k, m]
+            hit = named[0:1, :] == expert
+            for j in range(1, routes_ref.shape[1]):
+                hit = hit | (named[j : j + 1, :] == expert)
+            mask = jnp.where(hit, 1.0, 0.0)
+            rank = mm(mask.astype(bf), before)
+            slots[m] = slots[m] + mm((mask * (rank + (cap * k + 1))).astype(bf), put)
     number = lax.broadcasted_iota(jnp.int32, (blk, col), 0) + 1
     for m in range(micro):
         for d in range(8):
-            row = slots[m][d : d + 1, :].astype(jnp.int32)
-            onehot[m, d * blk : (d + 1) * blk, :] = jnp.where(row == number, 1.0, 0.0).astype(
+            spot = slots[m][d : d + 1, :].astype(jnp.int32)
+            onehot[m, d * blk : (d + 1) * blk, :] = jnp.where(spot == number, 1.0, 0.0).astype(
                 jnp.bfloat16
             )
 
@@ -654,7 +695,7 @@
 
     def pack(m, a):
         src, out, dst = ((gz, gs, gr), (xz, xs, xr))[a]
-        for k in range(1, 4):
+        for k in (1, 3):
             got_z[(m, a, k)].wait_recv()
 
         def body(i):
@@ -674,11 +715,11 @@
             got_p[(m, a, d)] = cp
 
     sent_p = {}
-    wide = lax.broadcasted_iota(jnp.int32, (EXPERTS, 128), 1)
-    double = (lax.rem(wide, EXPERTS) == lax.broadcasted_iota(jnp.int32, (EXPERTS, 128), 0)) & (
-        wide < 2 * EXPERTS
-    )
-    router = mm(router_ref[...], jnp.where(double, 1.0, 0.0).astype(bf)).astype(bf)
+    tall = lax.broadcasted_iota(jnp.int32, (128, EXPERTS), 0)
+    double = (lax.rem(tall, EXPERTS) == lax.broadcasted_iota(jnp.int32, (128, EXPERTS), 1)) & (
+        tall < 2 * EXPERTS
+    )
+    router = mm(jnp.where(double, 1.0, 0.0).astype(bf), router_ref[...]).astype(bf)
     for cp in got_part:
         cp.wait_recv()
     for m in range(micro):
@@ -686,13 +727,15 @@
         state = tok_ref[m].astype(f32) + (own_part[at, :] + other_part[at, :])
         hs_ref[m] = state
         scale = lax.rsqrt(jnp.mean(state * state, axis=1, keepdims=True) + epsilon)
-        low = (state * scale * gain_f[...]).astype(bf)
+        low = (state * scale * gain_f[...].reshape(1, width)).astype(bf)
         x_ref[m, :, 0:width] = low
-        logits = mm(low, router)
+        logits = mm_nt(low, router)
         names = lax.rem(lane, EXPERTS)
-        hit = routes_ref[m, :, 0:1] == names
-        for j in range(1, routes_ref.shape[2]):
-            hit = hit | (routes_ref[m, :, j : j + 1] == names)
+        hit = lane < 0
+        for j in range(routes_ref.shape[1]):
+            named = routes_ref[m, j : j + 1, :].astype(f32)
+            named = jnp.sum(jnp.where(row == column, named, 0.0), axis=1, keepdims=True)
+            hit = hit | (named.astype(jnp.int32) == names)
         hit = hit & (lane < 2 * EXPERTS)
         best = jnp.max(jnp.where(hit, logits, masked_score), axis=1, keepdims=True)
         weight = jnp.where(hit, jnp.exp(logits - best), 0.0)
@@ -701,9 +744,11 @@
         top = weight.astype(bf).astype(f32)
         x_ref[m, :, width:] = jnp.where(lane < EXPERTS, top, weight - top).astype(bf)
         z_send(m, 1)
-    for a in range(2):
-        for m in range(micro):
-            pack(m, a)
+    for m in range(micro):
+        pack(m, 0)
+    for m in range(micro):
+        z_forward(m, 1)
+        pack(m, 1)
     for cp in loads:
         cp.wait()
 
@@ -724,6 +769,17 @@
 
     loads.clear()
 
+    def send_back(m, a):
+        src, dst = ((ds_, dr), (ys, yr))[a]
+        dst[m, 0:blk, :] = src[m, 0:blk, :]
+        for d in range(1, 8):
+            i = (m * 2 + a) * 8 + d
+            at = pl.ds(d * blk, blk)
+            cp = remote(src.at[m, at, :], dst.at[m, at, :], xb_s.at[i], xb_r.at[i], p_back(d))
+            cp.start()
+            sent.append(cp)
+            got_b[(m, a, d)] = cp
+
     def run(m):
         for a in range(2):
             for d in range(1, 8):
@@ -781,21 +837,13 @@
         ds_[m, :, width:] = jnp.where(
             lane == me, high, jnp.where(lane == me + 32, total - high, 0.0)
         ).astype(jnp.bfloat16)
-        for a, (src, dst) in enumerate(((ds_, dr), (ys, yr))):
-            dst[m, 0:blk, :] = src[m, 0:blk, :]
-            for d in range(1, 8):
-                i = (m * 2 + a) * 8 + d
-                at = pl.ds(d * blk, blk)
-                cp = remote(
-                    src.at[m, at, :], dst.at[m, at, :], xb_s.at[i], xb_r.at[i], p_back(d)
-                )
-                cp.start()
-                sent.append(cp)
-                got_b[(m, a, d)] = cp
+        send_back(m, 0)
         to_pair(m)
 
     for m in range(micro):
         run(m)
+    for m in range(micro):
+        send_back(m, 1)
 
     got_c = {}
 
@@ -803,26 +851,45 @@
         src, out, dst = ((dr, zd, dz), (yr, zy, yz))[a]
         for d in range(1, 8):
             got_b[(m, a, d)].wait_recv()
+        pl.when(inner)(got_f[(m, 1 - a)].wait_send)
 
         def body(i):
             at = cols(i, tw)
-            out[m, :, at] = mm_tn(onehot[m], src[m, :, at]).astype(jnp.bfloat16)
+            out[m, :, at] = mm_tn(onehot[m], src[m, :, at]).astype(bf)
 
         tiles(nt, body)
         if a == 0:
-            out[m, :, width:] = mm_tn(onehot[m], src[m, :, width:]).astype(jnp.bfloat16)
-        for k in range(1, 4):
+            out[m, :, width:] = mm_tn(onehot[m], src[m, :, width:]).astype(bf)
+        part = rel.at[m, a] if a == 0 else rel.at[m, a, :, 0:width]
+        far = pl.ds(pl.multiple_of(far_back * half, half), half)
+        relay = remote(out.at[m, far, :], part, rel_s.at[m * 2 + a], rel_r.at[m * 2 + a], beside_dev)
+        start_if(edge, relay)
+        for k in (1, 3, 2):
             i = (m * 2 + a) * 4 + k
             at = pl.ds(k * half, half)
             cp = remote(out.at[m, at, :], dst.at[m, at, :], zb_s.at[i], zb_r.at[i], z_back(k))
-            cp.start()
-            sent.append(cp)
             got_c[(m, a, k)] = cp
+            if k == 2:
+
+                @pl.when(inner)
+                def _():
+                    relay.wait_recv()
+                    wide = out.shape[2]
+                    out[m, 2 * half : 3 * half, :] = (
+                        out[m, 2 * half : 3 * half, :].astype(f32)
+                        + rel[m, a, :, 0:wide].astype(f32)
+                    ).astype(bf)
+
+                cp.start()
+                sent.append(cp)
+            else:
+                start_if(not_first if k == 1 else not_last, cp)
 
     def finish(m, a):
         own, other, out = ((zd, dz, dx_ref), (zy, yz, lay_ref))[a]
-        for k in range(1, 4):
-            got_c[(m, a, k)].wait_recv()
+        pl.when(not_last)(got_c[(m, a, 1)].wait_recv)
+        pl.when(not_first)(got_c[(m, a, 3)].wait_recv)
+        got_c[(m, a, 2)].wait_recv()
         total = own[m, 0:half, :].astype(jnp.float32)
         for k in range(1, 4):
             total = total + other[m, k * half : (k + 1) * half, :].astype(jnp.float32)
@@ -852,17 +919,19 @@
         cp.wait()
     for cp in sent:
         cp.wait_send()
+    for cond, cp in sent_if:
+        pl.when(cond)(cp.wait_send)
 
 
 def front_call(
-    tokens, cotangent, positions, routes, routes_t, gain_a, gain_f, wq, wk, wv, wo, router, gate_weight,
+    tokens, cotangent, positions, routes, gain_a, gain_f, wq, wk, wv, wo, router, gate_weight,
     up_weight, down_weight,
 ):
     micro, length, width = tokens.shape
     wide = width + 128
     half = length // 2
     ff = gate_weight.shape[1] // 2
-    cap = 3 * half * routes.shape[2] // (2 * EXPERTS)
+    cap = 3 * half * routes.shape[1] // (2 * EXPERTS)
     rows = 8 * 4 * cap
     bf = jnp.bfloat16
     f32 = jnp.float32
@@ -898,19 +967,20 @@
             out(2, micro, rows, ff),
             out(2, micro, rows, width),
         ),
-        in_specs=[vmem] * 12 + [hbm] * 3,
+        in_specs=[vmem] * 11 + [hbm] * 3,
         out_specs=(vmem,) * 11 + (hbm,) * 5,
         scratch_shapes=[
-            buf(micro, col, wide), buf(micro, col, width), buf(4, 8, micro * half, dtype=jnp.int32),
+            buf(micro, col, wide), buf(micro, col, width), pltpu.VMEM((4, *routes.shape), jnp.int32),
             buf(micro, rows, wide), buf(micro, rows, width), buf(micro, rows, wide), buf(micro, rows, width),
             buf(micro, rows, width), buf(micro, rows, ff), buf(micro, rows, ff), buf(micro, rows, ff),
             buf(micro, rows, width), buf(micro, rows, wide), buf(micro, col, width), buf(micro, col, wide),
             buf(micro * length, width, dtype=f32), buf(micro * length, width, dtype=f32),
-            buf(micro, rows, col), buf(rows, 128, dtype=f32), buf(rows, 128, dtype=f32),
+            buf(micro, 2, half, wide), buf(micro, rows, col), buf(rows, 128, dtype=f32), buf(rows, 128, dtype=f32),
             buf(width, ff), buf(width, ff), buf(ff, width),
             sem((4,)), sem((4,)), sem((8 * micro,)), sem((8 * micro,)), sem((16 * micro,)), sem((16 * micro,)),
             sem((16 * micro,)), sem((16 * micro,)), sem((8 * micro,)), sem((8 * micro,)), sem((8 * micro,)),
-            sem((8 * micro,)), sem((3,)), sem((3,)), sem((3,)), sem((8 * micro,)),
+            sem((8 * micro,)), sem((3,)), sem((3,)), sem((2 * micro,)), sem((2 * micro,)), sem((2 * micro,)),
+            sem((2 * micro,)), sem((3,)), sem((8 * micro,)),
         ],
         compiler_params=pltpu.CompilerParams(
             collective_id=1, has_side_effects=True, vmem_limit_bytes=VMEM_LIMIT
@@ -920,7 +990,7 @@
         ),
         name="front",
     )(
-        tokens, cotangent, positions, routes, routes_t, gain_a, gain_f, wq, wk, wv, wo, router, gate_weight,
+        tokens, cotangent, positions, routes, gain_a, gain_f, wq, wk, wv, wo, router, gate_weight,
         up_weight, down_weight,
     )
 
@@ -970,8 +1040,8 @@
     dx_ref, nrm_ref, att_ref, q_ref, k_ref, v_ref, pr_ref, tab_ref, hs_ref, x_ref,
     tg_ref, oa, ob, os,
     d_ref, a_ref, s_ref, sg, ag, own_part, other_part,
-    fn, fd, fa, fg, fs, pa, pb, za, zb, zs,
-    f_s, f_r, y_s, y_r, z_s, z_r, p_s, p_r, part_s, part_r,
+    fn, fd, fa, fg, fs, pa, pb, za, zb, zs, ra, rb,
+    f_s, f_r, w_s, w_r, c_s, c_r, y_s, y_r, l_s, l_r, z_s, z_r, h_s, h_r, p_s, p_r, part_s, part_r,
 ):
     micro, length, width = tok_ref.shape
     f32 = jnp.float32
@@ -992,6 +1062,7 @@
     wn = n_ref.shape[1] // 2
     wd = d_ref.shape[1] // 2
     wa = att_ref.shape[1] // 2
+    per = length
     wg = a_ref.shape[1] // 2
     ws = s_ref.shape[1] // 4
     hs = s_ref.shape[0] // 4
@@ -1009,6 +1080,26 @@
 
     def part(i, size):
         return pl.ds(pl.multiple_of(i * size, size), size)
+
+    inner = (z == 1) | (z == 2)
+    edge = (z == 0) | (z == 3)
+    not_first = z != 0
+    not_last = z != 3
+    beside = jnp.where(edge, jnp.where(z == 0, 1, 2), jnp.where(z == 1, 0, 3))
+    beside_dev = (beside * 4 + q, c)
+    twin = (e, 1 - c)
+    sent_if = []
+
+    def start_if(cond, cp):
+        pl.when(cond)(cp.start)
+        sent_if.append((cond, cp))
+
+    def clear(slot):
+        za[slot] = jnp.zeros((ha, wd), bf)
+        zb[slot] = jnp.zeros((hb, wg), bf)
+
+    pl.when(z == 0)(lambda: clear(1))
+    pl.when(z == 3)(lambda: clear(3))
 
     barrier = pltpu.get_barrier_semaphore()
     for k in range(1, 4):
@@ -1018,26 +1109,61 @@
     pl.semaphore_wait(barrier, 7)
 
     sent = []
-    got = []
+    got_f = {}
+    bits = {0: 0, 3: 0, 1: 1, 2: 1}
+
+    def piece(src, i, d):
+        bit = flip(qx, d % 2) if bits[i] == 0 else flip(qy, d // 2)
+        return part(bit, src.shape[1] // 2)
+
+    def mine(d):
+        return pl.ds(pl.multiple_of(d * rows + c * per, per), per)
 
     def factor(i, src, dst):
-        for d in (3, 1, 2):
-            r = flip(qx, d % 2)
-            s = flip(qy, d // 2)
-            at = pl.ds(d * rows, rows)
-            if i == 0 or i == 2:
-                view = src.at[:, part(r, src.shape[1] // 2)]
-            elif i == 1 or i == 3:
-                view = src.at[:, part(s, src.shape[1] // 2)]
+        for d in (1, 2):
+            if bits[i] == 0:
+                view = src.at[pl.ds(pl.multiple_of(c * per, per), per), piece(src, i, d)]
+                to = dst.at[mine(d), :]
             else:
-                view = src.at[part(s * 2 + r, hs), :]
-            to = fs.at[d] if i == 4 else dst.at[at, :]
-            cp = remote(view, to, f_s.at[d * 5 + i], f_r.at[d * 5 + i], p_dev(d))
+                view = src.at[:, piece(src, i, d)]
+                to = dst.at[pl.ds(d * rows, rows), :]
+            cp = remote(view, to, f_s.at[d * 4 + i], f_r.at[d * 4 + i], p_dev(d))
             cp.start()
             sent.append(cp)
-            got.append(cp)
-
-    factor(0, n_ref, fn)
+            got_f[(i, d)] = cp
+
+    def to_twin(i, d, dst):
+        cp = remote(dst.at[mine(d), :], dst.at[mine(d), :], w_s.at[d * 4 + i], w_r.at[d * 4 + i], twin)
+        cp.start()
+        sent.append(cp)
+        got_f[("twin", i, d)] = cp
+
+    def relay(i, dst):
+        via, over = (1, 2) if bits[i] == 0 else (2, 1)
+        got_f[(i, via)].wait_recv()
+        if bits[i] == 0:
+            src, to = dst.at[mine(via), :], dst.at[mine(3), :]
+        else:
+            src, to = dst.at[pl.ds(via * rows, rows), :], dst.at[pl.ds(3 * rows, rows), :]
+        cp = remote(src, to, f_s.at[12 + i], f_r.at[12 + i], p_dev(over))
+        cp.start()
+        sent.append(cp)
+        got_f[(i, 3)] = cp
+        if bits[i] == 0:
+            to_twin(i, via, dst)
+            got_f[(i, over)].wait_recv()
+            to_twin(i, over, dst)
+
+    def arrive(i, dst):
+        if bits[i]:
+            got_f[(i, 1)].wait_recv()
+            got_f[(i, 3)].wait_recv()
+        else:
+            got_f[(i, 3)].wait_recv()
+            to_twin(i, 3, dst)
+            for d in (1, 2, 3):
+                got_f[("twin", i, d)].wait_recv()
+
     factor(2, att_ref, fa)
 
     lane = lax.broadcasted_iota(jnp.int32, (1, 128), 1)
@@ -1053,10 +1179,10 @@
         shared = jnp.sum(prob * grad, axis=1, keepdims=True)
         low = (prob * (grad - shared)).astype(bf)
         router_row = router_row + mm_tn(low, x_ref[m, :, 0:width])
-        full = dx_ref[m, :, 0:width] + mm_nt(low[:, 0:EXPERTS], router_ref[...])
+        full = dx_ref[m, :, 0:width] + mm(low[:, 0:EXPERTS], router_ref[...])
         state = hs_ref[m]
         scale = lax.rsqrt(jnp.mean(state * state, axis=1, keepdims=True) + epsilon)
-        u = full * gain_f[...]
+        u = full * gain_f[...].reshape(1, width)
         common = jnp.mean(u * state, axis=1, keepdims=True) * (scale * scale * scale)
         total = g_ref[m].astype(f32) + (scale * u - state * common)
         sg[m] = total
@@ -1064,6 +1190,8 @@
         gain_row = gain_row + jnp.sum(full * state * scale, axis=0, keepdims=True)
     s_ref[0:EXPERTS, :] = router_row[0:EXPERTS].astype(bf)
     factor(3, a_ref, fg)
+    factor(0, n_ref, fn)
+    relay(2, fa)
 
     def inward(i):
         at = cols(i, tw)
@@ -1074,6 +1202,7 @@
                 ag[m, to, :] = both[m * length : (m + 1) * length, j * head : (j + 1) * head]
 
     tiles(wq // tw, inward)
+    relay(3, fg)
 
     def unrope(u, m):
         return u * tab_ref[m, 0] - pltpu.roll(u, head // 2, 1) * tab_ref[m, 1]
@@ -1092,6 +1221,7 @@
         d_ref[here, wq : wq + head] = unrope(dk, m).astype(bf)
         d_ref[here, wq + head : wq + 2 * head] = mm_tn(prob.astype(bf), ag[m]).astype(bf)
     factor(1, d_ref, fd)
+    relay(0, fn)
     got_part = []
     for j in range(3):
 
@@ -1113,8 +1243,48 @@
         got_part.append(cp)
     fn[0:rows, :] = n_ref[:, part(qx, wn)]
     fd[0:rows, :] = d_ref[:, part(qy, wd)]
-    fa[0:rows, :] = att_ref[:, part(qx, wa)]
-    fg[0:rows, :] = a_ref[:, part(qy, wg)]
+    fa[0:rows, :] = att_ref[:, part(qy, wa)]
+    fg[0:rows, :] = a_ref[:, part(qx, wg)]
+    arrive(2, fa)
+    arrive(3, fg)
+
+    def two(i):
+        at = cols(i, tw)
+        pb[:, at] = mm_tn(fa[...], fg[:, at]).astype(bf)
+
+    tiles(wg // tw, two)
+    got_y = {}
+
+    def spread(i):
+        src, dst, size, rest = ((pa, za, ha, ra), (pb, zb, hb, rb))[i]
+        far = lax.rem(z + jnp.where(z == 0, 3, 1), 4)
+        cp = remote(src.at[part(far, size), :], rest, l_s.at[i], l_r.at[i], beside_dev)
+        start_if(edge, cp)
+        got_y[("far", i)] = cp
+        for k in (1, 3):
+            cp = remote(
+                src.at[part(lax.rem(z + k, 4), size), :], dst.at[k],
+                y_s.at[k * 3 + i], y_r.at[k * 3 + i], z_dev(k),
+            )
+            start_if(not_last if k == 1 else not_first, cp)
+            got_y[(i, k)] = cp
+
+    def spread_rest(i):
+        src, dst, size, rest = ((pa, za, ha, ra), (pb, zb, hb, rb))[i]
+        across = part(lax.rem(z + 2, 4), size)
+
+        @pl.when(inner)
+        def _():
+            got_y[("far", i)].wait_recv()
+            src[across, :] = (src[across, :].astype(f32) + rest[...].astype(f32)).astype(bf)
+
+        cp = remote(src.at[across, :], dst.at[2], y_s.at[6 + i], y_r.at[6 + i], z_dev(2))
+        cp.start()
+        sent.append(cp)
+        got_y[(i, 2)] = cp
+
+    spread(1)
+    relay(1, fd)
     for cp in got_part:
         cp.wait_recv()
     last_row = jnp.zeros((1, width), f32)
@@ -1123,7 +1293,7 @@
         full = own_part[here, :] + other_part[here, :]
         state = tok_ref[m].astype(f32)
         scale = lax.rsqrt(jnp.mean(state * state, axis=1, keepdims=True) + epsilon)
-        u = full * gain_a[...]
+        u = full * gain_a[...].reshape(1, width)
         common = jnp.mean(u * state, axis=1, keepdims=True) * (scale * scale * scale)
         tg_ref[m] = sg[m] + (scale * u - state * common)
         last_row = last_row + jnp.sum(full * state * scale, axis=0, keepdims=True)
@@ -1131,111 +1301,135 @@
     s_ref[2 * hs : 3 * hs, :] = jnp.where(
         index == 0, gain_row, jnp.where(index == 1, last_row, 0.0)
     ).astype(bf)
-    factor(4, s_ref, fs)
+    got_s = []
+    for d in (3, 1, 2):
+        to = flip(qy, d // 2) * 2 + flip(qx, d % 2)
+        cp = remote(s_ref.at[part(to, hs), :], fs.at[d], c_s.at[d], c_r.at[d], p_dev(d))
+        cp.start()
+        sent.append(cp)
+        got_s.append(cp)
+    spread_rest(1)
+    arrive(0, fn)
+    arrive(1, fd)
+
+    def one(i):
+        at = cols(i, tw)
+        pa[:, at] = mm_tn(fn[...], fd[:, at]).astype(bf)
+
+    tiles(wd // tw, one)
+    spread(0)
     total = s_ref[part(q, hs), :].astype(jnp.float32)
-    for cp in got:
+    for cp in got_s:
         cp.wait_recv()
     for d in range(1, 4):
         total = total + fs[d].astype(jnp.float32)
     fs[0] = total.astype(jnp.bfloat16)
-
-    def one(i):
-        at = cols(i, tw)
-        pa[:, at] = mm_tn(fn[...], fd[:, at]).astype(jnp.bfloat16)
-
-    tiles(wd // tw, one)
-
-    def two(i):
-        at = cols(i, tw)
-        pb[:, at] = mm_tn(fa[...], fg[:, at]).astype(jnp.bfloat16)
-
-    tiles(wg // tw, two)
-
-    got = []
     for k in (2, 1, 3):
-        t = lax.rem(z + k, 4)
-        for i, (src, dst) in enumerate(
-            (
-                (pa.at[part(t, ha), :], za.at[k]),
-                (pb.at[part(t, hb), :], zb.at[k]),
-                (fs.at[0, :, part(t, ws)], zs.at[k]),
-            )
-        ):
-            cp = remote(src, dst, y_s.at[k * 3 + i], y_r.at[k * 3 + i], z_dev(k))
-            cp.start()
-            sent.append(cp)
-            got.append(cp)
-    for cp in got:
-        cp.wait_recv()
+        cp = remote(
+            fs.at[0, :, part(lax.rem(z + k, 4), ws)], zs.at[k],
+            y_s.at[k * 3 + 2], y_r.at[k * 3 + 2], z_dev(k),
+        )
+        cp.start()
+        sent.append(cp)
+        got_y[(2, k)] = cp
+    spread_rest(0)
 
     def spots(px, py, t):
         return (
             oa.at[part(px * 4 + t, ha), part(py, wd)],
-            ob.at[part(px * 4 + t, hb), part(py, wg)],
+            ob.at[part(py * 4 + t, hb), part(px, wg)],
             os.at[part(py * 2 + px, hs), part(t, ws)],
         )
 
-    def store(ref, first, others):
-        acc = first.astype(jnp.float32)
+    home = spots(qx, qy, z)
+
+    def total_of(i):
+        first, others = (
+            (pa[part(z, ha), :], za), (pb[part(z, hb), :], zb), (fs[0, :, part(z, ws)], zs),
+        )[i]
+        if i < 2:
+            pl.when(not_first)(got_y[(i, 1)].wait_recv)
+            pl.when(not_last)(got_y[(i, 3)].wait_recv)
+        else:
+            got_y[(i, 1)].wait_recv()
+            got_y[(i, 3)].wait_recv()
+        got_y[(i, 2)].wait_recv()
+        acc = first.astype(f32)
         for k in range(1, 4):
-            acc = acc + others[k].astype(jnp.float32)
-        ref[...] = acc.astype(jnp.bfloat16)
-
-    mine = spots(qx, qy, z)
-    store(mine[0], pa[part(z, ha), :], za)
-    store(mine[1], pb[part(z, hb), :], zb)
-    store(mine[2], fs[0, :, part(z, ws)], zs)
-
-    got_z = {}
+            acc = acc + others[k].astype(f32)
+        home[i][...] = acc.astype(bf)
+        for k in (2, 1, 3):
+            cp = remote(home[i], home[i], z_s.at[k * 3 + i], z_r.at[k * 3 + i], z_dev(k))
+            if k == 2:
+                cp.start()
+                sent.append(cp)
+            else:
+                start_if(not_last if k == 1 else not_first, cp)
+
+    turns = (
+        0,
+        jnp.where(inner, 2, jnp.where(z == 0, 3, 1)),
+        jnp.where(inner, 1, 2),
+        jnp.where(inner, 3, jnp.where(z == 0, 1, 3)),
+    )
     got_p = {}
 
-    def send(ref, i, k, d, j):
-        n = ((k * 3) + i) * 4 + j
-        cp = remote(ref, ref, p_s.at[n], p_r.at[n], p_dev(d))
+    def send(ref, i, n, d, j):
+        at = ((n * 3) + i) * 4 + j
+        cp = remote(ref, ref, p_s.at[at], p_r.at[at], p_dev(d))
         cp.start()
         sent.append(cp)
-        got_p[(k, i, j)] = cp
-
-    for k in (2, 1, 3):
+        got_p[(n, i, j)] = cp
+
+    def own(n, i):
+        k = turns[n]
+        here = spots(qx, qy, lax.rem(z + 4 - k, 4))[i]
+        if n:
+            cp = remote(here, here, z_s.at[k * 3 + i], z_r.at[k * 3 + i], beside_dev)
+            cp.wait_recv()
+        if n == 1:
+            to = jnp.where(z == 1, 1, 3)
+            cp = remote(here, here, h_s.at[i], z_r.at[to * 3 + i], beside_dev)
+            start_if(inner, cp)
+        send(here, i, n, 1, 1)
+        send(here, i, n, 2, 2)
+
+    def forward(n, i):
+        t = lax.rem(z + 4 - turns[n], 4)
+        if i == 1:
+            got_p[(n, i, 2)].wait_recv()
+            send(spots(qx, flip(qy, 1), t)[i], i, n, 1, 3)
+        else:
+            got_p[(n, i, 1)].wait_recv()
+            send(spots(flip(qx, 1), qy, t)[i], i, n, 2, 3)
+
+    total_of(1)
+    own(0, 1)
+    total_of(0)
+    own(0, 0)
+    total_of(2)
+    own(0, 2)
+    own(1, 1)
+    forward(0, 1)
+    own(1, 0)
+    forward(0, 0)
+    forward(0, 2)
+    own(1, 2)
+    for n in (2, 3):
+        for i in (1, 0, 2):
+            own(n, i)
+            forward(n - 1, i)
+    for i in (1, 0, 2):
+        forward(3, i)
+    for n in range(4):
         for i in range(3):
-            cp = remote(mine[i], mine[i], z_s.at[k * 3 + i], z_r.at[k * 3 + i], z_dev(k))
-            cp.start()
-            sent.append(cp)
-            got_z[(k, i)] = cp
-
-    def own(k):
-        here = spots(qx, qy, lax.rem(z + 4 - k, 4))
-        if k:
-            for i in range(3):
-                got_z[(k, i)].wait_recv()
-        for i in range(3):
-            send(here[i], i, k, 1, 1)
-            send(here[i], i, k, 2, 2)
-
-    def forward(k):
-        t = lax.rem(z + 4 - k, 4)
-        beside = spots(flip(qx, 1), qy, t)
-        above = spots(qx, flip(qy, 1), t)
-        got_p[(k, 0, 1)].wait_recv()
-        send(beside[0], 0, k, 2, 3)
-        got_p[(k, 2, 1)].wait_recv()
-        send(beside[2], 2, k, 2, 3)
-        got_p[(k, 1, 2)].wait_recv()
-        send(above[1], 1, k, 1, 3)
-
-    turns = (0, 1, 3, 2)
-    for n, k in enumerate(turns):
-        own(k)
-        if n:
-            forward(turns[n - 1])
-    forward(turns[-1])
-    for k in range(4):
-        for i in range(3):
-            first = 2 if i in (0, 2) else 1
-            got_p[(k, i, first)].wait_recv()
-            got_p[(k, i, 3)].wait_recv()
+            first = 1 if i == 1 else 2
+            got_p[(n, i, first)].wait_recv()
+            got_p[(n, i, 3)].wait_recv()
     for cp in sent:
         cp.wait_send()
+    for cond, cp in sent_if:
+        pl.when(cond)(cp.wait_send)
 
 
 def back_call(
@@ -1273,7 +1467,9 @@
             buf(4, hsm, width),
             buf(width // 2, wd // 2), buf(wa // 2, width // 2),
             buf(4, width // 8, wd // 2), buf(4, wa // 8, width // 2), buf(4, hsm, wsm),
-            sem((20,)), sem((20,)), sem((12,)), sem((12,)), sem((12,)), sem((12,)), sem((48,)), sem((48,)),
+            buf(width // 8, wd // 2), buf(wa // 8, width // 2),
+            sem((16,)), sem((16,)), sem((16,)), sem((16,)), sem((4,)), sem((4,)), sem((12,)), sem((12,)),
+            sem((2,)), sem((2,)), sem((12,)), sem((12,)), sem((3,)), sem((3,)), sem((48,)), sem((48,)),
             sem((3,)), sem((3,)),
         ],
         compiler_params=pltpu.CompilerParams(
@@ -1298,21 +1494,16 @@
     value_matrix, output_weight, router_weight, gate_weight, up_weight, down_weight,
 ):
     micro_count, length, model_width = tokens.shape
-    half = length // 2
-    c = lax.axis_index("tensor")
     f32 = jnp.float32
-    mine = lax.dynamic_slice_in_dim(routes, c * half, half, 1)
-    routes_t = mine.transpose(2, 0, 1).reshape(routes.shape[2], micro_count * half)
-    routes_t = jnp.concatenate([routes_t, jnp.full_like(routes_t, -1)], axis=0)
-    gain_a = attention_gain[None]
-    gain_f = feedforward_gain[None]
+    gain_a, gain_f = attention_gain, feedforward_gain
+    router_t = router_weight.T
     layer_out, dx, nrm, att, q, k, v, pr, tab, hs, xrows, rx, rh, rg, ru, re = front_call(
-        tokens, cotangent, positions, routes, routes_t, gain_a, gain_f, query_weight, key_matrix,
-        value_matrix, output_weight, router_weight, gate_weight, up_weight, down_weight,
+        tokens, cotangent, positions, routes.transpose(0, 2, 1), gain_a, gain_f, query_weight, key_matrix,
+        value_matrix, output_weight, router_t, gate_weight, up_weight, down_weight,
     )
     tokens_grad, oa, ob, os = back_call(
         tokens, cotangent, gain_a, gain_f, query_weight, key_matrix, value_matrix, output_weight,
-        router_weight, dx, nrm, att, q, k, v, pr, tab, hs, xrows,
+        router_t, dx, nrm, att, q, k, v, pr, tab, hs, xrows,
     )
     gate_sum, up_sum, down_sum = grads_call(rx, rh, rg, ru, re)
     wq = query_weight.shape[1]

time: 418 us -> 306 us (0.73)
  Pallas kernels: 398 us -> 293 us
  local copies, waits for them, and re-layouts: 10.7 us -> 3.36 us
    pallas_call x1, Pallas kernels: 182 us -> 111 us  [back_call(): pl.pallas_call(back_kernel, out_shape=(jax.ShapeDtypeStruct((micro, lengt...]
    pallas_call x1, Pallas kernels: 196 us -> 162 us  [front_call(): pl.pallas_call(front_kernel, out_shape=(out(micro, length, width), out(mi...]
where the time goes in v3:
time: 306 us; the launch traced here: 305 us
  Pallas kernels  293 us (96%)
  other arithmetic  8.55 us (3%)
  local copies, waits for them, and re-layouts  3.36 us (1%)
    pallas_call x1, Pallas kernels, front_call(): pl.pallas_call(front_kernel, out_shape=(out(micro, length, width), out(mi...  162 us
    pallas_call x1, Pallas kernels, back_call(): pl.pallas_call(back_kernel, out_shape=(jax.ShapeDtypeStruct((micro, lengt...  111 us
    pallas_call x1, Pallas kernels, grads_call(): pl.pallas_call(grads_kernel, grid=(2 * per,), in_specs=[wide, thin, thin,...  20.2 us

profile of v3, /device:TPU:16, one launch (start us, length us, event | category | flops | bytes accessed | tf_op | source)
XLA Modules:
  0.0 305.2 jit_solution(14998075303375023189)
XLA Ops:
  0.6 161.8 %front.1 = (bf16[2,128,1536]{2,1,0:T(8,128)(2,1)}, f32[2,128,1664]{2,1,0:T(8,128)}, bf16[2,128,1536]{2,1,0:T(8,128)(2,1)}, bf16[2,128,768]{2,1,0:T(8,128)(2,1)},...) custom-call(bf16[2,128,1536]{2,1,0:T(8,128)(2,1)} %tok_ref.3, ...), custom_call_target="tpu_custom_call" | custom-call | flops 10871635968 | bytes 41943040 | tf_op jit(solution)/shard_map/front/pallas_call | solution.py:950
  162.4 20.2 %expert_grads.1 = (f32[1536,1536]{1,0:T(8,128)}, f32[1536,1536]{1,0:T(8,128)}, f32[1536,1536]{1,0:T(8,128)}) custom-call(bf16[2,768,1536]{2,1,0:T(8,128)(2,1)} %bitcast.16, bf16[2,768,768]{2,1,0:T(8,128)(2,1)} %bitcast.18, bf16[2,768,768]{2,1,0:T(8,128)(2,1)} %bitcast.19, bf16[2,768,768]{2,1,0:T(8,128)(2,1)} %bitcast.20, bf16[2,768,1536]{2,1,0:T(8,128)(2,1)} %bitcast.17), custom_call_target="tpu_custom_call" | custom-call | flops 10871635968 | bytes 47185920 | tf_op jit(solution)/shard_map/expert_grads/pallas_call | solution.py:1013
  182.7 110.6 %back.1 = (f32[2,128,1536]{2,1,0:T(8,128)}, bf16[1536,1024]{1,0:T(8,128)(2,1)}, bf16[768,1536]{1,0:T(8,128)(2,1)}, bf16[64,1536]{1,0:T(8,128)(2,1)}) custom-call(bf16[2,128,1536]{2,1,0:T(8,128)(2,1)} %tok_ref.3, bf16[2,128,1536]{2,1,0:T(8,128)(2,1)} %g_ref.3, f32[1536]{0:T(1024)} %gain_a.3, f32[1536]{0:T(1024)} %gain_f.3, bf16[1536,768]{1,0:T(8,128)(2,1)} %wq_ref.3, ...), custom_call_target="tpu_custom_call" | custom-call | flops 1409286144 | bytes 20971520 | tf_op jit(solution)/shard_map/back/pallas_call | solution.py:1453
  293.3 0.0 copy-start
  293.3 4.6 %convert_element_type.19 = f32[768,1536]{1,0:T(8,128)} convert(bf16[768,1536]{1,0:T(8,128)(2,1)} %get-tuple-element.49) | non-fusion elementwise | flops 1179648 | bytes 7077888 | tf_op jit(solution)/shard_map/convert_element_type | solution.py:1520
  297.9 0.0 copy-done
  298.0 0.0 copy-start.3
  298.0 2.6 slice_convert_fusion
  300.6 0.0 copy-start.2
  300.6 0.0 copy-start.1
  300.6 1.2 slice_convert_fusion.1
  301.8 0.0 copy-done.3
  301.9 0.7 slice_bitcast_fusion
  302.6 0.6 slice_reduce_fusion
  303.2 0.0 copy-done.2
  303.2 0.9 copy.28
  304.1 0.0 copy-done.1
  304.1 1.1 copy.29
  (1 shorter events, 0.0 us)
Async XLA Ops:
  293.3 4.7 %copy-start = (bf16[1536,1024]{1,0:T(8,128)(2,1)S(1)}, bf16[1536,1024]{1,0:T(8,128)(2,1)}, u32[]{:S(2)}) copy-start(bf16[1536,1024]{1,0:T(8,128)(2,1)} %get-tuple-element.48) | copy-start | bytes 9437188
  298.0 3.9 %copy-start.3 = (bf16[64,1536]{1,0:T(8,128)(2,1)S(1)}, bf16[64,1536]{1,0:T(8,128)(2,1)}, u32[]{:S(2)}) copy-start(bf16[64,1536]{1,0:T(8,128)(2,1)} %get-tuple-element.47) | copy-start | bytes 589828
  300.6 2.6 copy-start.2
  300.6 3.5 %copy-start.1 = (f32[2,128,1536]{2,1,0:T(8,128)S(1)}, f32[2,128,1536]{2,1,0:T(8,128)}, u32[]{:S(2)}) copy-start(f32[2,128,1536]{2,1,0:T(8,128)} %get-tuple-element.75) | copy-start | bytes 4718596

commit v4 on v3

--- a/solution.py
+++ b/solution.py
@@ -471,15 +471,17 @@
 
 
 def front_kernel(
-    tok_ref, g_ref, pos_ref, routes_ref, gain_a, gain_f, wq_ref, wk_ref, wv_ref, wo_ref, router_ref,
-    wg_hbm, wu_hbm, wd_hbm,
-    lay_ref, dx_ref, nrm_ref, att_ref, q_ref, k_ref, v_ref, pr_ref, tab_ref, hs_ref, x_ref,
-    rx_ref, rh_ref, rg_ref, ru_ref, re_ref,
-    xz, gz, rz, xs, gs, xr, gr, eg, hid, gpg, upg, yr, dr, yz, dz, own_part, other_part, rel,
+    tok_hbm, g_hbm, wq_hbm, wk_hbm, wv_hbm, wo_hbm, wg_hbm, wu_hbm, wd_hbm,
+    pos_ref, routes_ref, gain_a, gain_f, router_ref,
+    dx_ref, nrm_hbm, att_hbm, q_hbm, k_hbm, v_hbm, pr_hbm, tab_hbm, hs_hbm, x_hbm, y0_hbm, y1_hbm, hot_hbm,
+    fn, fa, rx_ref, rh_ref, rg_ref, ru_ref, re_ref,
+    tok_ref, wq_ref, wk_ref, wv_ref, wo_ref, nrm_ref, att_ref, q_ref, k_ref, v_ref, pr_ref, tab_ref, hs_ref, x_ref,
+    xz, gz, rz, xs, gs, xr, gr, eg, hid, gpg, upg, y0r, dr, dz, own_part, other_part, rel,
     onehot, prob, gg, wg, wu, wd,
-    r_s, r_r, za_s, za_r, xa_s, xa_r, xb_s, xb_r, zb_s, zb_r, pair_s, pair_r, part_s, part_r, fw_s, fw_r, rel_s, rel_r, w_sem, own_sem,
+    r_s, r_r, za_s, za_r, xa_s, xa_r, xb_s, xb_r, zb_s, zb_r, pair_s, pair_r, part_s, part_r, fw_s, rel_s, rel_r,
+    f_s, f_r, w_s, w_r, in_sem, out_sem, own_sem,
 ):
-    ys, ds_, zy, zd = gs, xs, gz, xz
+    ys, ds_, zd = gs, xs, xz
     e = lax.axis_index("expert")
     c = lax.axis_index("tensor")
     z = e // 4
@@ -523,13 +525,11 @@
     @pl.when(z == 3)
     def _():
         for m in range(micro):
-            yz[m, half : 2 * half, :] = jnp.zeros((half, width), bf)
             dz[m, half : 2 * half, :] = jnp.zeros((half, width + 128), bf)
 
     @pl.when(z == 0)
     def _():
         for m in range(micro):
-            yz[m, 3 * half : 4 * half, :] = jnp.zeros((half, width), bf)
             dz[m, 3 * half : 4 * half, :] = jnp.zeros((half, width + 128), bf)
 
     barrier = pltpu.get_barrier_semaphore()
@@ -537,13 +537,23 @@
         pl.semaphore_signal(barrier, inc=1, device_id=z_dev(k), device_id_type=MESH)
     for d in range(1, 8):
         pl.semaphore_signal(barrier, inc=1, device_id=p_dev(d), device_id_type=MESH)
-    loads = [
-        pltpu.make_async_copy(wg_hbm.at[:, cols(c, ff)], wg, w_sem.at[0]),
-        pltpu.make_async_copy(wu_hbm.at[:, cols(c, ff)], wu, w_sem.at[1]),
-        pltpu.make_async_copy(wd_hbm.at[cols(c, ff), :], wd, w_sem.at[2]),
-    ]
-    for cp in loads:
+    loads = {}
+    for i, (name, src, dst) in enumerate(
+        (
+            ("tok", tok_hbm, tok_ref), ("wq", wq_hbm, wq_ref), ("wk", wk_hbm, wk_ref), ("wv", wv_hbm, wv_ref),
+            ("wo", wo_hbm, wo_ref), ("wg", wg_hbm.at[:, cols(c, ff)], wg), ("wu", wu_hbm.at[:, cols(c, ff)], wu),
+            ("wd", wd_hbm.at[cols(c, ff), :], wd),
+        )
+    ):
+        loads[name] = pltpu.make_async_copy(src, dst, in_sem.at[i])
+        loads[name].start()
+    saves = []
+
+    def save(src, dst):
+        cp = pltpu.make_async_copy(src, dst, out_sem.at[len(saves)])
         cp.start()
+        saves.append(cp)
+
     pl.semaphore_wait(barrier, 10)
 
     mine = pl.ds(pl.multiple_of(c * half, half), half)
@@ -557,43 +567,121 @@
     got_z = {}
 
     sent_if = []
+    away = {}
     got_f = {}
 
     def start_if(cond, cp):
         pl.when(cond)(cp.start)
         sent_if.append((cond, cp))
 
+    cut = width // 2
+    parts = (((0, width),), ((0, cut), (cut, width + 128 - cut)))
+
+    def sem_of(m, a, j, k, per):
+        return ((m * 2 + a) * 2 + j) * per + k
+
     def z_send(m, a):
-        src, dst = ((g_ref, gz), (x_ref, xz))[a]
-        for k in (2, 1, 3):
-            i = (m * 2 + a) * 4 + k
+        src, dst = ((g_hbm, gz), (x_ref, xz))[a]
+        for j, (left, size) in enumerate(parts[a]):
+            wide = pl.ds(left, size)
+            for k in (2, 1, 3):
+                i = sem_of(m, a, j, k, 4)
+                cp = remote(
+                    src.at[m, mine, wide], dst.at[m, pl.ds(k * half, half), wide],
+                    za_s.at[i], za_r.at[i], z_dev(k),
+                )
+                cond = {1: not_last, 2: True, 3: not_first}[k]
+                if k == 2:
+                    cp.start()
+                else:
+                    pl.when(cond)(cp.start)
+                got_z[(m, a, j, k)] = cp
+                away.setdefault((m, a), []).append((cond, cp))
+        if a == 1:
+            dst[m, 0:half, :] = src[m, mine, :]
+        else:
+            cp = pltpu.make_async_copy(src.at[m, mine, :], dst.at[m, 0:half, :], in_sem.at[8 + m])
+            cp.start()
+            loads[("g", m)] = cp
+
+    def z_sent(m, a):
+        for cond, cp in away.pop((m, a)):
+            if cond is True:
+                cp.wait_send()
+            else:
+                pl.when(cond)(cp.wait_send)
+
+    def z_forward(m, a):
+        dst = (gz, xz)[a]
+        for j, (left, size) in enumerate(parts[a]):
+            wide = pl.ds(left, size)
+            got_z[(m, a, j, 2)].wait_recv()
             cp = remote(
-                src.at[m, mine, :], dst.at[m, pl.ds(k * half, half), :],
-                za_s.at[i], za_r.at[i], z_dev(k),
+                dst.at[m, pl.ds(2 * half, half), wide],
+                dst.at[m, pl.ds(pl.multiple_of(far_slot * half, half), half), wide],
+                fw_s.at[sem_of(m, a, j, 0, 1)], za_r.at[sem_of(m, a, j, 0, 4) + far_slot], beside_dev,
             )
-            if k == 2:
+            pl.when(inner)(cp.start)
+            got_f[(m, a, j)] = cp
+
+    z_send(0, 0)
+    rz[0] = routes_ref[...]
+
+    qx = lax.rem(e, 2)
+    qy = lax.rem(e, 4) // 2
+    every = micro * length
+    twin = (e, 1 - c)
+    got_a = {}
+
+    def f_dev(d):
+        return (z * 4 + lax.rem(qy + d // 2, 2) * 2 + lax.rem(qx + d % 2, 2), c)
+
+    def block(d):
+        return pl.ds(pl.multiple_of(d * every + c * length, length), length)
+
+    def factor(i, dst):
+        for d in (1, 2):
+            if i == 0:
+                size = width // 2
+                view = nrm_ref.at[c, :, cols(lax.rem(qx + d % 2, 2), size)]
+                to = dst.at[block(d), :]
+                copies = [(view, to)]
+            else:
+                size = att_ref.shape[2] // 2
+                at = cols(lax.rem(qy + d // 2, 2), size)
+                copies = [
+                    (att_ref.at[m, :, at], dst.at[pl.ds(d * every + m * length, length), :])
+                    for m in range(micro)
+                ]
+            for m, (view, to) in enumerate(copies):
+                n = (d * 2 + i // 2) * 2 + m
+                cp = remote(view, to, f_s.at[n], f_r.at[n], f_dev(d))
                 cp.start()
                 sent.append(cp)
-            else:
-                start_if(not_last if k == 1 else not_first, cp)
-            got_z[(m, a, k)] = cp
-        dst[m, 0:half, :] = src[m, mine, :]
-
-    def z_forward(m, a):
-        dst = (gz, xz)[a]
-        i = (m * 2 + a) * 4
-        got_z[(m, a, 2)].wait_recv()
+                got_a[(i, d, m)] = cp
+
+    def to_twin(d):
+        got_a[(0, d, 0)].wait_recv()
+        cp = remote(fn.at[block(d), :], fn.at[block(d), :], w_s.at[d], w_r.at[d], twin)
+        cp.start()
+        sent.append(cp)
+        got_a[("twin", d)] = cp
+
+    def pass_on():
+        to_twin(1)
+        to_twin(2)
+        cp = remote(fn.at[block(1), :], fn.at[block(3), :], f_s.at[12], f_r.at[12], f_dev(2))
+        cp.start()
+        sent.append(cp)
+        got_a[(0, 3, 0)] = cp
+        for m in range(micro):
+            got_a[(2, 2, m)].wait_recv()
         cp = remote(
-            dst.at[m, pl.ds(2 * half, half), :],
-            dst.at[m, pl.ds(pl.multiple_of(far_slot * half, half), half), :],
-            fw_s.at[m * 2 + a], za_r.at[i + far_slot], beside_dev,
-        )
-        pl.when(inner)(cp.start)
-        got_f[(m, a)] = cp
-
-    for m in range(micro):
-        z_send(m, 0)
-    rz[0] = routes_ref[...]
+            fa.at[pl.ds(2 * every, every), :], fa.at[pl.ds(3 * every, every), :], f_s.at[13], f_r.at[13], f_dev(1)
+        )
+        cp.start()
+        sent.append(cp)
+        got_a[(2, 3, 0)] = cp
 
     head = HEAD_SIZE
     heads = wq_ref.shape[1] // head
@@ -604,6 +692,7 @@
         (-2.0 / head * jnp.log(jnp.float32(theta_base))) * lax.rem(lane, head // 2).astype(f32)
     )
     allowed = []
+    loads["tok"].wait()
     for m in range(micro):
         states = tok_ref[m].astype(f32)
         scale = lax.rsqrt(jnp.mean(states * states, axis=1, keepdims=True) + epsilon)
@@ -618,6 +707,9 @@
     def rope(u, m):
         return u * tab_ref[m, 0] + pltpu.roll(u, head // 2, 1) * tab_ref[m, 1]
 
+    factor(0, fn)
+    save(nrm_ref, nrm_hbm)
+    save(tab_ref, tab_hbm)
     everything = nrm_ref[...].reshape(micro * length, width)
 
     def project(i):
@@ -628,8 +720,9 @@
                 u = both[m * length : (m + 1) * length, j * head : (j + 1) * head]
                 q_ref[m, at, :] = rope(u, m).astype(bf)
 
+    for name in ("wq", "wk", "wv"):
+        loads[name].wait()
     tiles(wq_ref.shape[1] // tw, project)
-    z_forward(0, 0)
     key_pre = mm(everything, wk_ref[...])
     value_pre = mm(everything, wv_ref[...])
     for m in range(micro):
@@ -646,6 +739,14 @@
         out = mm(weight.astype(bf), v_ref[m]).astype(bf)
         for h in range(heads):
             att_ref[m, :, h * head : (h + 1) * head] = out[h * length : (h + 1) * length]
+    for src, dst in ((q_ref, q_hbm), (k_ref, k_hbm), (v_ref, v_hbm), (pr_ref, pr_hbm), (att_ref, att_hbm)):
+        save(src, dst)
+    factor(2, fa)
+    z_forward(0, 0)
+    z_sent(0, 0)
+    for m in range(1, micro):
+        z_send(m, 0)
+    loads["wo"].wait()
     att_all = att_ref[...].reshape(micro * length, heads * head)
     got_part = []
     for j in range(3):
@@ -663,7 +764,6 @@
         sent.append(cp)
         got_part.append(cp)
 
-    z_forward(1, 0)
     for cp in got_r:
         cp.wait_recv()
 
@@ -695,26 +795,34 @@
 
     def pack(m, a):
         src, out, dst = ((gz, gs, gr), (xz, xs, xr))[a]
-        for k in (1, 3):
-            got_z[(m, a, k)].wait_recv()
-
-        def body(i):
-            at = cols(i, tw)
-            out[m, :, at] = mm(onehot[m], src[m, :, at]).astype(bf)
-
-        tiles(nt, body)
-        if a == 1:
-            out[m, :, width:] = mm(onehot[m], src[m, :, width:]).astype(bf)
-        dst[m, 0:blk, :] = out[m, 0:blk, :]
-        for d in range(1, 8):
-            i = (m * 2 + a) * 8 + d
-            at = pl.ds(d * blk, blk)
-            cp = remote(out.at[m, at, :], dst.at[m, at, :], xa_s.at[i], xa_r.at[i], p_dev(d))
-            cp.start()
-            sent_p.setdefault((m, a), []).append(cp)
-            got_p[(m, a, d)] = cp
+        if a == 0:
+            loads[("g", m)].wait()
+        for j, (left, size) in enumerate(parts[a]):
+            for k in (1, 3):
+                got_z[(m, a, j, k)].wait_recv()
+
+            def body(i, left=left):
+                at = cols(i + left // tw, tw)
+                out[m, :, at] = mm(onehot[m], src[m, :, at]).astype(bf)
+
+            tiles(size // tw, body)
+            if (left + size) % tw:
+                out[m, :, width:] = mm(onehot[m], src[m, :, width:]).astype(bf)
+            wide = slice(left, left + size)
+            dst[m, 0:blk, wide] = out[m, 0:blk, wide]
+            wide = pl.ds(left, size)
+            for d in range(1, 8):
+                i = sem_of(m, a, j, d, 8)
+                at = pl.ds(d * blk, blk)
+                cp = remote(
+                    out.at[m, at, wide], dst.at[m, at, wide], xa_s.at[i], xa_r.at[i], p_dev(d)
+                )
+                cp.start()
+                sent_p.setdefault((m, a), []).append(cp)
+                got_p[(m, a, j, d)] = cp
 
     sent_p = {}
+    pack(0, 0)
     tall = lax.broadcasted_iota(jnp.int32, (128, EXPERTS), 0)
     double = (lax.rem(tall, EXPERTS) == lax.broadcasted_iota(jnp.int32, (128, EXPERTS), 1)) & (
         tall < 2 * EXPERTS
@@ -726,6 +834,7 @@
         at = slice(m * length, (m + 1) * length)
         state = tok_ref[m].astype(f32) + (own_part[at, :] + other_part[at, :])
         hs_ref[m] = state
+        save(hs_ref.at[m], hs_hbm.at[m])
         scale = lax.rsqrt(jnp.mean(state * state, axis=1, keepdims=True) + epsilon)
         low = (state * scale * gain_f[...].reshape(1, width)).astype(bf)
         x_ref[m, :, 0:width] = low
@@ -743,14 +852,24 @@
         weight = weight / first
         top = weight.astype(bf).astype(f32)
         x_ref[m, :, width:] = jnp.where(lane < EXPERTS, top, weight - top).astype(bf)
+        if m == 0:
+            z_send(m, 1)
+        save(x_ref.at[m], x_hbm.at[m])
+    for m in range(1, micro):
+        z_forward(m, 0)
+        pack(m, 0)
+    pass_on()
+    z_forward(0, 1)
+    z_sent(0, 1)
+    for m in range(1, micro):
         z_send(m, 1)
-    for m in range(micro):
-        pack(m, 0)
-    for m in range(micro):
+    pack(0, 1)
+    for m in range(1, micro):
         z_forward(m, 1)
         pack(m, 1)
-    for cp in loads:
-        cp.wait()
+    for name in ("wg", "wu", "wd"):
+        loads[name].wait()
+    save(onehot.at[1], hot_hbm)
 
     got_b = {}
     def to_pair(m):
@@ -765,25 +884,27 @@
             got_b[("pair", m, i)] = cp
             cp = pltpu.make_async_copy(src_at, dst.at[c, m], own_sem.at[n])
             cp.start()
-            loads.append(cp)
-
-    loads.clear()
-
-    def send_back(m, a):
-        src, dst = ((ds_, dr), (ys, yr))[a]
-        dst[m, 0:blk, :] = src[m, 0:blk, :]
+            saves.append(cp)
+
+    def send_back(m, a, j):
+        src, dst = ((ds_.at[m], dr.at[m]), (ys.at[m], y0r))[a]
+        left, size = parts[1 - a][j]
+        wide = slice(left, left + size)
+        dst[0:blk, wide] = src[0:blk, wide]
+        wide = pl.ds(left, size)
         for d in range(1, 8):
-            i = (m * 2 + a) * 8 + d
+            i = sem_of(m, a, j, d, 8)
             at = pl.ds(d * blk, blk)
-            cp = remote(src.at[m, at, :], dst.at[m, at, :], xb_s.at[i], xb_r.at[i], p_back(d))
+            cp = remote(src.at[at, wide], dst.at[at, wide], xb_s.at[i], xb_r.at[i], p_back(d))
             cp.start()
             sent.append(cp)
-            got_b[(m, a, d)] = cp
+            got_b[(m, a, j, d)] = cp
 
     def run(m):
         for a in range(2):
-            for d in range(1, 8):
-                got_p[(m, a, d)].wait_recv()
+            for j in range(len(parts[a])):
+                for d in range(1, 8):
+                    got_p[(m, a, j, d)].wait_recv()
             for cp in sent_p[(m, a)]:
                 cp.wait_send()
         tail = xr[m, :, width:].astype(jnp.float32)
@@ -831,53 +952,56 @@
                 jnp.bfloat16
             )
 
-        tiles(nt, inputs)
+        tiles(cut // tw, inputs)
+        send_back(m, 0, 0)
+        tiles((width - cut) // tw, lambda i: inputs(i + cut // tw))
         total = gg[...]
         high = total.astype(jnp.bfloat16).astype(jnp.float32)
         ds_[m, :, width:] = jnp.where(
             lane == me, high, jnp.where(lane == me + 32, total - high, 0.0)
         ).astype(jnp.bfloat16)
-        send_back(m, 0)
+        send_back(m, 0, 1)
         to_pair(m)
 
     for m in range(micro):
         run(m)
-    for m in range(micro):
-        send_back(m, 1)
+    send_back(0, 1, 0)
+    save(ys.at[1], y1_hbm)
 
     got_c = {}
 
-    def gather(m, a):
-        src, out, dst = ((dr, zd, dz), (yr, zy, yz))[a]
+    def gather(m, j):
+        left, size = parts[1][j]
         for d in range(1, 8):
-            got_b[(m, a, d)].wait_recv()
-        pl.when(inner)(got_f[(m, 1 - a)].wait_send)
+            got_b[(m, 0, j, d)].wait_recv()
+        pl.when(inner)(got_f[(m, 1, j)].wait_send)
 
         def body(i):
-            at = cols(i, tw)
-            out[m, :, at] = mm_tn(onehot[m], src[m, :, at]).astype(bf)
-
-        tiles(nt, body)
-        if a == 0:
-            out[m, :, width:] = mm_tn(onehot[m], src[m, :, width:]).astype(bf)
-        part = rel.at[m, a] if a == 0 else rel.at[m, a, :, 0:width]
+            at = cols(i + left // tw, tw)
+            zd[m, :, at] = mm_tn(onehot[m], dr[m, :, at]).astype(bf)
+
+        tiles(size // tw, body)
+        if j == 1:
+            zd[m, :, width:] = mm_tn(onehot[m], dr[m, :, width:]).astype(bf)
+        wide = pl.ds(left, size)
         far = pl.ds(pl.multiple_of(far_back * half, half), half)
-        relay = remote(out.at[m, far, :], part, rel_s.at[m * 2 + a], rel_r.at[m * 2 + a], beside_dev)
+        relay = remote(
+            zd.at[m, far, wide], rel.at[m, :, wide], rel_s.at[m * 2 + j], rel_r.at[m * 2 + j], beside_dev
+        )
         start_if(edge, relay)
         for k in (1, 3, 2):
-            i = (m * 2 + a) * 4 + k
+            i = (m * 2 + j) * 4 + k
             at = pl.ds(k * half, half)
-            cp = remote(out.at[m, at, :], dst.at[m, at, :], zb_s.at[i], zb_r.at[i], z_back(k))
-            got_c[(m, a, k)] = cp
+            cp = remote(zd.at[m, at, wide], dz.at[m, at, wide], zb_s.at[i], zb_r.at[i], z_back(k))
+            got_c[(m, j, k)] = cp
             if k == 2:
 
                 @pl.when(inner)
                 def _():
                     relay.wait_recv()
-                    wide = out.shape[2]
-                    out[m, 2 * half : 3 * half, :] = (
-                        out[m, 2 * half : 3 * half, :].astype(f32)
-                        + rel[m, a, :, 0:wide].astype(f32)
+                    here = slice(left, left + size)
+                    zd[m, 2 * half : 3 * half, here] = (
+                        zd[m, 2 * half : 3 * half, here].astype(f32) + rel[m, :, here].astype(f32)
                     ).astype(bf)
 
                 cp.start()
@@ -885,37 +1009,56 @@
             else:
                 start_if(not_first if k == 1 else not_last, cp)
 
-    def finish(m, a):
-        own, other, out = ((zd, dz, dx_ref), (zy, yz, lay_ref))[a]
-        pl.when(not_last)(got_c[(m, a, 1)].wait_recv)
-        pl.when(not_first)(got_c[(m, a, 3)].wait_recv)
-        got_c[(m, a, 2)].wait_recv()
-        total = own[m, 0:half, :].astype(jnp.float32)
+    def finish(m, j):
+        left, size = parts[1][j]
+        here = slice(left, left + size)
+        pl.when(not_last)(got_c[(m, j, 1)].wait_recv)
+        pl.when(not_first)(got_c[(m, j, 3)].wait_recv)
+        got_c[(m, j, 2)].wait_recv()
+        total = zd[m, 0:half, here].astype(f32)
         for k in range(1, 4):
-            total = total + other[m, k * half : (k + 1) * half, :].astype(jnp.float32)
-        if a == 1:
-            total = hs_ref[m, mine, :] + total
-        out[m, mine, :] = total.astype(out.dtype)
-        n = m * 8 + 5 + a
+            total = total + dz[m, k * half : (k + 1) * half, here].astype(f32)
+        dx_ref[m, mine, here] = total
+        n = m * 8 + 5 + j
+        wide = pl.ds(left, size)
         cp = remote(
-            out.at[m, mine, :], out.at[m, mine, :], pair_s.at[n], pair_r.at[n], (e, 1 - c)
+            dx_ref.at[m, mine, wide], dx_ref.at[m, mine, wide], pair_s.at[n], pair_r.at[n], (e, 1 - c)
         )
         cp.start()
         sent.append(cp)
-        got_c[("pair", m, a)] = cp
-
-    order = [(m, a) for a in range(2) for m in range(micro)]
-    for i, (m, a) in enumerate(order):
-        gather(m, a)
+        got_c[("pair", m, j)] = cp
+
+    order = [(m, j) for m in range(micro) for j in range(2)]
+    for i, (m, j) in enumerate(order):
+        gather(m, j)
         if i >= 1:
             finish(*order[i - 1])
+    for d in range(1, 8):
+        got_b[(0, 1, 0, d)].wait_recv()
+    pl.when(inner)(got_f[(0, 0, 0)].wait_send)
+
+    def outputs(i):
+        at = cols(i, tw)
+        gz[0, :, at] = mm_tn(onehot[0], y0r[:, at]).astype(bf)
+
+    tiles(nt, outputs)
+    save(gz.at[0], y0_hbm)
+    pl.when(inner)(got_f[(1, 0, 0)].wait_send)
     finish(*order[-1])
+    to_twin(3)
+    got_a[(2, 3, 0)].wait_recv()
+    for m in range(micro):
+        got_a[(2, 1, m)].wait_recv()
+    for d in range(1, 4):
+        got_a[("twin", d)].wait_recv()
     for m in range(micro):
         for i in range(5):
             got_b[("pair", m, i)].wait_recv()
-        for a in range(2):
-            got_c[("pair", m, a)].wait_recv()
-    for cp in loads:
+        for j in range(2):
+            got_c[("pair", m, j)].wait_recv()
+    for at in list(away):
+        z_sent(*at)
+    for cp in saves:
         cp.wait()
     for cp in sent:
         cp.wait_send()
@@ -947,13 +1090,13 @@
 
     sem = pltpu.SemaphoreType.DMA
     col = 4 * half
+    hw = wq.shape[1]
     return pl.pallas_call(
         front_kernel,
         out_shape=(
-            out(micro, length, width),
             out(micro, length, wide, dtype=f32),
             out(micro, length, width),
-            out(micro, length, wq.shape[1]),
+            out(micro, length, hw),
             out(micro, heads * length, HEAD_SIZE),
             out(micro, length, HEAD_SIZE),
             out(micro, length, HEAD_SIZE),
@@ -961,26 +1104,36 @@
             out(micro, 2, length, HEAD_SIZE, dtype=f32),
             out(micro, length, width, dtype=f32),
             out(micro, length, wide),
+            out(col, width),
+            out(rows, width),
+            out(rows, col),
+            out(4 * micro * length, width // 2),
+            out(4 * micro * length, hw // 2),
             out(2, micro, rows, width),
             out(2, micro, rows, ff),
             out(2, micro, rows, ff),
             out(2, micro, rows, ff),
             out(2, micro, rows, width),
         ),
-        in_specs=[vmem] * 11 + [hbm] * 3,
-        out_specs=(vmem,) * 11 + (hbm,) * 5,
+        in_specs=[hbm] * 9 + [vmem] * 5,
+        out_specs=(vmem,) + (hbm,) * 19,
         scratch_shapes=[
+            buf(micro, length, width), buf(width, hw), buf(width, HEAD_SIZE), buf(width, HEAD_SIZE), buf(hw, width),
+            buf(micro, length, width), buf(micro, length, hw), buf(micro, heads * length, HEAD_SIZE),
+            buf(micro, length, HEAD_SIZE), buf(micro, length, HEAD_SIZE),
+            buf(micro, heads * length, length, dtype=f32), buf(micro, 2, length, HEAD_SIZE, dtype=f32),
+            buf(micro, length, width, dtype=f32), buf(micro, length, wide),
             buf(micro, col, wide), buf(micro, col, width), pltpu.VMEM((4, *routes.shape), jnp.int32),
             buf(micro, rows, wide), buf(micro, rows, width), buf(micro, rows, wide), buf(micro, rows, width),
             buf(micro, rows, width), buf(micro, rows, ff), buf(micro, rows, ff), buf(micro, rows, ff),
-            buf(micro, rows, width), buf(micro, rows, wide), buf(micro, col, width), buf(micro, col, wide),
+            buf(rows, width), buf(micro, rows, wide), buf(micro, col, wide),
             buf(micro * length, width, dtype=f32), buf(micro * length, width, dtype=f32),
-            buf(micro, 2, half, wide), buf(micro, rows, col), buf(rows, 128, dtype=f32), buf(rows, 128, dtype=f32),
+            buf(micro, half, wide), buf(micro, rows, col), buf(rows, 128, dtype=f32), buf(rows, 128, dtype=f32),
             buf(width, ff), buf(width, ff), buf(ff, width),
-            sem((4,)), sem((4,)), sem((8 * micro,)), sem((8 * micro,)), sem((16 * micro,)), sem((16 * micro,)),
-            sem((16 * micro,)), sem((16 * micro,)), sem((8 * micro,)), sem((8 * micro,)), sem((8 * micro,)),
-            sem((8 * micro,)), sem((3,)), sem((3,)), sem((2 * micro,)), sem((2 * micro,)), sem((2 * micro,)),
-            sem((2 * micro,)), sem((3,)), sem((8 * micro,)),
+            sem((4,)), sem((4,)), sem((16 * micro,)), sem((16 * micro,)), sem((32 * micro,)), sem((32 * micro,)),
+            sem((32 * micro,)), sem((32 * micro,)), sem((8 * micro,)), sem((8 * micro,)), sem((8 * micro,)),
+            sem((8 * micro,)), sem((3,)), sem((3,)), sem((4 * micro,)), sem((2 * micro,)), sem((2 * micro,)),
+            sem((14,)), sem((14,)), sem((4,)), sem((4,)), sem((8 + micro,)), sem((16 + 5 * micro,)), sem((8 * micro,)),
         ],
         compiler_params=pltpu.CompilerParams(
             collective_id=1, has_side_effects=True, vmem_limit_bytes=VMEM_LIMIT
@@ -990,60 +1143,25 @@
         ),
         name="front",
     )(
-        tokens, cotangent, positions, routes, gain_a, gain_f, wq, wk, wv, wo, router, gate_weight,
-        up_weight, down_weight,
-    )
-
-
-def grads_kernel(x_ref, h_ref, g_ref, u_ref, e_ref, gate_out, up_out, down_out):
-    gate_out[...] = mm_tn(x_ref[0], g_ref[0])
-    up_out[...] = mm_tn(x_ref[0], u_ref[0])
-    down_out[...] = mm_tn(h_ref[0], e_ref[0])
-
-
-def grads_call(rx, rh, rg, ru, re):
-    _, micro, rows, width = rx.shape
-    ff = rh.shape[3]
-    n = micro * rows
-    tw = 256
-    per = ff // tw
-    f32 = jnp.float32
-    wide = pl.BlockSpec((1, n, width), lambda i: (i // per, 0, 0))
-    thin = pl.BlockSpec((1, n, tw), lambda i: (i // per, 0, i % per))
-    return pl.pallas_call(
-        grads_kernel,
-        grid=(2 * per,),
-        in_specs=[wide, thin, thin, thin, wide],
-        out_specs=(
-            pl.BlockSpec((width, tw), lambda i: (0, i)),
-            pl.BlockSpec((width, tw), lambda i: (0, i)),
-            pl.BlockSpec((tw, width), lambda i: (i, 0)),
-        ),
-        out_shape=(
-            jax.ShapeDtypeStruct((width, 2 * ff), f32),
-            jax.ShapeDtypeStruct((width, 2 * ff), f32),
-            jax.ShapeDtypeStruct((2 * ff, width), f32),
-        ),
-        compiler_params=pltpu.CompilerParams(vmem_limit_bytes=VMEM_LIMIT),
-        cost_estimate=pl.CostEstimate(
-            flops=2 * 6 * n * width * ff, bytes_accessed=45 * 2**20, transcendentals=0
-        ),
-        name="expert_grads",
-    )(
-        rx.reshape(2, n, width), rh.reshape(2, n, ff), rg.reshape(2, n, ff),
-        ru.reshape(2, n, ff), re.reshape(2, n, width),
+        tokens, cotangent, wq, wk, wv, wo, gate_weight, up_weight, down_weight,
+        positions, routes, gain_a, gain_f, router,
     )
 
 
 def back_kernel(
-    tok_ref, g_ref, gain_a, gain_f, wq_ref, wk_ref, wv_ref, wo_ref, router_ref,
-    dx_ref, nrm_ref, att_ref, q_ref, k_ref, v_ref, pr_ref, tab_ref, hs_ref, x_ref,
-    tg_ref, oa, ob, os,
+    tok_hbm, g_hbm, wq_hbm, wk_hbm, wv_hbm, wo_hbm,
+    dx_hbm, nrm_hbm, att_hbm, q_hbm, k_hbm, v_hbm, pr_hbm, tab_hbm, hs_hbm, x_hbm, y0_hbm, y1_hbm, hot_hbm,
+    fn_hbm, fa_hbm, gain_a, gain_f, router_ref,
+    lay_ref, tg_hbm, oa, ob_hbm, os,
+    tok_ref, g_ref, wq_ref, wk_ref, wv_ref, wo_ref, dx_ref, q_ref, k_ref, v_ref, pr_ref, tab_ref, hs_ref, x_ref,
+    hot, y1r, zy, yz, rel, tg_ref, ob,
     d_ref, a_ref, s_ref, sg, ag, own_part, other_part,
     fn, fd, fa, fg, fs, pa, pb, za, zb, zs, ra, rb,
     f_s, f_r, w_s, w_r, c_s, c_r, y_s, y_r, l_s, l_r, z_s, z_r, h_s, h_r, p_s, p_r, part_s, part_r,
+    yp_s, yp_r, yz_s, yz_r, rel_s, rel_r, pair_s, pair_r, in_sem, out_sem,
 ):
     micro, length, width = tok_ref.shape
+    half = length // 2
     f32 = jnp.float32
     bf = jnp.bfloat16
     head = HEAD_SIZE
@@ -1051,7 +1169,6 @@
     wq = wq_ref.shape[1]
     tw = 256
     nt = width // tw
-    n_ref = nrm_ref
     e = lax.axis_index("expert")
     c = lax.axis_index("tensor")
     z = e // 4
@@ -1059,9 +1176,9 @@
     qx = lax.rem(q, 2)
     qy = q // 2
     rows = micro * length
-    wn = n_ref.shape[1] // 2
+    wn = fn.shape[1]
     wd = d_ref.shape[1] // 2
-    wa = att_ref.shape[1] // 2
+    wa = fa.shape[1]
     per = length
     wg = a_ref.shape[1] // 2
     ws = s_ref.shape[1] // 4
@@ -1094,6 +1211,21 @@
         pl.when(cond)(cp.start)
         sent_if.append((cond, cp))
 
+    o = q * 2 + c
+    blk = y1r.shape[0] // 8
+    own_rows = pl.ds(pl.multiple_of(c * half, half), half)
+
+    def any_dev(n):
+        t = lax.rem(o + n, 8)
+        return (z * 4 + t // 2, lax.rem(t, 2))
+
+    def any_back(n):
+        t = lax.rem(o + 8 - n, 8)
+        return (z * 4 + t // 2, lax.rem(t, 2))
+
+    def fill(m, slot):
+        yz[m, slot * half : (slot + 1) * half, :] = jnp.zeros((half, width), bf)
+
     def clear(slot):
         za[slot] = jnp.zeros((ha, wd), bf)
         zb[slot] = jnp.zeros((hb, wg), bf)
@@ -1101,16 +1233,45 @@
     pl.when(z == 0)(lambda: clear(1))
     pl.when(z == 3)(lambda: clear(3))
 
+    for m in range(micro):
+        pl.when(z == 3)(lambda m=m: fill(m, 1))
+        pl.when(z == 0)(lambda m=m: fill(m, 3))
+
     barrier = pltpu.get_barrier_semaphore()
-    for k in range(1, 4):
-        pl.semaphore_signal(barrier, inc=1, device_id=z_dev(k), device_id_type=MESH)
-        pl.semaphore_signal(barrier, inc=1, device_id=p_dev(k), device_id_type=MESH)
-    pl.semaphore_signal(barrier, inc=1, device_id=(e, 1 - c), device_id_type=MESH)
-    pl.semaphore_wait(barrier, 7)
+    for n in range(1, 4):
+        pl.semaphore_signal(barrier, inc=1, device_id=z_dev(n), device_id_type=MESH)
+    for n in range(1, 8):
+        pl.semaphore_signal(barrier, inc=1, device_id=any_dev(n), device_id_type=MESH)
+    loads = {}
+    for i, (name, src, dst) in enumerate(
+        (
+            ("dx", dx_hbm, dx_ref), ("x", x_hbm, x_ref), ("hs", hs_hbm, hs_ref), ("g", g_hbm, g_ref),
+            ("y0", y0_hbm, zy.at[0]), ("y1", y1_hbm.at[0:blk, :], y1r.at[0:blk, :]), ("wo", wo_hbm, wo_ref),
+            ("v", v_hbm, v_ref), ("pr", pr_hbm, pr_ref), ("k", k_hbm, k_ref), ("q", q_hbm, q_ref),
+            ("tab", tab_hbm, tab_ref), ("wq", wq_hbm, wq_ref), ("wk", wk_hbm, wk_ref), ("wv", wv_hbm, wv_ref),
+            ("hot", hot_hbm, hot), ("tok", tok_hbm, tok_ref),
+            ("fa", fa_hbm.at[rows:, :], fa.at[rows:, :]), ("fa0", att_hbm.at[:, part(qy, wa)], fa.at[0:rows, :]),
+            ("fn", fn_hbm.at[rows:, :], fn.at[rows:, :]), ("fn0", nrm_hbm.at[:, part(qx, wn)], fn.at[0:rows, :]),
+        )
+    ):
+        loads[name] = pltpu.make_async_copy(src, dst, in_sem.at[i])
+        loads[name].start()
+    saves = []
+
+    def save(src, dst):
+        cp = pltpu.make_async_copy(src, dst, out_sem.at[len(saves)])
+        cp.start()
+        saves.append(cp)
+
+    def need(*names):
+        for name in names:
+            loads[name].wait()
+
+    pl.semaphore_wait(barrier, 10)
 
     sent = []
     got_f = {}
-    bits = {0: 0, 3: 0, 1: 1, 2: 1}
+    bits = {3: 0, 1: 1}
 
     def piece(src, i, d):
         bit = flip(qx, d % 2) if bits[i] == 0 else flip(qy, d // 2)
@@ -1164,8 +1325,63 @@
             for d in (1, 2, 3):
                 got_f[("twin", i, d)].wait_recv()
 
-    factor(2, att_ref, fa)
-
+    got_v = {}
+    def send_y1(j):
+        wide = pl.ds(j * (width // 2), width // 2)
+        for n in range(1, 8):
+            at = pl.ds(n * blk, blk)
+            cp = remote(
+                y1_hbm.at[at, wide], y1r.at[at, wide], yp_s.at[j * 8 + n], yp_r.at[j * 8 + n], any_back(n)
+            )
+            cp.start()
+            sent.append(cp)
+            got_v[(n, j, "row")] = cp
+
+    send_y1(0)
+
+    def z_back(n):
+        return (lax.rem(z + 4 - n, 4) * 4 + q, c)
+
+    def send_far(m):
+        far = part(jnp.where(z == 0, 1, 3), half)
+        cp = remote(zy.at[m, far, :], rel.at[m], rel_s.at[m], rel_r.at[m], beside_dev)
+        start_if(edge, cp)
+        got_v[("far", m)] = cp
+        for n in (1, 3):
+            at = pl.ds(n * half, half)
+            cp = remote(zy.at[m, at, :], yz.at[m, at, :], yz_s.at[m * 4 + n], yz_r.at[m * 4 + n], z_back(n))
+            start_if(not_first if n == 1 else not_last, cp)
+            got_v[(m, n)] = cp
+
+    def send_near(m):
+        at = pl.ds(2 * half, half)
+
+        @pl.when(inner)
+        def _():
+            got_v[("far", m)].wait_recv()
+            zy[m, at, :] = (zy[m, at, :].astype(f32) + rel[m].astype(f32)).astype(bf)
+
+        cp = remote(zy.at[m, at, :], yz.at[m, at, :], yz_s.at[m * 4 + 2], yz_r.at[m * 4 + 2], z_back(2))
+        cp.start()
+        sent.append(cp)
+        got_v[(m, 2)] = cp
+
+    def layer(m):
+        pl.when(not_last)(got_v[(m, 1)].wait_recv)
+        pl.when(not_first)(got_v[(m, 3)].wait_recv)
+        got_v[(m, 2)].wait_recv()
+        total = zy[m, 0:half, :].astype(f32)
+        for n in range(1, 4):
+            total = total + yz[m, n * half : (n + 1) * half, :].astype(f32)
+        lay_ref[m, own_rows, :] = (hs_ref[m, own_rows, :] + total).astype(bf)
+        cp = remote(
+            lay_ref.at[m, own_rows, :], lay_ref.at[m, own_rows, :], pair_s.at[m], pair_r.at[m], twin
+        )
+        cp.start()
+        sent.append(cp)
+        got_v[("pair", m)] = cp
+
+    need("dx", "x", "hs", "g")
     lane = lax.broadcasted_iota(jnp.int32, (1, 128), 1)
     gain_row = jnp.zeros((1, width), f32)
     s_ref[...] = jnp.zeros_like(s_ref)
@@ -1190,8 +1406,8 @@
         gain_row = gain_row + jnp.sum(full * state * scale, axis=0, keepdims=True)
     s_ref[0:EXPERTS, :] = router_row[0:EXPERTS].astype(bf)
     factor(3, a_ref, fg)
-    factor(0, n_ref, fn)
-    relay(2, fa)
+    need("y0", "wo")
+    send_far(0)
 
     def inward(i):
         at = cols(i, tw)
@@ -1203,6 +1419,8 @@
 
     tiles(wq // tw, inward)
     relay(3, fg)
+    send_near(0)
+    need("v", "pr", "k", "q", "tab")
 
     def unrope(u, m):
         return u * tab_ref[m, 0] - pltpu.roll(u, head // 2, 1) * tab_ref[m, 1]
@@ -1221,7 +1439,7 @@
         d_ref[here, wq : wq + head] = unrope(dk, m).astype(bf)
         d_ref[here, wq + head : wq + 2 * head] = mm_tn(prob.astype(bf), ag[m]).astype(bf)
     factor(1, d_ref, fd)
-    relay(0, fn)
+    need("wq", "wk", "wv")
     got_part = []
     for j in range(3):
 
@@ -1241,11 +1459,9 @@
         cp.start()
         sent.append(cp)
         got_part.append(cp)
-    fn[0:rows, :] = n_ref[:, part(qx, wn)]
     fd[0:rows, :] = d_ref[:, part(qy, wd)]
-    fa[0:rows, :] = att_ref[:, part(qy, wa)]
     fg[0:rows, :] = a_ref[:, part(qx, wg)]
-    arrive(2, fa)
+    need("fa", "fa0")
     arrive(3, fg)
 
     def two(i):
@@ -1285,6 +1501,8 @@
 
     spread(1)
     relay(1, fd)
+    send_y1(1)
+    need("tok")
     for cp in got_part:
         cp.wait_recv()
     last_row = jnp.zeros((1, width), f32)
@@ -1296,6 +1514,7 @@
         u = full * gain_a[...].reshape(1, width)
         common = jnp.mean(u * state, axis=1, keepdims=True) * (scale * scale * scale)
         tg_ref[m] = sg[m] + (scale * u - state * common)
+        save(tg_ref.at[m], tg_hbm.at[m])
         last_row = last_row + jnp.sum(full * state * scale, axis=0, keepdims=True)
     index = lax.broadcasted_iota(jnp.int32, (hs, 1), 0)
     s_ref[2 * hs : 3 * hs, :] = jnp.where(
@@ -1309,7 +1528,7 @@
         sent.append(cp)
         got_s.append(cp)
     spread_rest(1)
-    arrive(0, fn)
+    need("fn", "fn0")
     arrive(1, fd)
 
     def one(i):
@@ -1333,6 +1552,18 @@
         sent.append(cp)
         got_y[(2, k)] = cp
     spread_rest(0)
+    layer(0)
+    need("y1", "hot")
+    for n in range(1, 8):
+        for j in range(2):
+            got_v[(n, j, "row")].wait_recv()
+
+    def outputs(i):
+        at = cols(i, tw)
+        zy[1, :, at] = mm_tn(hot[...], y1r[:, at]).astype(bf)
+
+    tiles(nt, outputs)
+    send_far(1)
 
     def spots(px, py, t):
         return (
@@ -1412,6 +1643,7 @@
     own(1, 1)
     forward(0, 1)
     own(1, 0)
+    send_near(1)
     forward(0, 0)
     forward(0, 2)
     own(1, 2)
@@ -1421,11 +1653,18 @@
             forward(n - 1, i)
     for i in (1, 0, 2):
         forward(3, i)
-    for n in range(4):
-        for i in range(3):
+    layer(1)
+    for i in (1, 0, 2):
+        for n in range(4):
             first = 1 if i == 1 else 2
             got_p[(n, i, first)].wait_recv()
             got_p[(n, i, 3)].wait_recv()
+        if i == 1:
+            save(ob, ob_hbm)
+    for m in range(micro):
+        got_v[("pair", m)].wait_recv()
+    for cp in saves:
+        cp.wait()
     for cp in sent:
         cp.wait_send()
     for cond, cp in sent_if:
@@ -1433,19 +1672,25 @@
 
 
 def back_call(
-    tokens, cotangent, gain_a, gain_f, wq, wk, wv, wo, router, dx, nrm, att, q, k, v, pr, tab, hs, xrows
+    tokens, cotangent, gain_a, gain_f, wq, wk, wv, wo, router,
+    dx, nrm, att, q, k, v, pr, tab, hs, xrows, y0, y1, hot, fn, fa,
 ):
     bf = jnp.bfloat16
     f32 = jnp.float32
     micro, length, width = tokens.shape
     rows = micro * length
+    half = length // 2
     wd = wq.shape[1] + wk.shape[1] + wv.shape[1]
     wa = wq.shape[1]
     heads = wa // HEAD_SIZE
     vmem = pl.BlockSpec(memory_space=pltpu.VMEM)
+    hbm = pl.BlockSpec(memory_space=ANY)
 
     def buf(*shape, dtype=bf):
         return pltpu.VMEM(shape, dtype)
+
+    def like(array):
+        return pltpu.VMEM(array.shape, array.dtype)
 
     sem = pltpu.SemaphoreType.DMA
     small = (64, width)
@@ -1453,14 +1698,18 @@
     return pl.pallas_call(
         back_kernel,
         out_shape=(
+            jax.ShapeDtypeStruct((micro, length, width), bf),
             jax.ShapeDtypeStruct((micro, length, width), f32),
             jax.ShapeDtypeStruct((width, wd), bf),
             jax.ShapeDtypeStruct((wa, width), bf),
             jax.ShapeDtypeStruct(small, bf),
         ),
-        in_specs=[vmem] * 19,
-        out_specs=(vmem,) * 4,
+        in_specs=[hbm] * 21 + [vmem] * 3,
+        out_specs=(vmem, hbm, vmem, hbm, vmem),
         scratch_shapes=[
+            like(tokens), like(cotangent), like(wq), like(wk), like(wv), like(wo), like(dx), like(q), like(k),
+            like(v), like(pr), like(tab), like(hs), like(xrows), like(hot), like(y1), buf(micro, 4 * half, width),
+            buf(micro, 4 * half, width), buf(micro, half, width), buf(micro, length, width, dtype=f32), buf(wa, width),
             buf(rows, wd), buf(rows, width), buf(*small), buf(micro, length, width, dtype=f32),
             buf(micro, heads * length, HEAD_SIZE), buf(rows, width, dtype=f32), buf(rows, width, dtype=f32),
             buf(4 * rows, width // 2), buf(4 * rows, wd // 2), buf(4 * rows, wa // 2), buf(4 * rows, width // 2),
@@ -1471,6 +1720,8 @@
             sem((16,)), sem((16,)), sem((16,)), sem((16,)), sem((4,)), sem((4,)), sem((12,)), sem((12,)),
             sem((2,)), sem((2,)), sem((12,)), sem((12,)), sem((3,)), sem((3,)), sem((48,)), sem((48,)),
             sem((3,)), sem((3,)),
+            sem((16,)), sem((16,)), sem((4 * micro,)), sem((4 * micro,)), sem((micro,)), sem((micro,)), sem((micro,)),
+            sem((micro,)), sem((21,)), sem((1 + micro,)),
         ],
         compiler_params=pltpu.CompilerParams(
             collective_id=2, has_side_effects=True, vmem_limit_bytes=VMEM_LIMIT
@@ -1480,8 +1731,77 @@
         ),
         name="back",
     )(
-        tokens, cotangent, gain_a, gain_f, wq, wk, wv, wo, router,
-        dx, nrm.reshape(rows, width), att.reshape(rows, wa), q, k, v, pr, tab, hs, xrows,
+        tokens, cotangent, wq, wk, wv, wo,
+        dx, nrm.reshape(rows, width), att.reshape(rows, wa), q, k, v, pr, tab, hs, xrows, y0, y1, hot, fn, fa,
+        gain_a, gain_f, router,
+    )
+
+
+def grads_kernel(
+    x_ref, h_ref, g_ref, u_ref, e_ref, qkv_ref, o_ref, s_ref,
+    gate_out, up_out, down_out, q_out, k_out, v_out, o_out, router_out, ffn_out, att_out,
+):
+    gate_out[...] = mm_tn(x_ref[0], g_ref[0])
+    up_out[...] = mm_tn(x_ref[0], u_ref[0])
+    down_out[...] = mm_tn(h_ref[0], e_ref[0])
+    wq = q_out.shape[1]
+    wk = wq + k_out.shape[1]
+    f32 = jnp.float32
+    q_out[...] = qkv_ref[:, 0:wq].astype(f32)
+    k_out[...] = qkv_ref[:, wq:wk].astype(f32)
+    v_out[...] = qkv_ref[:, wk:].astype(f32)
+    o_out[...] = o_ref[...].astype(f32)
+
+    @pl.when(pl.program_id(0) == 0)
+    def _():
+        small = s_ref[...].astype(f32)
+        router_out[...] = small[0:EXPERTS]
+        width = small.shape[1]
+        ffn_out[...] = small[EXPERTS : EXPERTS + 1].reshape(width)
+        att_out[...] = small[EXPERTS + 1 : EXPERTS + 2].reshape(width)
+
+
+def grads_call(rx, rh, rg, ru, re, qkv, o, small, wq, wk):
+    _, micro, rows, width = rx.shape
+    ff = rh.shape[3]
+    n = micro * rows
+    tw = 256
+    per = ff // tw
+    steps = 2 * per
+    f32 = jnp.float32
+    wide = pl.BlockSpec((1, n, width), lambda i: (i // per, 0, 0))
+    thin = pl.BlockSpec((1, n, tw), lambda i: (i // per, 0, i % per))
+    down = lambda a, w: pl.BlockSpec((a // steps, w), lambda i: (i, 0))
+    whole = lambda *s: pl.BlockSpec(s, lambda i: (0,) * len(s))
+    out = lambda *s: jax.ShapeDtypeStruct(s, f32)
+    wv = qkv.shape[1] - wq - wk
+    return pl.pallas_call(
+        grads_kernel,
+        grid=(steps,),
+        in_specs=[
+            wide, thin, thin, thin, wide,
+            down(*qkv.shape), down(*o.shape), whole(*small.shape),
+        ],
+        out_specs=(
+            pl.BlockSpec((width, tw), lambda i: (0, i)),
+            pl.BlockSpec((width, tw), lambda i: (0, i)),
+            pl.BlockSpec((tw, width), lambda i: (i, 0)),
+            down(width, wq), down(width, wk), down(width, wv), down(*o.shape),
+            whole(EXPERTS, width), whole(width), whole(width),
+        ),
+        out_shape=(
+            out(width, 2 * ff), out(width, 2 * ff), out(2 * ff, width),
+            out(width, wq), out(width, wk), out(width, wv), out(*o.shape),
+            out(EXPERTS, width), out(width), out(width),
+        ),
+        compiler_params=pltpu.CompilerParams(vmem_limit_bytes=VMEM_LIMIT),
+        cost_estimate=pl.CostEstimate(
+            flops=2 * 6 * n * width * ff, bytes_accessed=62 * 2**20, transcendentals=0
+        ),
+        name="expert_grads",
+    )(
+        rx.reshape(2, n, width), rh.reshape(2, n, ff), rg.reshape(2, n, ff),
+        ru.reshape(2, n, ff), re.reshape(2, n, width), qkv, o, small,
     )
 
 
@@ -1494,34 +1814,21 @@
     value_matrix, output_weight, router_weight, gate_weight, up_weight, down_weight,
 ):
     micro_count, length, model_width = tokens.shape
-    f32 = jnp.float32
     gain_a, gain_f = attention_gain, feedforward_gain
     router_t = router_weight.T
-    layer_out, dx, nrm, att, q, k, v, pr, tab, hs, xrows, rx, rh, rg, ru, re = front_call(
+    dx, *kept, rx, rh, rg, ru, re = front_call(
         tokens, cotangent, positions, routes.transpose(0, 2, 1), gain_a, gain_f, query_weight, key_matrix,
         value_matrix, output_weight, router_t, gate_weight, up_weight, down_weight,
     )
-    tokens_grad, oa, ob, os = back_call(
+    layer_out, tokens_grad, oa, ob, os = back_call(
         tokens, cotangent, gain_a, gain_f, query_weight, key_matrix, value_matrix, output_weight,
-        router_t, dx, nrm, att, q, k, v, pr, tab, hs, xrows,
-    )
-    gate_sum, up_sum, down_sum = grads_call(rx, rh, rg, ru, re)
-    wq = query_weight.shape[1]
-    wk = wq + key_matrix.shape[1]
-    os = os.astype(f32)
+        router_t, dx, *kept,
+    )
+    gate, up, down, dq, dk, dv, do, router, ffn_gain, att_gain = grads_call(
+        rx, rh, rg, ru, re, oa, ob, os, query_weight.shape[1], key_matrix.shape[1]
+    )
     return (
-        layer_out,
-        tokens_grad,
-        os[EXPERTS + 1],
-        os[EXPERTS],
-        oa[:, :wq].astype(f32),
-        oa[:, wq:wk].astype(f32),
-        oa[:, wk:].astype(f32),
-        ob.astype(f32),
-        os[:EXPERTS].T,
-        gate_sum,
-        up_sum,
-        down_sum,
+        layer_out, tokens_grad, att_gain, ffn_gain, dq, dk, dv, do, router.T, gate, up, down,
     )
 
 

time: 306 us -> 285 us (0.931)
  Pallas kernels: 293 us -> 281 us
  other arithmetic: 8.55 us -> 0 us
    pallas_call x2, Pallas kernels: 182 us -> 163 us  [the longest x1 136 us: front_call(): pl.pallas_call(front_kernel, out_shape=(out(micro, length, wide, dtype=f3...]
    convert_element_type x4 -> x0, other arithmetic: 8.55 us -> none  [the longest x1 4.65 us: local_fast(): ob.astype(f32)]
    pallas_call x1, Pallas kernels: 111 us -> 118 us  [back_call(): pl.pallas_call(back_kernel, out_shape=(jax.ShapeDtypeStruct((micro, lengt...]
where the time goes in v4:
time: 285 us; the launch traced here: 284 us
  Pallas kernels  281 us (99%)
    pallas_call x1, Pallas kernels, front_call(): pl.pallas_call(front_kernel, out_shape=(out(micro, length, wide, dtype=f3...  136 us
    pallas_call x1, Pallas kernels, back_call(): pl.pallas_call(back_kernel, out_shape=(jax.ShapeDtypeStruct((micro, lengt...  118 us
    pallas_call x1, Pallas kernels, grads_call(): pl.pallas_call(grads_kernel, grid=(steps,), in_specs=[wide, thin, thin, t...  26.2 us

profile of v4, /device:TPU:16, one launch (start us, length us, event | category | flops | bytes accessed | tf_op | source)
XLA Modules:
  0.0 284.3 jit_solution(5179079538098569771)
XLA Ops:
  0.6 136.5 %front.1 = (f32[2,128,1664]{2,1,0:T(8,128)}, bf16[2,128,1536]{2,1,0:T(8,128)(2,1)}, bf16[2,128,768]{2,1,0:T(8,128)(2,1)}, bf16[2,768,128]{2,1,0:T(8,128)(2,1)}, ...) custom-call(bf16[2,128,1536]{2,1,0:T(8,128)(2,1)} %tok_hbm.3, ...), custom_call_target="tpu_custom_call" | custom-call | flops 10871635968 | bytes 41943040 | tf_op jit(solution)/shard_map/front/pallas_call | solution.py:1094
  137.1 118.1 %back.1 = (bf16[2,128,1536]{2,1,0:T(8,128)(2,1)}, f32[2,128,1536]{2,1,0:T(8,128)}, bf16[1536,1024]{1,0:T(8,128)(2,1)}, bf16[768,1536]{1,0:T(8,128)(2,1)}, bf16[64,1536]{1,0:T(8,128)(2,1)}) custom-call(bf16[2,128,1536]{2,1,0:T(8,128)(2,1)} %tok_hbm.3, bf16[2,128,1536]{2,1,0:T(8,128)(2,1)} %g_hbm.3, bf16[1536,768]{1,0:T(8,128)(2,1)} %wq_hbm.3, ...), custom_call_target="tpu_custom_call" | custom-call | flops 1409286144 | bytes 20971520 | tf_op jit(solution)/shard_map/back/pallas_call | solution.py:1698
  255.2 0.0 copy-start.1
  255.2 26.2 %expert_grads.1 = (f32[1536,1536]{1,0:T(8,128)}, f32[1536,1536]{1,0:T(8,128)}, f32[1536,1536]{1,0:T(8,128)}, f32[1536,768]{1,0:T(8,128)}, f32[1536,128]{1,0:T(8,...) custom-call(bf16[2,768,1536]{2,1,0:T(8,128)(2,1)} %bitcast.15, ...), custom_call_target="tpu_custom_call" | custom-call | flops 10871635968 | bytes 65011712 | tf_op jit(solution)/shard_map/expert_grads/pallas_call | solution.py:1778
  281.5 0.0 copy-start
  281.5 0.0 copy-done.1
  281.5 0.9 copy.28
  282.4 0.8 copy-done
  283.2 1.1 copy.29
Async XLA Ops:
  255.2 26.3 %copy-start.1 = (bf16[2,128,1536]{2,1,0:T(8,128)(2,1)S(1)}, bf16[2,128,1536]{2,1,0:T(8,128)(2,1)}, u32[]{:S(2)}) copy-start(bf16[2,128,1536]{2,1,0:T(8,128)(2,1)} %get-tuple-element.94) | copy-start | bytes 2359300
  281.5 1.7 copy-start

commit v5 on v4

--- a/solution.py
+++ b/solution.py
@@ -473,10 +473,10 @@
 def front_kernel(
     tok_hbm, g_hbm, wq_hbm, wk_hbm, wv_hbm, wo_hbm, wg_hbm, wu_hbm, wd_hbm,
     pos_ref, routes_ref, gain_a, gain_f, router_ref,
-    dx_ref, nrm_hbm, att_hbm, q_hbm, k_hbm, v_hbm, pr_hbm, tab_hbm, hs_hbm, x_hbm, y0_hbm, y1_hbm, hot_hbm,
+    dx_hbm, nrm_hbm, att_hbm, q_hbm, k_hbm, v_hbm, pr_hbm, tab_hbm, hs_hbm, x_hbm, y0_hbm, y1_hbm, hot_hbm,
     fn, fa, rx_ref, rh_ref, rg_ref, ru_ref, re_ref,
     tok_ref, wq_ref, wk_ref, wv_ref, wo_ref, nrm_ref, att_ref, q_ref, k_ref, v_ref, pr_ref, tab_ref, hs_ref, x_ref,
-    xz, gz, rz, xs, gs, xr, gr, eg, hid, gpg, upg, y0r, dr, dz, own_part, other_part, rel,
+    xz, gz, rz, xs, gs, xr, gr, eg, hid, gpg, upg, dx_ref, dr, dz, own_part, other_part, rel,
     onehot, prob, gg, wg, wu, wd,
     r_s, r_r, za_s, za_r, xa_s, xa_r, xb_s, xb_r, zb_s, zb_r, pair_s, pair_r, part_s, part_r, fw_s, rel_s, rel_r,
     f_s, f_r, w_s, w_r, in_sem, out_sem, own_sem,
@@ -823,6 +823,7 @@
 
     sent_p = {}
     pack(0, 0)
+    pass_on()
     tall = lax.broadcasted_iota(jnp.int32, (128, EXPERTS), 0)
     double = (lax.rem(tall, EXPERTS) == lax.broadcasted_iota(jnp.int32, (128, EXPERTS), 1)) & (
         tall < 2 * EXPERTS
@@ -858,7 +859,6 @@
     for m in range(1, micro):
         z_forward(m, 0)
         pack(m, 0)
-    pass_on()
     z_forward(0, 1)
     z_sent(0, 1)
     for m in range(1, micro):
@@ -869,7 +869,7 @@
         pack(m, 1)
     for name in ("wg", "wu", "wd"):
         loads[name].wait()
-    save(onehot.at[1], hot_hbm)
+    save(onehot, hot_hbm)
 
     got_b = {}
     def to_pair(m):
@@ -887,10 +887,13 @@
             saves.append(cp)
 
     def send_back(m, a, j):
-        src, dst = ((ds_.at[m], dr.at[m]), (ys.at[m], y0r))[a]
+        src, dst = ((ds_.at[m], dr.at[m]), (ys.at[m], y0_hbm))[a]
         left, size = parts[1 - a][j]
-        wide = slice(left, left + size)
-        dst[0:blk, wide] = src[0:blk, wide]
+        if a == 0:
+            wide = slice(left, left + size)
+            dst[0:blk, wide] = src[0:blk, wide]
+        else:
+            save(src.at[0:blk, :], dst.at[0:blk, :])
         wide = pl.ds(left, size)
         for d in range(1, 8):
             i = sem_of(m, a, j, d, 8)
@@ -1033,18 +1036,9 @@
         gather(m, j)
         if i >= 1:
             finish(*order[i - 1])
-    for d in range(1, 8):
-        got_b[(0, 1, 0, d)].wait_recv()
-    pl.when(inner)(got_f[(0, 0, 0)].wait_send)
-
-    def outputs(i):
-        at = cols(i, tw)
-        gz[0, :, at] = mm_tn(onehot[0], y0r[:, at]).astype(bf)
-
-    tiles(nt, outputs)
-    save(gz.at[0], y0_hbm)
-    pl.when(inner)(got_f[(1, 0, 0)].wait_send)
     finish(*order[-1])
+    for m in range(micro):
+        pl.when(inner)(got_f[(m, 0, 0)].wait_send)
     to_twin(3)
     got_a[(2, 3, 0)].wait_recv()
     for m in range(micro):
@@ -1056,6 +1050,9 @@
             got_b[("pair", m, i)].wait_recv()
         for j in range(2):
             got_c[("pair", m, j)].wait_recv()
+        save(dx_ref.at[m], dx_hbm.at[m])
+    for d in range(1, 8):
+        got_b[(0, 1, 0, d)].wait_recv()
     for at in list(away):
         z_sent(*at)
     for cp in saves:
@@ -1104,9 +1101,9 @@
             out(micro, 2, length, HEAD_SIZE, dtype=f32),
             out(micro, length, width, dtype=f32),
             out(micro, length, wide),
-            out(col, width),
             out(rows, width),
-            out(rows, col),
+            out(rows, width),
+            out(micro, rows, col),
             out(4 * micro * length, width // 2),
             out(4 * micro * length, hw // 2),
             out(2, micro, rows, width),
@@ -1116,7 +1113,7 @@
             out(2, micro, rows, width),
         ),
         in_specs=[hbm] * 9 + [vmem] * 5,
-        out_specs=(vmem,) + (hbm,) * 19,
+        out_specs=(hbm,) * 20,
         scratch_shapes=[
             buf(micro, length, width), buf(width, hw), buf(width, HEAD_SIZE), buf(width, HEAD_SIZE), buf(hw, width),
             buf(micro, length, width), buf(micro, length, hw), buf(micro, heads * length, HEAD_SIZE),
@@ -1126,7 +1123,7 @@
             buf(micro, col, wide), buf(micro, col, width), pltpu.VMEM((4, *routes.shape), jnp.int32),
             buf(micro, rows, wide), buf(micro, rows, width), buf(micro, rows, wide), buf(micro, rows, width),
             buf(micro, rows, width), buf(micro, rows, ff), buf(micro, rows, ff), buf(micro, rows, ff),
-            buf(rows, width), buf(micro, rows, wide), buf(micro, col, wide),
+            buf(micro, length, wide, dtype=f32), buf(micro, rows, wide), buf(micro, col, wide),
             buf(micro * length, width, dtype=f32), buf(micro * length, width, dtype=f32),
             buf(micro, half, wide), buf(micro, rows, col), buf(rows, 128, dtype=f32), buf(rows, 128, dtype=f32),
             buf(width, ff), buf(width, ff), buf(ff, width),
@@ -1154,7 +1151,7 @@
     fn_hbm, fa_hbm, gain_a, gain_f, router_ref,
     lay_ref, tg_hbm, oa, ob_hbm, os,
     tok_ref, g_ref, wq_ref, wk_ref, wv_ref, wo_ref, dx_ref, q_ref, k_ref, v_ref, pr_ref, tab_ref, hs_ref, x_ref,
-    hot, y1r, zy, yz, rel, tg_ref, ob,
+    hot, y0r, y1r, zy, yz, rel, tg_ref, ob,
     d_ref, a_ref, s_ref, sg, ag, own_part, other_part,
     fn, fd, fa, fg, fs, pa, pb, za, zb, zs, ra, rb,
     f_s, f_r, w_s, w_r, c_s, c_r, y_s, y_r, l_s, l_r, z_s, z_r, h_s, h_r, p_s, p_r, part_s, part_r,
@@ -1246,10 +1243,10 @@
     for i, (name, src, dst) in enumerate(
         (
             ("dx", dx_hbm, dx_ref), ("x", x_hbm, x_ref), ("hs", hs_hbm, hs_ref), ("g", g_hbm, g_ref),
-            ("y0", y0_hbm, zy.at[0]), ("y1", y1_hbm.at[0:blk, :], y1r.at[0:blk, :]), ("wo", wo_hbm, wo_ref),
+            ("y0", y0_hbm, y0r), ("hot", hot_hbm, hot), ("y1", y1_hbm.at[0:blk, :], y1r.at[0:blk, :]), ("wo", wo_hbm, wo_ref),
             ("v", v_hbm, v_ref), ("pr", pr_hbm, pr_ref), ("k", k_hbm, k_ref), ("q", q_hbm, q_ref),
             ("tab", tab_hbm, tab_ref), ("wq", wq_hbm, wq_ref), ("wk", wk_hbm, wk_ref), ("wv", wv_hbm, wv_ref),
-            ("hot", hot_hbm, hot), ("tok", tok_hbm, tok_ref),
+            ("tok", tok_hbm, tok_ref),
             ("fa", fa_hbm.at[rows:, :], fa.at[rows:, :]), ("fa0", att_hbm.at[:, part(qy, wa)], fa.at[0:rows, :]),
             ("fn", fn_hbm.at[rows:, :], fn.at[rows:, :]), ("fn0", nrm_hbm.at[:, part(qx, wn)], fn.at[0:rows, :]),
         )
@@ -1315,6 +1312,26 @@
             got_f[(i, over)].wait_recv()
             to_twin(i, over, dst)
 
+    def d_rows(d, m):
+        return pl.ds(d * rows + m * per, per)
+
+    def factor_d(m):
+        for d in (2, 1):
+            cp = remote(
+                d_ref.at[pl.ds(m * per, per), part(flip(qy, d // 2), wd)], fd.at[d_rows(d, m), :],
+                f_s.at[d * 4 + m], f_r.at[d * 4 + m], p_dev(d),
+            )
+            cp.start()
+            sent.append(cp)
+            got_f[("d", m, d)] = cp
+
+    def relay_d(m):
+        got_f[("d", m, 2)].wait_recv()
+        cp = remote(fd.at[d_rows(2, m), :], fd.at[d_rows(3, m), :], f_s.at[12 + m], f_r.at[12 + m], p_dev(1))
+        cp.start()
+        sent.append(cp)
+        got_f[("d", m, 3)] = cp
+
     def arrive(i, dst):
         if bits[i]:
             got_f[(i, 1)].wait_recv()
@@ -1341,6 +1358,13 @@
 
     def z_back(n):
         return (lax.rem(z + 4 - n, 4) * 4 + q, c)
+
+    def regroup(m, src):
+        def outputs(i):
+            at = cols(i, tw)
+            zy[m, :, at] = mm_tn(hot[m], src[:, at]).astype(bf)
+
+        tiles(nt, outputs)
 
     def send_far(m):
         far = part(jnp.where(z == 0, 1, 3), half)
@@ -1406,7 +1430,8 @@
         gain_row = gain_row + jnp.sum(full * state * scale, axis=0, keepdims=True)
     s_ref[0:EXPERTS, :] = router_row[0:EXPERTS].astype(bf)
     factor(3, a_ref, fg)
-    need("y0", "wo")
+    need("y0", "hot", "wo")
+    regroup(0, y0r)
     send_far(0)
 
     def inward(i):
@@ -1438,7 +1463,8 @@
         dk = mm_tn(low, q_ref[m]) * (head**-0.5)
         d_ref[here, wq : wq + head] = unrope(dk, m).astype(bf)
         d_ref[here, wq + head : wq + 2 * head] = mm_tn(prob.astype(bf), ag[m]).astype(bf)
-    factor(1, d_ref, fd)
+    for m in range(micro):
+        factor_d(m)
     need("wq", "wk", "wv")
     got_part = []
     for j in range(3):
@@ -1500,7 +1526,8 @@
         got_y[(i, 2)] = cp
 
     spread(1)
-    relay(1, fd)
+    relay_d(0)
+    relay_d(1)
     send_y1(1)
     need("tok")
     for cp in got_part:
@@ -1529,7 +1556,9 @@
         got_s.append(cp)
     spread_rest(1)
     need("fn", "fn0")
-    arrive(1, fd)
+    for m in range(micro):
+        got_f[("d", m, 1)].wait_recv()
+        got_f[("d", m, 3)].wait_recv()
 
     def one(i):
         at = cols(i, tw)
@@ -1553,16 +1582,12 @@
         got_y[(2, k)] = cp
     spread_rest(0)
     layer(0)
-    need("y1", "hot")
+    need("y1")
     for n in range(1, 8):
         for j in range(2):
             got_v[(n, j, "row")].wait_recv()
 
-    def outputs(i):
-        at = cols(i, tw)
-        zy[1, :, at] = mm_tn(hot[...], y1r[:, at]).astype(bf)
-
-    tiles(nt, outputs)
+    regroup(1, y1r)
     send_far(1)
 
     def spots(px, py, t):
@@ -1708,7 +1733,7 @@
         out_specs=(vmem, hbm, vmem, hbm, vmem),
         scratch_shapes=[
             like(tokens), like(cotangent), like(wq), like(wk), like(wv), like(wo), like(dx), like(q), like(k),
-            like(v), like(pr), like(tab), like(hs), like(xrows), like(hot), like(y1), buf(micro, 4 * half, width),
+            like(v), like(pr), like(tab), like(hs), like(xrows), like(hot), like(y0), like(y1), buf(micro, 4 * half, width),
             buf(micro, 4 * half, width), buf(micro, half, width), buf(micro, length, width, dtype=f32), buf(wa, width),
             buf(rows, wd), buf(rows, width), buf(*small), buf(micro, length, width, dtype=f32),
             buf(micro, heads * length, HEAD_SIZE), buf(rows, width, dtype=f32), buf(rows, width, dtype=f32),
@@ -1738,8 +1763,8 @@
 
 
 def grads_kernel(
-    x_ref, h_ref, g_ref, u_ref, e_ref, qkv_ref, o_ref, s_ref,
-    gate_out, up_out, down_out, q_out, k_out, v_out, o_out, router_out, ffn_out, att_out,
+    x_ref, h_ref, g_ref, u_ref, e_ref, qkv_ref, o_ref, s_ref, lay_ref, tok_ref,
+    gate_out, up_out, down_out, q_out, k_out, v_out, o_out, router_out, ffn_out, att_out, lay_out, tok_out,
 ):
     gate_out[...] = mm_tn(x_ref[0], g_ref[0])
     up_out[...] = mm_tn(x_ref[0], u_ref[0])
@@ -1751,6 +1776,8 @@
     k_out[...] = qkv_ref[:, wq:wk].astype(f32)
     v_out[...] = qkv_ref[:, wk:].astype(f32)
     o_out[...] = o_ref[...].astype(f32)
+    lay_out[...] = lay_ref[...]
+    tok_out[...] = tok_ref[...]
 
     @pl.when(pl.program_id(0) == 0)
     def _():
@@ -1761,7 +1788,7 @@
         att_out[...] = small[EXPERTS + 1 : EXPERTS + 2].reshape(width)
 
 
-def grads_call(rx, rh, rg, ru, re, qkv, o, small, wq, wk):
+def grads_call(rx, rh, rg, ru, re, qkv, o, small, layer, tokens_grad, wq, wk):
     _, micro, rows, width = rx.shape
     ff = rh.shape[3]
     n = micro * rows
@@ -1773,6 +1800,8 @@
     thin = pl.BlockSpec((1, n, tw), lambda i: (i // per, 0, i % per))
     down = lambda a, w: pl.BlockSpec((a // steps, w), lambda i: (i, 0))
     whole = lambda *s: pl.BlockSpec(s, lambda i: (0,) * len(s))
+    tall = layer.shape[0] // 4
+    some = pl.BlockSpec((tall, width), lambda i: (jnp.minimum(i, 3), 0))
     out = lambda *s: jax.ShapeDtypeStruct(s, f32)
     wv = qkv.shape[1] - wq - wk
     return pl.pallas_call(
@@ -1780,19 +1809,20 @@
         grid=(steps,),
         in_specs=[
             wide, thin, thin, thin, wide,
-            down(*qkv.shape), down(*o.shape), whole(*small.shape),
+            down(*qkv.shape), down(*o.shape), whole(*small.shape), some, some,
         ],
         out_specs=(
             pl.BlockSpec((width, tw), lambda i: (0, i)),
             pl.BlockSpec((width, tw), lambda i: (0, i)),
             pl.BlockSpec((tw, width), lambda i: (i, 0)),
             down(width, wq), down(width, wk), down(width, wv), down(*o.shape),
-            whole(EXPERTS, width), whole(width), whole(width),
+            whole(EXPERTS, width), whole(width), whole(width), some, some,
         ),
         out_shape=(
             out(width, 2 * ff), out(width, 2 * ff), out(2 * ff, width),
             out(width, wq), out(width, wk), out(width, wv), out(*o.shape),
             out(EXPERTS, width), out(width), out(width),
+            jax.ShapeDtypeStruct(layer.shape, layer.dtype), out(*tokens_grad.shape),
         ),
         compiler_params=pltpu.CompilerParams(vmem_limit_bytes=VMEM_LIMIT),
         cost_estimate=pl.CostEstimate(
@@ -1801,7 +1831,7 @@
         name="expert_grads",
     )(
         rx.reshape(2, n, width), rh.reshape(2, n, ff), rg.reshape(2, n, ff),
-        ru.reshape(2, n, ff), re.reshape(2, n, width), qkv, o, small,
+        ru.reshape(2, n, ff), re.reshape(2, n, width), qkv, o, small, layer, tokens_grad,
     )
 
 
@@ -1824,11 +1854,15 @@
         tokens, cotangent, gain_a, gain_f, query_weight, key_matrix, value_matrix, output_weight,
         router_t, dx, *kept,
     )
-    gate, up, down, dq, dk, dv, do, router, ffn_gain, att_gain = grads_call(
-        rx, rh, rg, ru, re, oa, ob, os, query_weight.shape[1], key_matrix.shape[1]
+    shape = layer_out.shape
+    flat = (shape[0] * shape[1], shape[2])
+    gate, up, down, dq, dk, dv, do, router, ffn_gain, att_gain, layer_out, tokens_grad = grads_call(
+        rx, rh, rg, ru, re, oa, ob, os, layer_out.reshape(flat), tokens_grad.reshape(flat),
+        query_weight.shape[1], key_matrix.shape[1],
     )
     return (
-        layer_out, tokens_grad, att_gain, ffn_gain, dq, dk, dv, do, router.T, gate, up, down,
+        layer_out.reshape(shape), tokens_grad.reshape(shape), att_gain, ffn_gain, dq, dk, dv, do, router.T, gate,
+        up, down,
     )
 
 

time: 285 us -> 279 us (0.979)
  Pallas kernels: 281 us -> 277 us
    pallas_call x1, Pallas kernels: 136 us -> 130 us  [front_call(): pl.pallas_call(front_kernel, out_shape=(out(micro, length, wide, dtype=f3...]
where the time goes in v5:
time: 279 us; the launch traced here: 278 us
  Pallas kernels  277 us (99%)
    pallas_call x1, Pallas kernels, front_call(): pl.pallas_call(front_kernel, out_shape=(out(micro, length, wide, dtype=f3...  130 us
    pallas_call x1, Pallas kernels, back_call(): pl.pallas_call(back_kernel, out_shape=(jax.ShapeDtypeStruct((micro, lengt...  119 us
    pallas_call x1, Pallas kernels, grads_call(): pl.pallas_call(grads_kernel, grid=(steps,), in_specs=[wide, thin, thin, t...  27.7 us

profile of v5, /device:TPU:16, one launch (start us, length us, event | category | flops | bytes accessed | tf_op | source)
XLA Modules:
  0.0 277.9 jit_solution(4210763726564189574)
XLA Ops:
  0.6 130.4 %front.1 = (f32[2,128,1664]{2,1,0:T(8,128)}, bf16[2,128,1536]{2,1,0:T(8,128)(2,1)}, bf16[2,128,768]{2,1,0:T(8,128)(2,1)}, bf16[2,768,128]{2,1,0:T(8,128)(2,1)}, ...) custom-call(bf16[2,128,1536]{2,1,0:T(8,128)(2,1)} %tok_hbm.3, ...), custom_call_target="tpu_custom_call" | custom-call | flops 10871635968 | bytes 41943040 | tf_op jit(solution)/shard_map/front/pallas_call | solution.py:1091
  131.1 119.0 %back.1 = (bf16[2,128,1536]{2,1,0:T(8,128)(2,1)}, f32[2,128,1536]{2,1,0:T(8,128)}, bf16[1536,1024]{1,0:T(8,128)(2,1)}, bf16[768,1536]{1,0:T(8,128)(2,1)}, bf16[64,1536]{1,0:T(8,128)(2,1)}) custom-call(bf16[2,128,1536]{2,1,0:T(8,128)(2,1)} %tok_hbm.3, bf16[2,128,1536]{2,1,0:T(8,128)(2,1)} %g_hbm.3, bf16[1536,768]{1,0:T(8,128)(2,1)} %wq_hbm.3, ...), custom_call_target="tpu_custom_call" | custom-call | flops 1409286144 | bytes 20971520 | tf_op jit(solution)/shard_map/back/pallas_call | solution.py:1723
  250.1 27.7 %expert_grads.1 = (f32[1536,1536]{1,0:T(8,128)}, f32[1536,1536]{1,0:T(8,128)}, f32[1536,1536]{1,0:T(8,128)}, f32[1536,768]{1,0:T(8,128)}, f32[1536,128]{1,0:T(8,...) custom-call(bf16[2,768,1536]{2,1,0:T(8,128)(2,1)} %bitcast.21, ...), custom_call_target="tpu_custom_call" | custom-call | flops 10871635968 | bytes 65011712 | tf_op jit(solution)/shard_map/expert_grads/pallas_call | solution.py:1807

commit v6 on v5

--- a/solution.py
+++ b/solution.py
@@ -474,12 +474,12 @@
     tok_hbm, g_hbm, wq_hbm, wk_hbm, wv_hbm, wo_hbm, wg_hbm, wu_hbm, wd_hbm,
     pos_ref, routes_ref, gain_a, gain_f, router_ref,
     dx_hbm, nrm_hbm, att_hbm, q_hbm, k_hbm, v_hbm, pr_hbm, tab_hbm, hs_hbm, x_hbm, y0_hbm, y1_hbm, hot_hbm,
-    fn, fa, rx_ref, rh_ref, rg_ref, ru_ref, re_ref,
+    fn, fa, gate_hbm, up_hbm, down_hbm,
     tok_ref, wq_ref, wk_ref, wv_ref, wo_ref, nrm_ref, att_ref, q_ref, k_ref, v_ref, pr_ref, tab_ref, hs_ref, x_ref,
     xz, gz, rz, xs, gs, xr, gr, eg, hid, gpg, upg, dx_ref, dr, dz, own_part, other_part, rel,
     onehot, prob, gg, wg, wu, wd,
     r_s, r_r, za_s, za_r, xa_s, xa_r, xb_s, xb_r, zb_s, zb_r, pair_s, pair_r, part_s, part_r, fw_s, rel_s, rel_r,
-    f_s, f_r, w_s, w_r, in_sem, out_sem, own_sem,
+    f_s, f_r, w_s, w_r, in_sem, out_sem,
 ):
     ys, ds_, zd = gs, xs, xz
     e = lax.axis_index("expert")
@@ -872,19 +872,26 @@
     save(onehot, hot_hbm)
 
     got_b = {}
-    def to_pair(m):
-        for i, (src, dst) in enumerate(
-            ((xr, rx_ref), (hid, rh_ref), (gpg, rg_ref), (upg, ru_ref), (eg, re_ref))
-        ):
-            src_at = src.at[m, :, 0:width] if i == 0 else src.at[m]
-            n = m * 8 + i
-            cp = remote(src_at, dst.at[c, m], pair_s.at[n], pair_r.at[n], (e, 1 - c))
+    def weight_grads():
+        def columns(i):
+            at = cols(i, tw)
+            for out, back in ((wg, gpg), (wu, upg)):
+                total = mm_tn(xr[0, :, 0:width], back[0, :, at])
+                for m in range(1, micro):
+                    total = total + mm_tn(xr[m, :, 0:width], back[m, :, at])
+                out[:, at] = total.astype(bf)
+            total = mm_tn(hid[0, :, at], eg[0])
+            for m in range(1, micro):
+                total = total + mm_tn(hid[m, :, at], eg[m])
+            wd[at, :] = total.astype(bf)
+
+        tiles(ff // tw, columns)
+        for n, (src, dst) in enumerate(((wg, gate_hbm), (wu, up_hbm), (wd, down_hbm))):
+            cp = remote(src, dst.at[c], pair_s.at[n], pair_r.at[n], twin)
             cp.start()
             sent.append(cp)
-            got_b[("pair", m, i)] = cp
-            cp = pltpu.make_async_copy(src_at, dst.at[c, m], own_sem.at[n])
-            cp.start()
-            saves.append(cp)
+            got_b[("pair", n)] = cp
+            save(src, dst.at[c])
 
     def send_back(m, a, j):
         src, dst = ((ds_.at[m], dr.at[m]), (ys.at[m], y0_hbm))[a]
@@ -964,7 +971,6 @@
             lane == me, high, jnp.where(lane == me + 32, total - high, 0.0)
         ).astype(jnp.bfloat16)
         send_back(m, 0, 1)
-        to_pair(m)
 
     for m in range(micro):
         run(m)
@@ -1034,6 +1040,8 @@
     order = [(m, j) for m in range(micro) for j in range(2)]
     for i, (m, j) in enumerate(order):
         gather(m, j)
+        if i == 1:
+            weight_grads()
         if i >= 1:
             finish(*order[i - 1])
     finish(*order[-1])
@@ -1046,11 +1054,11 @@
     for d in range(1, 4):
         got_a[("twin", d)].wait_recv()
     for m in range(micro):
-        for i in range(5):
-            got_b[("pair", m, i)].wait_recv()
         for j in range(2):
             got_c[("pair", m, j)].wait_recv()
         save(dx_ref.at[m], dx_hbm.at[m])
+    for n in range(3):
+        got_b[("pair", n)].wait_recv()
     for d in range(1, 8):
         got_b[(0, 1, 0, d)].wait_recv()
     for at in list(away):
@@ -1106,14 +1114,12 @@
             out(micro, rows, col),
             out(4 * micro * length, width // 2),
             out(4 * micro * length, hw // 2),
-            out(2, micro, rows, width),
-            out(2, micro, rows, ff),
-            out(2, micro, rows, ff),
-            out(2, micro, rows, ff),
-            out(2, micro, rows, width),
+            out(2, width, ff),
+            out(2, width, ff),
+            out(2, ff, width),
         ),
         in_specs=[hbm] * 9 + [vmem] * 5,
-        out_specs=(hbm,) * 20,
+        out_specs=(hbm,) * 18,
         scratch_shapes=[
             buf(micro, length, width), buf(width, hw), buf(width, HEAD_SIZE), buf(width, HEAD_SIZE), buf(hw, width),
             buf(micro, length, width), buf(micro, length, hw), buf(micro, heads * length, HEAD_SIZE),
@@ -1130,7 +1136,7 @@
             sem((4,)), sem((4,)), sem((16 * micro,)), sem((16 * micro,)), sem((32 * micro,)), sem((32 * micro,)),
             sem((32 * micro,)), sem((32 * micro,)), sem((8 * micro,)), sem((8 * micro,)), sem((8 * micro,)),
             sem((8 * micro,)), sem((3,)), sem((3,)), sem((4 * micro,)), sem((2 * micro,)), sem((2 * micro,)),
-            sem((14,)), sem((14,)), sem((4,)), sem((4,)), sem((8 + micro,)), sem((16 + 5 * micro,)), sem((8 * micro,)),
+            sem((14,)), sem((14,)), sem((4,)), sem((4,)), sem((8 + micro,)), sem((16 + 5 * micro,)),
         ],
         compiler_params=pltpu.CompilerParams(
             collective_id=1, has_side_effects=True, vmem_limit_bytes=VMEM_LIMIT
@@ -1762,16 +1768,18 @@
     )
 
 
-def grads_kernel(
-    x_ref, h_ref, g_ref, u_ref, e_ref, qkv_ref, o_ref, s_ref, lay_ref, tok_ref,
+def results_kernel(
+    gate_ref, up_ref, down_ref, qkv_ref, o_ref, s_ref, lay_ref, tok_ref,
     gate_out, up_out, down_out, q_out, k_out, v_out, o_out, router_out, ffn_out, att_out, lay_out, tok_out,
 ):
-    gate_out[...] = mm_tn(x_ref[0], g_ref[0])
-    up_out[...] = mm_tn(x_ref[0], u_ref[0])
-    down_out[...] = mm_tn(h_ref[0], e_ref[0])
     wq = q_out.shape[1]
     wk = wq + k_out.shape[1]
+    ff = gate_ref.shape[2]
     f32 = jnp.float32
+    for i in range(2):
+        gate_out[:, i * ff : (i + 1) * ff] = gate_ref[i].astype(f32)
+        up_out[:, i * ff : (i + 1) * ff] = up_ref[i].astype(f32)
+    down_out[...] = down_ref[...].astype(f32)
     q_out[...] = qkv_ref[:, 0:wq].astype(f32)
     k_out[...] = qkv_ref[:, wq:wk].astype(f32)
     v_out[...] = qkv_ref[:, wk:].astype(f32)
@@ -1788,34 +1796,27 @@
         att_out[...] = small[EXPERTS + 1 : EXPERTS + 2].reshape(width)
 
 
-def grads_call(rx, rh, rg, ru, re, qkv, o, small, layer, tokens_grad, wq, wk):
-    _, micro, rows, width = rx.shape
-    ff = rh.shape[3]
-    n = micro * rows
-    tw = 256
-    per = ff // tw
-    steps = 2 * per
+def results_call(gate, up, down, qkv, o, small, layer, tokens_grad, wq, wk):
+    _, width, ff = gate.shape
+    steps = 6
     f32 = jnp.float32
-    wide = pl.BlockSpec((1, n, width), lambda i: (i // per, 0, 0))
-    thin = pl.BlockSpec((1, n, tw), lambda i: (i // per, 0, i % per))
-    down = lambda a, w: pl.BlockSpec((a // steps, w), lambda i: (i, 0))
+    down_rows = lambda a, w: pl.BlockSpec((a // steps, w), lambda i: (i, 0))
+    pair = pl.BlockSpec((2, width // steps, ff), lambda i: (0, i, 0))
     whole = lambda *s: pl.BlockSpec(s, lambda i: (0,) * len(s))
-    tall = layer.shape[0] // 4
-    some = pl.BlockSpec((tall, width), lambda i: (jnp.minimum(i, 3), 0))
     out = lambda *s: jax.ShapeDtypeStruct(s, f32)
     wv = qkv.shape[1] - wq - wk
+    few = 4
+    some = pl.BlockSpec((layer.shape[0] // few, width), lambda i: (jnp.minimum(i, few - 1), 0))
     return pl.pallas_call(
-        grads_kernel,
+        results_kernel,
         grid=(steps,),
         in_specs=[
-            wide, thin, thin, thin, wide,
-            down(*qkv.shape), down(*o.shape), whole(*small.shape), some, some,
+            pair, pair, down_rows(2 * ff, width), down_rows(*qkv.shape), down_rows(*o.shape), whole(*small.shape),
+            some, some,
         ],
         out_specs=(
-            pl.BlockSpec((width, tw), lambda i: (0, i)),
-            pl.BlockSpec((width, tw), lambda i: (0, i)),
-            pl.BlockSpec((tw, width), lambda i: (i, 0)),
-            down(width, wq), down(width, wk), down(width, wv), down(*o.shape),
+            down_rows(width, 2 * ff), down_rows(width, 2 * ff), down_rows(2 * ff, width),
+            down_rows(width, wq), down_rows(width, wk), down_rows(width, wv), down_rows(*o.shape),
             whole(EXPERTS, width), whole(width), whole(width), some, some,
         ),
         out_shape=(
@@ -1825,14 +1826,9 @@
             jax.ShapeDtypeStruct(layer.shape, layer.dtype), out(*tokens_grad.shape),
         ),
         compiler_params=pltpu.CompilerParams(vmem_limit_bytes=VMEM_LIMIT),
-        cost_estimate=pl.CostEstimate(
-            flops=2 * 6 * n * width * ff, bytes_accessed=62 * 2**20, transcendentals=0
-        ),
-        name="expert_grads",
-    )(
-        rx.reshape(2, n, width), rh.reshape(2, n, ff), rg.reshape(2, n, ff),
-        ru.reshape(2, n, ff), re.reshape(2, n, width), qkv, o, small, layer, tokens_grad,
-    )
+        cost_estimate=pl.CostEstimate(flops=0, bytes_accessed=64 * 2**20, transcendentals=0),
+        name="results",
+    )(gate, up, down.reshape(2 * ff, width), qkv, o, small, layer, tokens_grad)
 
 
 def suits(mesh):
@@ -1846,7 +1842,7 @@
     micro_count, length, model_width = tokens.shape
     gain_a, gain_f = attention_gain, feedforward_gain
     router_t = router_weight.T
-    dx, *kept, rx, rh, rg, ru, re = front_call(
+    dx, *kept, gate_low, up_low, down_low = front_call(
         tokens, cotangent, positions, routes.transpose(0, 2, 1), gain_a, gain_f, query_weight, key_matrix,
         value_matrix, output_weight, router_t, gate_weight, up_weight, down_weight,
     )
@@ -1856,8 +1852,8 @@
     )
     shape = layer_out.shape
     flat = (shape[0] * shape[1], shape[2])
-    gate, up, down, dq, dk, dv, do, router, ffn_gain, att_gain, layer_out, tokens_grad = grads_call(
-        rx, rh, rg, ru, re, oa, ob, os, layer_out.reshape(flat), tokens_grad.reshape(flat),
+    gate, up, down, dq, dk, dv, do, router, ffn_gain, att_gain, layer_out, tokens_grad = results_call(
+        gate_low, up_low, down_low, oa, ob, os, layer_out.reshape(flat), tokens_grad.reshape(flat),
         query_weight.shape[1], key_matrix.shape[1],
     )
     return (

time: 279 us -> 276 us (0.989)
  Pallas kernels: 277 us -> 274 us
    pallas_call x1, Pallas kernels: 27.7 us -> 21.4 us  [results_call(): pl.pallas_call(results_kernel, grid=(steps,), in_specs=[pair, pair, down_...]
    pallas_call x1, Pallas kernels: 130 us -> 134 us  [front_call(): pl.pallas_call(front_kernel, out_shape=(out(micro, length, wide, dtype=f3...]
where the time goes in v6:
time: 276 us; the launch traced here: 274 us
  Pallas kernels  274 us (99%)
    pallas_call x1, Pallas kernels, front_call(): pl.pallas_call(front_kernel, out_shape=(out(micro, length, wide, dtype=f3...  134 us
    pallas_call x1, Pallas kernels, back_call(): pl.pallas_call(back_kernel, out_shape=(jax.ShapeDtypeStruct((micro, lengt...  118 us
    pallas_call x1, Pallas kernels, results_call(): pl.pallas_call(results_kernel, grid=(steps,), in_specs=[pair, pair, down_...  21.4 us

profile of v6, /device:TPU:16, one launch (start us, length us, event | category | flops | bytes accessed | tf_op | source)
XLA Modules:
  0.0 274.4 jit_solution(10688856972413757237)
XLA Ops:
  0.6 134.4 %front.1 = (f32[2,128,1664]{2,1,0:T(8,128)}, bf16[2,128,1536]{2,1,0:T(8,128)(2,1)}, bf16[2,128,768]{2,1,0:T(8,128)(2,1)}, bf16[2,768,128]{2,1,0:T(8,128)(2,1)}, ...) custom-call(bf16[2,128,1536]{2,1,0:T(8,128)(2,1)} %tok_hbm.3, ...), custom_call_target="tpu_custom_call" | custom-call | flops 10871635968 | bytes 41943040 | tf_op jit(solution)/shard_map/front/pallas_call | solution.py:1099
  135.1 117.7 %back.1 = (bf16[2,128,1536]{2,1,0:T(8,128)(2,1)}, f32[2,128,1536]{2,1,0:T(8,128)}, bf16[1536,1024]{1,0:T(8,128)(2,1)}, bf16[768,1536]{1,0:T(8,128)(2,1)}, bf16[64,1536]{1,0:T(8,128)(2,1)}) custom-call(bf16[2,128,1536]{2,1,0:T(8,128)(2,1)} %tok_hbm.3, bf16[2,128,1536]{2,1,0:T(8,128)(2,1)} %g_hbm.3, bf16[1536,768]{1,0:T(8,128)(2,1)} %wq_hbm.3, ...), custom_call_target="tpu_custom_call" | custom-call | flops 1409286144 | bytes 20971520 | tf_op jit(solution)/shard_map/back/pallas_call | solution.py:1729
  252.9 21.4 %results.1 = (f32[1536,1536]{1,0:T(8,128)}, f32[1536,1536]{1,0:T(8,128)}, f32[1536,1536]{1,0:T(8,128)}, f32[1536,768]{1,0:T(8,128)}, f32[1536,128]{1,0:T(8,128)}...) custom-call(bf16[2,1536,768]{2,1,0:T(8,128)(2,1)} %get-tuple-element, ...), custom_call_target="tpu_custom_call" | custom-call | bytes 67108864 | tf_op jit(solution)/shard_map/results/pallas_call | solution.py:1810

commit v7 on v6

--- a/solution.py
+++ b/solution.py
@@ -546,7 +546,8 @@
         )
     ):
         loads[name] = pltpu.make_async_copy(src, dst, in_sem.at[i])
-        loads[name].start()
+        if name not in ("wg", "wu", "wd"):
+            loads[name].start()
     saves = []
 
     def save(src, dst):
@@ -722,7 +723,13 @@
 
     for name in ("wq", "wk", "wv"):
         loads[name].wait()
+    for name in ("wg", "wu", "wd"):
+        loads[name].start()
     tiles(wq_ref.shape[1] // tw, project)
+    z_forward(0, 0)
+    z_sent(0, 0)
+    for m in range(1, micro):
+        z_send(m, 0)
     key_pre = mm(everything, wk_ref[...])
     value_pre = mm(everything, wv_ref[...])
     for m in range(micro):
@@ -742,10 +749,6 @@
     for src, dst in ((q_ref, q_hbm), (k_ref, k_hbm), (v_ref, v_hbm), (pr_ref, pr_hbm), (att_ref, att_hbm)):
         save(src, dst)
     factor(2, fa)
-    z_forward(0, 0)
-    z_sent(0, 0)
-    for m in range(1, micro):
-        z_send(m, 0)
     loads["wo"].wait()
     att_all = att_ref[...].reshape(micro * length, heads * head)
     got_part = []
@@ -822,8 +825,8 @@
                 got_p[(m, a, j, d)] = cp
 
     sent_p = {}
+    pass_on()
     pack(0, 0)
-    pass_on()
     tall = lax.broadcasted_iota(jnp.int32, (128, EXPERTS), 0)
     double = (lax.rem(tall, EXPERTS) == lax.broadcasted_iota(jnp.int32, (128, EXPERTS), 1)) & (
         tall < 2 * EXPERTS
@@ -1588,13 +1591,6 @@
         got_y[(2, k)] = cp
     spread_rest(0)
     layer(0)
-    need("y1")
-    for n in range(1, 8):
-        for j in range(2):
-            got_v[(n, j, "row")].wait_recv()
-
-    regroup(1, y1r)
-    send_far(1)
 
     def spots(px, py, t):
         return (
@@ -1669,6 +1665,13 @@
     own(0, 1)
     total_of(0)
     own(0, 0)
+    need("y1")
+    for n in range(1, 8):
+        for j in range(2):
+            got_v[(n, j, "row")].wait_recv()
+
+    regroup(1, y1r)
+    send_far(1)
     total_of(2)
     own(0, 2)
     own(1, 1)

time: 276 us -> 273 us (0.989)
  no operation moved by 1% of the time
where the time goes in v7:
time: 273 us; the launch traced here: 272 us
  Pallas kernels  272 us (100%)
    pallas_call x1, Pallas kernels, front_call(): pl.pallas_call(front_kernel, out_shape=(out(micro, length, wide, dtype=f3...  133 us
    pallas_call x1, Pallas kernels, back_call(): pl.pallas_call(back_kernel, out_shape=(jax.ShapeDtypeStruct((micro, lengt...  117 us
    pallas_call x1, Pallas kernels, results_call(): pl.pallas_call(results_kernel, grid=(steps,), in_specs=[pair, pair, down_...  21.4 us

profile of v7, /device:TPU:16, one launch (start us, length us, event | category | flops | bytes accessed | tf_op | source)
XLA Modules:
  0.0 272.4 jit_solution(2715444747588367927)
XLA Ops:
  0.6 132.8 %front.1 = (f32[2,128,1664]{2,1,0:T(8,128)}, bf16[2,128,1536]{2,1,0:T(8,128)(2,1)}, bf16[2,128,768]{2,1,0:T(8,128)(2,1)}, bf16[2,768,128]{2,1,0:T(8,128)(2,1)}, ...) custom-call(bf16[2,128,1536]{2,1,0:T(8,128)(2,1)} %tok_hbm.3, ...), custom_call_target="tpu_custom_call" | custom-call | flops 10871635968 | bytes 41943040 | tf_op jit(solution)/shard_map/front/pallas_call | solution.py:1102
  133.4 117.4 %back.1 = (bf16[2,128,1536]{2,1,0:T(8,128)(2,1)}, f32[2,128,1536]{2,1,0:T(8,128)}, bf16[1536,1024]{1,0:T(8,128)(2,1)}, bf16[768,1536]{1,0:T(8,128)(2,1)}, bf16[64,1536]{1,0:T(8,128)(2,1)}) custom-call(bf16[2,128,1536]{2,1,0:T(8,128)(2,1)} %tok_hbm.3, bf16[2,128,1536]{2,1,0:T(8,128)(2,1)} %g_hbm.3, bf16[1536,768]{1,0:T(8,128)(2,1)} %wq_hbm.3, ...), custom_call_target="tpu_custom_call" | custom-call | flops 1409286144 | bytes 20971520 | tf_op jit(solution)/shard_map/back/pallas_call | solution.py:1732
  250.9 21.4 %results.1 = (f32[1536,1536]{1,0:T(8,128)}, f32[1536,1536]{1,0:T(8,128)}, f32[1536,1536]{1,0:T(8,128)}, f32[1536,768]{1,0:T(8,128)}, f32[1536,128]{1,0:T(8,128)}...) custom-call(bf16[2,1536,768]{2,1,0:T(8,128)(2,1)} %get-tuple-element, ...), custom_call_target="tpu_custom_call" | custom-call | bytes 67108864 | tf_op jit(solution)/shard_map/results/pallas_call | solution.py:1813
